TPU v7x, 512 devices: a whole 4x8x8 slice. The times are simulated.
512 devices in a mesh: dp: 8 (over z), vocab: 64 (over y, x, core).
Axes of the slice: x: 4, y: 8, z: 8, core: 2. Of those that a mesh axis runs over, the one named last changes fastest.
Arguments:
- hidden: bfloat16 [384, 7168], P(None, 'dp'), may hold values from -150 to 150
- tokens: int32 [384], replicated, may hold values from 0 to 65535
- final_gain: float32 [7168], P('dp'), may hold values from 0.25 to 1.75
- hidden_gain: float32 [7168], P('dp'), may hold values from 0.25 to 1.75
- embed_gain: float32 [7168], P('dp'), may hold values from 0.25 to 1.75
- embed_table: bfloat16 [65536, 7168], P('vocab', 'dp'), may hold values from -150 to 150
- proj_hidden: bfloat16 [7168, 7168], P('dp', 'vocab'), may hold values from -0.046875 to 0.046875
- proj_embed: bfloat16 [7168, 7168], P('dp', 'vocab'), may hold values from -0.046875 to 0.046875
- draft_gain: float32 [7168], P('vocab'), may hold values from 0.25 to 1.75
- head_weight: bfloat16 [7168, 65536], P('dp', 'vocab'), may hold values from -6.1419227 to 6.1419227
Outputs:
- main_logp: bfloat16 [384, 65536], P('dp', 'vocab')
- draft_logp: bfloat16 [384, 65536], P('dp', 'vocab')
All inputs are finite; a program needn't handle non-finite values.
Results may differ from a plain program's by a relative error of at most 0.0047.
Values may be sent and summed in bfloat16 or wider, within the bound.
No kernel may reach another device: no remote copies, remote signals or barrier semaphores. Data moves between devices by JAX's collectives and lax.ppermute only.
A program may use at most 64 MiB of HBM per device.

v0:
```python
import jax
import jax.numpy as jnp
from jax import lax
from jax.sharding import PartitionSpec as P

EPS = 1e-06


def log_rows(logits):
    top = lax.pmax(jnp.max(logits, axis=1), "vocab")
    total = lax.psum(jnp.sum(jnp.exp(logits - top[:, None]), axis=1), "vocab")
    return (logits - top[:, None] - jnp.log(total)[:, None]).astype(jnp.bfloat16)


def vocab_head(normed, head_weight):
    return lax.psum_scatter(
        jnp.dot(normed, head_weight, preferred_element_type=jnp.float32),
        "dp",
        scatter_dimension=0,
        tiled=True,
    )


def embed_lookup(tokens, embed_table):
    vocab_dev = embed_table.shape[0]
    offset = lax.axis_index("vocab") * vocab_dev
    column = lax.broadcasted_iota(jnp.int32, (tokens.shape[0], vocab_dev), 1)
    onehot = (tokens[:, None] - offset == column).astype(jnp.bfloat16)
    picked = jnp.dot(onehot, embed_table, preferred_element_type=jnp.float32)
    return lax.psum(picked, "vocab")


def draft_scale(projected, draft_gain, model_width):
    squares = lax.psum(jnp.sum(projected * projected, axis=1), "vocab")
    inverse = lax.rsqrt(squares / model_width + EPS)
    return (projected * inverse[:, None] * draft_gain).astype(jnp.bfloat16)


def per_device(
    hidden,
    tokens,
    final_gain,
    hidden_gain,
    embed_gain,
    embed_table,
    proj_hidden,
    proj_embed,
    draft_gain,
    head_weight,
):
    rows_all, width_dp = hidden.shape
    dp_count = lax.axis_size("dp")
    model_width = width_dp * dp_count
    hidden_f = hidden.astype(jnp.float32)
    hidden_sq = jnp.sum(hidden_f * hidden_f, axis=1)
    hidden_total = lax.psum(hidden_sq, "dp")
    inv_hidden = lax.rsqrt(hidden_total / model_width + EPS)[:, None]
    main_normed = (hidden_f * inv_hidden * final_gain).astype(jnp.bfloat16)
    main_logp = log_rows(vocab_head(main_normed, head_weight))
    embedded = embed_lookup(tokens, embed_table)
    embed_total = lax.psum(jnp.sum(embedded * embedded, axis=1), "dp")
    inv_embed = lax.rsqrt(embed_total / model_width + EPS)[:, None]
    joined_hidden = (hidden_f * inv_hidden * hidden_gain).astype(jnp.bfloat16)
    joined_embed = (embedded * inv_embed * embed_gain).astype(jnp.bfloat16)
    partial_sum = jnp.dot(joined_hidden, proj_hidden, preferred_element_type=jnp.float32) + jnp.dot(
        joined_embed, proj_embed, preferred_element_type=jnp.float32
    )
    projected = lax.psum(partial_sum, "dp")
    slab = draft_scale(projected, draft_gain, model_width)
    whole = lax.all_gather(slab, "vocab", axis=1, tiled=True)
    draft_normed = lax.dynamic_slice_in_dim(whole, lax.axis_index("dp") * width_dp, width_dp, 1)
    draft_logp = log_rows(vocab_head(draft_normed, head_weight))
    return (main_logp, draft_logp)


def solution(mesh):
    return jax.shard_map(
        per_device,
        mesh=mesh,
        in_specs=(
            P(None, "dp"),
            P(),
            P("dp"),
            P("dp"),
            P("dp"),
            P("vocab", "dp"),
            P("dp", "vocab"),
            P("dp", "vocab"),
            P("vocab"),
            P("dp", "vocab"),
        ),
        out_specs=(P("dp", "vocab"), P("dp", "vocab")),
        check_vma=False,
    )
```

profile of v0, /device:TPU:1, one launch (start us, length us, event | category | flops | bytes accessed | tf_op | source)
XLA Modules:
  0.0 868.9 jit_solution(8162640423158853429)
XLA Ops:
  7.2 0.0 copy-start
  7.2 0.0 all-reduce.6.cloned.1.call-start
  7.2 0.8 broadcast_subtract_fusion
  8.0 3.6 fusion.2
  11.7 0.0 copy-start.2
  11.7 0.0 all-reduce.6.cloned.1.call-update
  11.7 0.0 copy-start.6
  11.7 0.0 all-reduce.8.cloned.1.call-start
  11.8 1.0 copy-done.2
  12.8 0.2 fusion.5
  13.0 0.0 copy-start.4
  13.0 200.5 %all-reduce.6.cloned.1.call-done = f32[384,896]{1,0:T(8,128)} async-done(((f32[384,896]{1,0:T(8,128)}), f32[384,896]{1,0:T(8,128)}) %all-reduce.6.cloned.1.call-update) | async-done | bytes 1376272 | tf_op jit(solution)/shard_map/psum | solution.py:30
  213.5 1.6 multiply_reduce_fusion
  215.1 14.3 %all-reduce.2 = (f32[384]{0:T(512)S(1)}, f32[384]{0:T(512)S(1)}) all-reduce(f32[384]{0:T(512)S(1)} %fusion.5, f32[384]{0:T(512)S(1)} %multiply_reduce_fusion), channel_id=1, replica_groups=mesh['dp'=8,'vocab'=64] {'dp'}, use_global_device_ids=true, to_apply=%region_1.0 | all-reduce | flops 768 | bytes 6144 | tf_op jit(solution)/shard_map/psum | solution.py:56
  229.5 0.0 copy-done.6
  229.5 1.6 fusion.7
  231.1 0.0 copy-done.3
  231.1 0.0 copy-done.4
  231.1 0.0 copy-done.1
  231.1 0.0 copy-start.5
  231.1 0.0 copy-start.7
  231.1 1.1 convolution_add_fusion
  232.2 0.0 all-reduce.8.cloned.1.call-update
  232.2 0.0 all-gather.2.cloned.1.call-start
  232.3 75.1 %all-reduce.8.cloned.1.call-done = f32[384,112]{0,1:T(8,128)} async-done(((f32[384,112]{0,1:T(8,128)}), f32[384,112]{0,1:T(8,128)}) %all-reduce.8.cloned.1.call-update) | async-done | bytes 172048 | tf_op jit(solution)/shard_map/psum | solution.py:68
  307.4 0.9 multiply_reduce_fusion.1
  308.4 128.9 %psum.54 = f32[384]{0:T(512)S(1)} all-reduce(f32[384]{0:T(512)S(1)} %multiply_reduce_fusion.1), channel_id=1, replica_groups=mesh['dp'=8,'vocab'=64] {'vocab'}, use_global_device_ids=true, to_apply=%region_12.0 | all-reduce | flops 384 | bytes 3072 | tf_op jit(solution)/shard_map/psum | solution.py:34
  437.3 0.0 copy-done.5
  437.3 1.6 multiply_convert_fusion.2
  438.9 0.0 all-gather.2.cloned.1.call-update
  438.9 0.0 reduce-scatter.3.cloned.1.call-start
  439.0 0.0 copy-done
  439.0 0.0 copy-done.7
  439.0 3.3 fusion.9
  442.3 0.0 reduce-scatter.3.cloned.1.call-update
  442.3 0.0 reduce-scatter.5.cloned.1.call-start
  442.4 78.3 %all-gather.2.cloned.1.call-done = bf16[384,7168]{0,1:T(8,128)(2,1)} async-done(((bf16[384,112]{0,1:T(8,128)(2,1)}), bf16[384,7168]{0,1:T(8,128)(2,1)}) %all-gather.2.cloned.1.call-update) | async-done | bytes 5505040 | tf_op jit(solution)/shard_map/all_gather | solution.py:70
  520.7 3.3 fusion.11
  524.0 0.0 reduce-scatter.5.cloned.1.call-update
  524.0 36.1 %reduce-scatter.3.cloned.1.call-done = f32[48,1024]{1,0:T(8,128)} async-done(((f32[384,1024]{1,0:T(8,128)}), f32[48,1024]{1,0:T(8,128)}) %reduce-scatter.3.cloned.1.call-update) | async-done | bytes 196624 | tf_op jit(solution)/shard_map/reduce_scatter | solution.py:16
  560.1 1.0 reduce_max.18
  561.1 43.6 %reduce-scatter.5.cloned.1.call-done = f32[48,1024]{1,0:T(8,128)} async-done(((f32[384,1024]{1,0:T(8,128)}), f32[48,1024]{1,0:T(8,128)}) %reduce-scatter.5.cloned.1.call-update) | async-done | bytes 196624 | tf_op jit(solution)/shard_map/reduce_scatter | solution.py:16
  604.7 1.0 reduce_max.19
  605.8 128.0 %all-reduce.1 = (f32[48]{0:T(128)S(1)}, f32[48]{0:T(128)S(1)}) all-reduce(f32[48]{0:T(128)S(1)} %reduce_max.18, f32[48]{0:T(128)S(1)} %reduce_max.19), channel_id=1, replica_groups=mesh['dp'=8,'vocab'=64] {'vocab'}, use_global_device_ids=true, to_apply=%region_4.0 | all-reduce | flops 96 | bytes 768 | tf_op jit(solution)/shard_map/pmax | solution.py:10
  733.8 1.1 exponential_reduce_fusion.1
  734.9 1.1 exponential_reduce_fusion
  736.1 124.5 %all-reduce = (f32[48]{0:T(128)S(1)}, f32[48]{0:T(128)S(1)}) all-reduce(f32[48]{0:T(128)S(1)} %exponential_reduce_fusion.1, f32[48]{0:T(128)S(1)} %exponential_reduce_fusion), channel_id=1, replica_groups=mesh['dp'=8,'vocab'=64] {'vocab'}, use_global_device_ids=true, to_apply=%region_6.0 | all-reduce | flops 96 | bytes 768 | tf_op jit(solution)/shard_map/psum | solution.py:11
  860.6 1.8 subtract_convert_fusion
  (7 shorter events, 0.0 us)
Async XLA Ops:
  7.2 431.8 %copy-start = (bf16[896,1024]{1,0:T(8,128)(2,1)S(1)}, bf16[896,1024]{1,0:T(8,128)(2,1)}, u32[]{:S(2)}) copy-start(bf16[896,1024]{1,0:T(8,128)(2,1)} %param.19) | copy-start | bytes 5505028
  7.2 206.3 %all-reduce.6.cloned.1.call-start = ((), (), s32[]{:S(2)}) async-start(), calls=%async_computation.3 | async-start | bytes 2752512 | tf_op jit(solution)/shard_map/psum | solution.py:30
  11.7 1.1 copy-start.2
  11.7 217.8 %copy-start.6 = (f32[896]{0:T(1024)S(1)}, f32[896]{0:T(1024)}, u32[]{:S(2)}) copy-start(f32[896]{0:T(1024)} %param.13) | copy-start | bytes 10756
  11.7 295.7 %all-reduce.8.cloned.1.call-start = ((), (), s32[]{:S(2)}) async-start(), calls=%async_computation.4 | async-start | bytes 344064 | tf_op jit(solution)/shard_map/psum | solution.py:68
  13.0 218.1 %copy-start.3 = (bf16[896,112]{0,1:T(8,128)(2,1)S(1)}, bf16[896,112]{0,1:T(8,128)(2,1)}, u32[]{:S(2)}) copy-start(bf16[896,112]{0,1:T(8,128)(2,1)} %param.17) | copy-start | bytes 602116
  13.0 218.1 %copy-start.4 = (f32[896]{0:T(1024)S(1)}, f32[896]{0:T(1024)}, u32[]{:S(2)}) copy-start(f32[896]{0:T(1024)} %param.14) | copy-start | bytes 10756
  213.5 17.6 %copy-start.1 = (f32[384,896]{1,0:T(8,128)S(1)}, f32[384,896]{1,0:T(8,128)}, u32[]{:S(2)}) copy-start(f32[384,896]{1,0:T(8,128)} %all-reduce.6.cloned.1.call-done) | copy-start | bytes 4128772
  231.1 206.2 %copy-start.5 = (f32[112]{0:T(128)S(1)}, f32[112]{0:T(128)}, u32[]{:S(2)}) copy-start(f32[112]{0:T(128)} %param.18) | copy-start | bytes 1348
  231.1 207.9 %copy-start.7 = (f32[896]{0:T(1024)S(1)}, f32[896]{0:T(1024)}, u32[]{:S(2)}) copy-start(f32[896]{0:T(1024)} %param.12) | copy-start | bytes 10756
  232.2 288.4 %all-gather.2.cloned.1.call-start = ((), (), s32[]{:S(2)}) async-start(), calls=%async_computation.5 | async-start | bytes 5591040 | tf_op jit(solution)/shard_map/all_gather | solution.py:70
  438.9 121.2 %reduce-scatter.3.cloned.1.call-start = ((), (), s32[]{:S(2)}) async-start(), calls=%async_computation.2 | async-start | bytes 1769472 | tf_op jit(solution)/shard_map/reduce_scatter | solution.py:16
  442.3 162.4 %reduce-scatter.5.cloned.1.call-start = ((), (), s32[]{:S(2)}) async-start(), calls=%async_computation.6 | async-start | bytes 1769472 | tf_op jit(solution)/shard_map/reduce_scatter | solution.py:16
Sparse Core Ops, SparseCore 0:
  11.8 201.6 all-reduce.5
  232.4 75.0 all-reduce.7
  439.0 81.5 all-gather.1
  523.4 36.6 reduce-scatter.2
  562.8 41.9 reduce-scatter.4
where the time goes:
time: 869 us
  waiting for transfers between devices  434 us (50%)
  blocking collectives  396 us (46%)
  between operations  13.9 us (2%)
  matrix products  12.9 us (1%)
  other arithmetic  11.4 us (1%)
    psum x1, waiting for transfers between devices, embed_lookup(): return lax.psum(picked, 'vocab')  201 us
    psum x1, blocking collectives, draft_scale(): squares = lax.psum(jnp.sum(projected * projected, axis=1), 'vocab')  129 us
    pmax x1, blocking collectives, log_rows(): top = lax.pmax(jnp.max(logits, axis=1), 'vocab')  128 us
    psum x1, blocking collectives, log_rows(): total = lax.psum(jnp.sum(jnp.exp(logits - top[:, None]), axis=1), 'vocab')  124 us
    reduce_scatter x2, waiting for transfers between devices, vocab_head(): lax.psum_scatter(jnp.dot(normed, head_weight, preferred_element_type=jnp....  79.7 us
    all_gather x1, waiting for transfers between devices, per_device(): whole = lax.all_gather(slab, 'vocab', axis=1, tiled=True)  78.3 us
    psum x1, waiting for transfers between devices, per_device(): projected = lax.psum(partial_sum, 'dp')  75.1 us
  transfers between devices with their start and end apart: 5, of which 5 were waited for; matrix products, arithmetic and copies ran while one was open for 1% of the time, Pallas kernels for 0%

commit v1 on v0

v1 whole, which is shorter than its diff:
```python
import functools

import jax
import jax.numpy as jnp
from jax import lax
from jax.experimental import pallas as pl
from jax.experimental.pallas import tpu as pltpu
from jax.sharding import PartitionSpec as P

EPS = 1e-06
BF, F32 = jnp.bfloat16, jnp.float32
ROWS, D, V = 384, 7168, 65536
NZ, NY, NX, NC = 8, 8, 4, 2
FD = D // NZ
VD = V // (NY * NX * NC)
CW = D // (NY * NX * NC)
RB = ROWS // NZ
UR = RB // (NX * NC)
L = 128
WROWS = 2 * FD + 16
ZROWS = 2 * RB + 16
HROWS = RB * (VD // L) + 8
PARAMS = pltpu.CompilerParams(vmem_limit_bytes=48 * 1024 * 1024)


def vid(y, x, c):
    return (y * NX + x) * NC + c


CORE = [[vid(y, x, c) for c in range(NC)] for y in range(NY) for x in range(NX)]
YS = [[vid(y, x, c) for y in range(NY)] for x in range(NX) for c in range(NC)]
XY = [[vid(y, x, c) for y in range(NY) for x in range(NX)] for c in range(NC)]
XC = [[vid(y, x, c) for x in range(NX) for c in range(NC)] for y in range(NY)]


def iota(shape, dim):
    return lax.broadcasted_iota(jnp.int32, shape, dim)


def split(x):
    hi = x.astype(BF).astype(F32)
    return hi, x - hi


def call(kernel, outs, *args):
    single = not isinstance(outs, (list, tuple))
    shapes = [outs] if single else list(outs)
    specs = [pl.BlockSpec(memory_space=pltpu.VMEM) for _ in shapes]
    return pl.pallas_call(
        kernel,
        out_shape=shapes[0] if single else shapes,
        in_specs=[pl.BlockSpec(memory_space=pltpu.VMEM)] * len(args),
        out_specs=specs[0] if single else specs,
        compiler_params=PARAMS,
    )(*args)


def struct(shape, dtype):
    return jax.ShapeDtypeStruct(shape, dtype)


def pack_kernel(ph, pe, gain, out):
    out[:, CW:] = jnp.zeros((WROWS, L - CW), BF)
    out[0:FD, 0:CW] = ph[...]
    out[FD : 2 * FD, 0:CW] = pe[...]
    hi, rest = split(gain[...])
    mid, low = split(rest)
    row = iota((16, CW), 0)
    out[2 * FD :, 0:CW] = jnp.where(row == 0, hi, jnp.where(row == 1, mid, jnp.where(row == 2, low, 0.0))).astype(BF)


def pick_kernel(tokens, table, out):
    base = lax.axis_index("vocab") * VD
    units = NY * NX
    rows = NC * units * 8
    tok = tokens[...]
    part = iota((8, ROWS), 0)
    high = jnp.broadcast_to(tok >> 8, (8, ROWS)).astype(F32)
    low = jnp.broadcast_to(tok & 255, (8, ROWS)).astype(F32)
    codes = jnp.where(part == 0, high, jnp.where(part == 1, low, 0.0)).astype(BF)
    pos = iota((rows, ROWS), 0)
    step, unit, core = pos & 7, (pos >> 3) & (units - 1), pos >> 8
    source = (unit * NC + core) * UR + step
    select = ((iota((rows, ROWS), 1) == source) & (step < UR)).astype(F32).astype(BF)
    found = lax.dot_general(select, codes, (((1,), (1,)), ((), ())), preferred_element_type=F32)
    local = (found[:, 0:1] * 256.0 + found[:, 1:2]).astype(jnp.int32) - base
    local = jnp.where((iota((rows, 1), 0) & 7) < UR, local, -1)
    for start in range(0, rows, 128):
        hot = (iota((128, VD), 1) == local[start : start + 128]).astype(F32).astype(BF)
        out[start : start + 128, :] = jnp.dot(hot, table[...], preferred_element_type=F32).astype(BF)


def proj_kernel(picked, hidden, hidden_gain, embed_gain, weights, out):
    y = lax.axis_index("vocab") // (NX * NC)
    h = hidden[pl.ds(pl.multiple_of(y * RB, 16), RB), :].astype(F32)
    row, col = iota((RB, 64), 0), iota((RB, 64), 1)
    source = (row // UR) * 8 + row % UR
    select = (col == source).astype(F32).astype(BF)
    e = jnp.dot(select, picked[...], preferred_element_type=F32)
    lane = iota((RB, L), 1)

    def extra(x):
        hi, low = split(jnp.sum(x * x, axis=1, keepdims=True))
        return jnp.where(lane == CW, hi, jnp.where(lane == CW + 1, low, 0.0))

    extra_h, extra_e = extra(h), extra(e)
    hg = (h * hidden_gain[...]).astype(BF)
    eg = (e * embed_gain[...]).astype(BF)
    for t in range(NY):
        out[t, 0:RB, :] = (jnp.dot(hg, weights[t, 0:FD, :], preferred_element_type=F32) + extra_h).astype(BF)
        out[t, RB : 2 * RB, :] = (
            jnp.dot(eg, weights[t, FD : 2 * FD, :], preferred_element_type=F32) + extra_e
        ).astype(BF)
        out[t, 2 * RB :, :] = weights[t, 2 * FD :, :]


def join_kernel(parts, out):
    total = parts[0].astype(F32)
    gain = jnp.sum(total[2 * RB :, :], axis=0, keepdims=True)
    for k in range(1, NZ):
        total = total + parts[k].astype(F32)
    lane = iota((RB, L), 1)
    sides = (lane == CW) | (lane == CW + 1)

    def scale(x):
        return lax.rsqrt(jnp.sum(jnp.where(sides, x, 0.0), axis=1, keepdims=True) / D + EPS)

    h, e = total[0:RB], total[RB : 2 * RB]
    inv_h = scale(h)
    projected = jnp.where(lane < CW, h * inv_h + e * scale(e), 0.0)
    sq_hi, sq_low = split(jnp.sum(projected * projected, axis=1, keepdims=True))
    h_hi, h_low = split(inv_h)
    x = projected * gain
    for k, v in enumerate((sq_hi, sq_low, h_hi, h_low)):
        x = jnp.where(lane == CW + k, v, x)
    out[...] = jnp.broadcast_to(x.astype(BF)[None], out.shape)


def head_kernel(rows, head, out, x_ref):
    squares = jnp.zeros((ROWS, L), F32)
    for x in range(NX):
        for c in range(NC):
            a = jnp.concatenate([rows[c, y * NX + x] for y in range(NY)], axis=0)
            j = x * NC + c
            x_ref[:, j * CW : (j + 1) * CW] = a[:, 0:CW]
            squares = squares + a.astype(F32)
            if j == 0:
                scales = a.astype(F32)
    lane = iota((ROWS, L), 1)
    sq = jnp.sum(jnp.where((lane == CW) | (lane == CW + 1), squares, 0.0), axis=1, keepdims=True)
    inv_h = jnp.sum(jnp.where((lane == CW + 2) | (lane == CW + 3), scales, 0.0), axis=1, keepdims=True)
    diagonal = iota((RB, L), 0) == iota((RB, L), 1)
    part = iota((8, L), 0)
    for k in range(NZ):
        tail = jnp.zeros((8, L), F32)
        for n, col in enumerate((sq, inv_h)):
            line = jnp.sum(jnp.where(diagonal, col[k * RB : (k + 1) * RB], 0.0), axis=0, keepdims=True)
            hi, low = split(line)
            tail = jnp.where(part == 2 * n, hi, jnp.where(part == 2 * n + 1, low, tail))
        out[k, HROWS - 8 :, :] = tail.astype(BF)
    for n in range(0, VD, 256):
        acc = jnp.dot(x_ref[...], head[:, n : n + 256], preferred_element_type=F32).astype(BF)
        for m in range(2):
            tile = n // L + m
            for k in range(NZ):
                out[k, tile * RB : (tile + 1) * RB, :] = acc[k * RB : (k + 1) * RB, m * L : (m + 1) * L]


def stats_kernel(parts, main, main_out, draft_out, stats):
    diagonal = iota((RB, L), 0) == iota((RB, L), 1)

    def column(line):
        return jnp.sum(jnp.where(diagonal, line, 0.0), axis=1, keepdims=True)

    def line(col):
        return jnp.sum(jnp.where(diagonal, col, 0.0), axis=0, keepdims=True)

    tail = parts[0, HROWS - 8 :, :].astype(F32)
    inv_h = column(tail[2:3] + tail[3:4])
    for k in range(1, NZ):
        tail = tail + parts[k, HROWS - 8 :, :].astype(F32)
    inv_d = lax.rsqrt(column(tail[0:1] + tail[1:2]) / D + EPS)
    main_logits = main[...] * inv_h
    main_out[...] = main_logits
    for t in range(VD // L):
        acc = parts[0, t * RB : (t + 1) * RB, :].astype(F32)
        for k in range(1, NZ):
            acc = acc + parts[k, t * RB : (t + 1) * RB, :].astype(F32)
        draft_out[:, t * L : (t + 1) * L] = acc * inv_d
    draft_logits = draft_out[...]
    part = iota((8, L), 0)
    value = jnp.zeros((8, L), F32)
    for n, logits in enumerate((main_logits, draft_logits)):
        top = jnp.max(logits, axis=1, keepdims=True)
        total = jnp.sum(jnp.exp(logits - top), axis=1, keepdims=True)
        value = jnp.where(part == 2 * n, line(top), jnp.where(part == 2 * n + 1, line(total), value))
    stats[...] = jnp.broadcast_to(value[None], stats.shape)


def final_kernel(stats, main, draft, main_out, draft_out):
    diagonal = iota((RB, L), 0) == iota((RB, L), 1)
    every = stats[...]
    for n, (logits, out) in enumerate(((main, main_out), (draft, draft_out))):
        tops, sums = every[:, 2 * n, :], every[:, 2 * n + 1, :]
        top = jnp.max(tops, axis=0, keepdims=True)
        total = jnp.sum(sums * jnp.exp(tops - top), axis=0, keepdims=True)
        top_col = jnp.sum(jnp.where(diagonal, top, 0.0), axis=1, keepdims=True)
        log_col = jnp.log(jnp.sum(jnp.where(diagonal, total, 0.0), axis=1, keepdims=True))
        out[...] = (logits[...] - top_col - log_col).astype(BF)


def exchange(x, groups):
    return lax.all_to_all(x, "vocab", 0, 0, axis_index_groups=groups)


def per_device(
    hidden,
    tokens,
    final_gain,
    hidden_gain,
    embed_gain,
    embed_table,
    proj_hidden,
    proj_embed,
    draft_gain,
    head_weight,
):
    packed = call(pack_kernel, struct((WROWS, L), BF), proj_hidden, proj_embed, draft_gain[None])
    weights = lax.all_gather(packed, "vocab", axis_index_groups=YS)

    picked = call(pick_kernel, struct((NC * NY * NX * 8, FD), BF), tokens[None], embed_table)
    half = exchange(picked.reshape(NC, NY * NX, 8, FD), CORE)
    half = half[0] + half[1]
    unit = jnp.sum(exchange(half, XY).astype(F32), axis=0).astype(BF)
    mine = exchange(jnp.broadcast_to(unit[None], (NX * NC, 8, FD)), XC).reshape(NX * NC * 8, FD)

    main_in = (hidden.astype(F32) * final_gain).astype(BF)
    main_part = jnp.dot(main_in, head_weight, preferred_element_type=F32)
    main = lax.psum_scatter(main_part, "dp", scatter_dimension=0, tiled=True)

    partial = call(
        proj_kernel, struct((NY, ZROWS, L), BF), mine, hidden, hidden_gain[None], embed_gain[None], weights
    )
    joined = call(join_kernel, struct((NY * NX, RB, L), BF), lax.all_to_all(partial, "dp", 0, 0))
    rows = lax.all_gather(exchange(joined, XY), "vocab", axis_index_groups=CORE)
    blocks = pl.pallas_call(
        head_kernel,
        out_shape=struct((NZ, HROWS, L), BF),
        in_specs=[pl.BlockSpec(memory_space=pltpu.VMEM)] * 2,
        out_specs=pl.BlockSpec(memory_space=pltpu.VMEM),
        scratch_shapes=[pltpu.VMEM((ROWS, FD), BF)],
        compiler_params=PARAMS,
    )(rows, head_weight)
    parts = lax.all_to_all(blocks, "dp", 0, 0)
    main_logits, draft_logits, stats = call(
        stats_kernel,
        (struct((RB, VD), F32), struct((RB, VD), F32), struct((NY * NX * NC, 8, L), F32)),
        parts,
        main,
    )
    stats = lax.all_to_all(stats, "vocab", 0, 0)
    main_logp, draft_logp = call(
        final_kernel, (struct((RB, VD), BF), struct((RB, VD), BF)), stats, main_logits, draft_logits
    )
    return (main_logp, draft_logp)


def solution(mesh):
    return jax.shard_map(
        per_device,
        mesh=mesh,
        in_specs=(
            P(None, "dp"),
            P(),
            P("dp"),
            P("dp"),
            P("dp"),
            P("vocab", "dp"),
            P("dp", "vocab"),
            P("dp", "vocab"),
            P("vocab"),
            P("dp", "vocab"),
        ),
        out_specs=(P("dp", "vocab"), P("dp", "vocab")),
        check_vma=False,
    )
```

time: 869 us -> 182 us (0.21)
  waiting for transfers between devices: 434 us -> 63.5 us
  blocking collectives: 396 us -> 71.1 us
  starting transfers between devices: 0.21 us -> 14.3 us
  matrix products: 12.9 us -> 2.14 us
  other arithmetic: 11.4 us -> 0.9 us
    psum x2 -> x0, waiting for transfers between devices: 276 us -> none  [the longest x1 201 us: embed_lookup(): return lax.psum(picked, 'vocab')]
    psum x3 -> x0, blocking collectives: 268 us -> none  [the longest x1 129 us: draft_scale(): squares = lax.psum(jnp.sum(projected * projected, axis=1), 'vocab')]
    pmax x1 -> x0, blocking collectives: 128 us -> none  [log_rows(): top = lax.pmax(jnp.max(logits, axis=1), 'vocab')]
    reduce_scatter x2 -> x1, waiting for transfers between devices: 79.7 us -> 0.03 us  [per_device(): main = lax.psum_scatter(main_part, 'dp', scatter_dimension=0, tiled=True)]
    all_to_all x0 -> x4, blocking collectives: none -> 64.4 us  [the longest x2 29.6 us: exchange(): return lax.all_to_all(x, 'vocab', 0, 0, axis_index_groups=groups)]
    all_gather x1, waiting for transfers between devices: 78.3 us -> 17.2 us  [per_device(): weights = lax.all_gather(packed, 'vocab', axis_index_groups=YS)]
    all_to_all x0 -> x3, waiting for transfers between devices: none -> 46.2 us  [the longest x1 23.9 us: per_device(): parts = lax.all_to_all(blocks, 'dp', 0, 0)]
    all_to_all x0 -> x3, starting transfers between devices: none -> 14.2 us  [the longest x2 10.7 us: exchange(): return lax.all_to_all(x, 'vocab', 0, 0, axis_index_groups=groups)]
  transfers between devices with their start and end apart: 5 -> 5, of which waited for: 5 -> 4; matrix products, arithmetic and copies ran while one was open for 1% -> 2% of each run, Pallas kernels for 0% -> 3%
where the time goes in v1:
time: 182 us
  blocking collectives  71.1 us (39%)
  waiting for transfers between devices  63.5 us (35%)
  between operations  15.6 us (9%)
  starting transfers between devices  14.3 us (8%)
  local copies, waits for them, and re-layouts  7.33 us (4%)
  Pallas kernels  6.86 us (4%)
  matrix products  2.14 us (1%)
    all_to_all x2, blocking collectives, exchange(): return lax.all_to_all(x, 'vocab', 0, 0, axis_index_groups=groups)  29.6 us
    all_to_all x1, waiting for transfers between devices, per_device(): parts = lax.all_to_all(blocks, 'dp', 0, 0)  23.9 us
    all_to_all x2, waiting for transfers between devices, exchange(): return lax.all_to_all(x, 'vocab', 0, 0, axis_index_groups=groups)  22.4 us
    all_to_all x1, blocking collectives, per_device(): stats = lax.all_to_all(stats, 'vocab', 0, 0)  17.8 us
    all_gather x1, waiting for transfers between devices, per_device(): weights = lax.all_gather(packed, 'vocab', axis_index_groups=YS)  17.2 us
    all_to_all x1, blocking collectives, per_device(): lax.all_to_all(partial, 'dp', 0, 0)  17.1 us
    all_to_all x2, starting transfers between devices, exchange(): return lax.all_to_all(x, 'vocab', 0, 0, axis_index_groups=groups)  10.7 us
    all_gather x1, blocking collectives, per_device(): rows = lax.all_gather(exchange(joined, XY), 'vocab', axis_index_groups=CORE)  6.7 us
  transfers between devices with their start and end apart: 5, of which 4 were waited for; matrix products, arithmetic and copies ran while one was open for 2% of the time, Pallas kernels for 3%

profile of v1, /device:TPU:1, one launch (start us, length us, event | category | flops | bytes accessed | tf_op | source)
XLA Modules:
  0.0 181.7 jit_solution(12375062443260529802)
XLA Ops:
  8.0 0.0 copy-start.1
  8.0 0.0 all-gather.4.cloned.1.call-start
  8.1 1.2 copy.14.ph
  9.3 1.1 copy.15.pe
  10.4 0.0 copy-start.5
  10.4 0.6 copy-done.5
  11.0 1.0 shard_map.114
  12.0 0.0 all-gather.4.cloned.1.call-update
  12.0 0.7 broadcast_in_dim.19.tokens
  12.7 0.0 copy-done.1
  12.7 1.6 shard_map.113
  14.3 0.0 copy-start.2
  14.4 0.0 copy-start.3
  14.4 0.0 copy-start.8
  14.4 11.1 %all_to_all.35 = bf16[2,32,8,896]{3,2,1,0:T(8,128)(2,1)S(1)} all-to-all(bf16[2,32,8,896]{3,2,1,0:T(8,128)(2,1)S(1)} %bitcast.9), channel_id=1, replica_groups={{0,1},{2,3},{4,5},{6,7},{8,9},{10,11},{12,13},{14,15},{16,17},{18,19},{..., dimensions={0} | all-to-all | bytes 1835008 | tf_op jit(solution)/shard_map/all_to_all | solution.py:213
  25.5 0.8 fusion.2
  26.3 4.3 %all-to-all-start.1 = ((bf16[32,8,896]{2,1,0:T(8,128)(2,1)}), bf16[32,8,896]{2,1,0:T(8,128)(2,1)S(1)}, u32[]{:S(2)}, u32[]{:S(2)}) async-start(bf16[32,8,896]{2,1,0:T(8,128)(2,1)} %fusion.2), calls=%async_computation.1 | async-start | bytes 917504 | tf_op jit(solution)/shard_map/all_to_all | solution.py:213
  30.6 0.0 reduce-scatter.2.cloned.1.call-start
  30.7 0.0 copy-done.2
  30.7 0.0 copy-done.3
  30.7 0.0 copy-done.8
  30.7 2.1 %fusion = f32[384,1024]{1,0:T(8,128)} fusion(bf16[896,1024]{1,0:T(8,128)(2,1)S(1)} %copy-done.2, bf16[384,896]{1,0:T(8,128)(2,1)S(1)} %copy-done.3, f32[896]{0:T(1024)S(1)} %copy-done.8), kind=kOutput, calls=%fused_computation.1 | convolution fusion | flops 705675264 | bytes 4099584 | tf_op jit(solution)/shard_map/dot_general | solution.py:238
  32.8 0.0 copy-start.6
  32.8 0.0 copy-start.7
  32.8 0.0 reduce-scatter.2.cloned.1.call-update
  32.9 17.2 %all-to-all-done.1 = bf16[32,8,896]{2,1,0:T(8,128)(2,1)S(1)} async-done(((bf16[32,8,896]{2,1,0:T(8,128)(2,1)}), bf16[32,8,896]{2,1,0:T(8,128)(2,1)S(1)}, u32[]{:S(2)}, u32[]{:S(2)}) %all-to-all-start.1) | async-done | bytes 458784 | tf_op jit(solution)/shard_map/all_to_all | solution.py:213
  50.1 0.1 reduce_sum.12
  50.2 0.7 broadcast_in_dim.20
  50.9 6.4 %all-to-all-start.2 = ((bf16[8,8,896]{2,1,0:T(8,128)(2,1)}), bf16[8,8,896]{2,1,0:T(8,128)(2,1)S(1)}, u32[]{:S(2)}, u32[]{:S(2)}) async-start(bf16[8,8,896]{2,1,0:T(8,128)(2,1)} %broadcast_in_dim.20), calls=%async_computation.2 | async-start | bytes 229376 | tf_op jit(solution)/shard_map/all_to_all | solution.py:213
  57.2 0.0 copy-done.6
  57.2 0.0 copy-done.7
  57.3 5.1 %all-to-all-done.2 = bf16[8,8,896]{2,1,0:T(8,128)(2,1)S(1)} async-done(((bf16[8,8,896]{2,1,0:T(8,128)(2,1)}), bf16[8,8,896]{2,1,0:T(8,128)(2,1)S(1)}, u32[]{:S(2)}, u32[]{:S(2)}) %all-to-all-start.2) | async-done | bytes 114720 | tf_op jit(solution)/shard_map/all_to_all | solution.py:213
  62.4 17.2 %all-gather.4.cloned.1.call-done = bf16[14464,128]{1,0:T(8,128)(2,1)} async-done(((bf16[1808,128]{1,0:T(8,128)(2,1)}), bf16[14464,128]{1,0:T(8,128)(2,1)}) %all-gather.4.cloned.1.call-update) | async-done | bytes 3702800 | tf_op jit(solution)/shard_map/all_gather | solution.py:229
  79.6 0.0 copy-start
  79.6 2.0 %copy-done = bf16[14464,128]{1,0:T(8,128)(2,1)S(1)} copy-done((bf16[14464,128]{1,0:T(8,128)(2,1)S(1)}, bf16[14464,128]{1,0:T(8,128)(2,1)}, u32[]{:S(2)}) %copy-start) | copy-done | bytes 3702808
  81.6 0.8 shard_map.115
  82.4 17.1 %all_to_all.36.parts = bf16[8,112,128]{2,1,0:T(8,128)(2,1)S(1)} all-to-all(bf16[8,112,128]{2,1,0:T(8,128)(2,1)S(1)} %shard_map.115), channel_id=1, replica_groups=mesh['dp'=8,'vocab'=64] {'dp'}, dimensions={0} | all-to-all | bytes 458752 | tf_op jit(solution)/shard_map/all_to_all | solution.py:244
  99.5 0.2 shard_map.116
  99.7 18.4 %all_to_all.37 = bf16[32,48,128]{2,1,0:T(8,128)(2,1)S(1)} all-to-all(bf16[32,48,128]{2,1,0:T(8,128)(2,1)S(1)} %shard_map.116), channel_id=1, replica_groups={{0,2,4,6,8,10,12,14,16,18,20,22,24,26,28,30,32,34,36,38,40,42,44,46,48,..., dimensions={0} | all-to-all | bytes 786432 | tf_op jit(solution)/shard_map/all_to_all | solution.py:213
  118.2 6.7 %all-gather.1 = bf16[64,48,128]{2,1,0:T(8,128)(2,1)S(1)} all-gather(bf16[32,48,128]{2,1,0:T(8,128)(2,1)S(1)} %all_to_all.37), channel_id=3, replica_groups={{0,1},{2,3},{4,5},{6,7},{8,9},{10,11},{12,13},{14,15},{16,17},{18,19},{..., dimensions={0}, use_global_device_ids=true | all-gather | bytes 1179648 | tf_op jit(solution)/shard_map/all_gather | solution.py:245
  124.9 2.0 %shard_map.117 = bf16[8,392,128]{2,1,0:T(8,128)(2,1)} custom-call(bf16[2,32,48,128]{3,2,1,0:T(8,128)(2,1)S(1)} %bitcast.10, bf16[896,1024]{1,0:T(8,128)(2,1)S(1)} %copy-done.2), custom_call_target="tpu_custom_call" | custom-call | tf_op jit(solution)/shard_map/pallas_call | solution.py:246
  126.9 3.5 %all-to-all-start.5 = ((bf16[8,392,128]{2,1,0:T(8,128)(2,1)}), bf16[8,392,128]{2,1,0:T(8,128)(2,1)S(1)}, u32[]{:S(2)}, u32[]{:S(2)}) async-start(bf16[8,392,128]{2,1,0:T(8,128)(2,1)} %shard_map.117), calls=%async_computation.5 | async-start | bytes 1605632 | tf_op jit(solution)/shard_map/all_to_all | solution.py:254
  130.5 0.0 reduce-scatter.2.cloned.1.call-done.main
  130.5 23.9 %all-to-all-done.5.parts = bf16[8,392,128]{2,1,0:T(8,128)(2,1)S(1)} async-done(((bf16[8,392,128]{2,1,0:T(8,128)(2,1)}), bf16[8,392,128]{2,1,0:T(8,128)(2,1)S(1)}, u32[]{:S(2)}, u32[]{:S(2)}) %all-to-all-start.5) | async-done | bytes 802848 | tf_op jit(solution)/shard_map/all_to_all | solution.py:254
  154.4 0.9 copy-done.4
  155.3 0.4 shard_map.118
  155.7 17.8 %all_to_all.38.stats = f32[64,8,128]{2,1,0:T(8,128)S(1)} all-to-all(f32[64,8,128]{2,1,0:T(8,128)S(1)} %get-tuple-element.5), channel_id=1, replica_groups=mesh['dp'=8,'vocab'=64] {'vocab'}, dimensions={0} | all-to-all | bytes 524288 | tf_op jit(solution)/shard_map/all_to_all | solution.py:261
  173.4 0.9 shard_map.119
  (3 shorter events, 0.0 us)
Async XLA Ops:
  8.0 4.7 %copy-start.1 = (bf16[1024,896]{1,0:T(8,128)(2,1)S(1)}, bf16[1024,896]{1,0:T(8,128)(2,1)}, u32[]{:S(2)}) copy-start(bf16[1024,896]{1,0:T(8,128)(2,1)} %table.1) | copy-start | bytes 5505028
  8.0 71.6 %all-gather.4.cloned.1.call-start = ((), (), s32[]{:S(2)}) async-start(), calls=%async_computation.9 | async-start | bytes 4165632 | tf_op jit(solution)/shard_map/all_gather | solution.py:229
  10.4 0.7 copy-start.5
  14.3 16.3 %copy-start.2 = (bf16[896,1024]{1,0:T(8,128)(2,1)S(1)}, bf16[896,1024]{1,0:T(8,128)(2,1)}, u32[]{:S(2)}) copy-start(bf16[896,1024]{1,0:T(8,128)(2,1)} %head.1) | copy-start | bytes 5505028
  14.4 16.3 %copy-start.3 = (bf16[384,896]{1,0:T(8,128)(2,1)S(1)}, bf16[384,896]{1,0:T(8,128)(2,1)}, u32[]{:S(2)}) copy-start(bf16[384,896]{1,0:T(8,128)(2,1)} %hidden.1) | copy-start | bytes 2064388
  14.4 16.3 %copy-start.8 = (f32[896]{0:T(1024)S(1)}, f32[896]{0:T(1024)}, u32[]{:S(2)}) copy-start(f32[896]{0:T(1024)} %param.12) | copy-start | bytes 10756
  26.3 23.8 %all-to-all-start.1 = ((bf16[32,8,896]{2,1,0:T(8,128)(2,1)}), bf16[32,8,896]{2,1,0:T(8,128)(2,1)S(1)}, u32[]{:S(2)}, u32[]{:S(2)}) async-start(bf16[32,8,896]{2,1,0:T(8,128)(2,1)} %fusion.2), calls=%async_computation.1 | async-start | bytes 917504 | tf_op jit(solution)/shard_map/all_to_all | solution.py:213
  30.6 99.9 %reduce-scatter.2.cloned.1.call-start = ((), (), s32[]{:S(2)}) async-start(), calls=%async_computation.8 | async-start | bytes 1769472 | tf_op jit(solution)/shard_map/reduce_scatter | solution.py:239
  32.8 24.4 %copy-start.6 = (f32[896]{0:T(1024)S(1)}, f32[896]{0:T(1024)}, u32[]{:S(2)}) copy-start(f32[896]{0:T(1024)} %param.13) | copy-start | bytes 10756
  32.8 24.4 %copy-start.7 = (f32[896]{0:T(1024)S(1)}, f32[896]{0:T(1024)}, u32[]{:S(2)}) copy-start(f32[896]{0:T(1024)} %param.14) | copy-start | bytes 10756
  50.9 11.5 %all-to-all-start.2 = ((bf16[8,8,896]{2,1,0:T(8,128)(2,1)}), bf16[8,8,896]{2,1,0:T(8,128)(2,1)S(1)}, u32[]{:S(2)}, u32[]{:S(2)}) async-start(bf16[8,8,896]{2,1,0:T(8,128)(2,1)} %broadcast_in_dim.20), calls=%async_computation.2 | async-start | bytes 229376 | tf_op jit(solution)/shard_map/all_to_all | solution.py:213
  79.6 2.0 %copy-start = (bf16[14464,128]{1,0:T(8,128)(2,1)S(1)}, bf16[14464,128]{1,0:T(8,128)(2,1)}, u32[]{:S(2)}) copy-start(bf16[14464,128]{1,0:T(8,128)(2,1)} %all-gather.4.cloned.1.call-done) | copy-start | bytes 11108356
  126.9 27.5 %all-to-all-start.5 = ((bf16[8,392,128]{2,1,0:T(8,128)(2,1)}), bf16[8,392,128]{2,1,0:T(8,128)(2,1)S(1)}, u32[]{:S(2)}, u32[]{:S(2)}) async-start(bf16[8,392,128]{2,1,0:T(8,128)(2,1)} %shard_map.117), calls=%async_computation.5 | async-start | bytes 1605632 | tf_op jit(solution)/shard_map/all_to_all | solution.py:254
  154.4 0.9 copy-start.4
Sparse Core Ops, SparseCore 0:
  12.1 67.4 all-gather.3
Sparse Core Ops, SparseCore 1:
  33.9 44.6 reduce-scatter.1

commit v2 on v0

v2 whole, which is shorter than its diff:
```python
import jax
import jax.numpy as jnp
from jax import lax
from jax.experimental import pallas as pl
from jax.experimental.pallas import tpu as pltpu
from jax.sharding import PartitionSpec as P

EPS = 1e-06
BF, F32 = jnp.bfloat16, jnp.float32
ROWS, D, V = 384, 7168, 65536
NZ, NY, NX, NC = 8, 8, 4, 2
NQ = NY * NX
FD = D // NZ
VD = V // (NQ * NC)
CW = D // (NQ * NC)
RB = ROWS // NZ
UR = ROWS // (NQ * NC)
PAIR = 2 * CW // NQ
L = 128
TILES = VD // L
ZR = NX * 8 + 16
HR = 2 * RB * TILES + 16
PARAMS = pltpu.CompilerParams(vmem_limit_bytes=48 * 1024 * 1024)


def vid(y, x, c):
    return (y * NX + x) * NC + c


CORE = [[vid(y, x, c) for c in range(NC)] for y in range(NY) for x in range(NX)]
XY = [[vid(y, x, c) for y in range(NY) for x in range(NX)] for c in range(NC)]


def iota(shape, dim):
    return lax.broadcasted_iota(jnp.int32, shape, dim)


def split(x):
    hi = x.astype(BF).astype(F32)
    return hi, x - hi


def ones(mask):
    return mask.astype(F32).astype(BF)


def dot(a, b):
    return jnp.dot(a, b, preferred_element_type=F32)


def dot_nt(a, b):
    return lax.dot_general(a, b, (((1,), (1,)), ((), ())), preferred_element_type=F32)


def dot_tn(a, b):
    return lax.dot_general(a, b, (((0,), (0,)), ((), ())), preferred_element_type=F32)


def line(col):
    same = iota((L, L), 0) == iota((L, L), 1)
    parts = [
        jnp.sum(jnp.where(same, col[k : k + L], 0.0), axis=0, keepdims=True) for k in range(0, col.shape[0], L)
    ]
    return jnp.concatenate(parts, axis=1)


def place(rows, shape):
    row = iota(shape, 0)
    out = jnp.zeros(shape, F32)
    for k, v in enumerate(rows):
        out = jnp.where(row == k, v, out)
    return out


def call(kernel, outs, *args, scratch=()):
    single = not isinstance(outs, (list, tuple))
    shapes = [outs] if single else list(outs)
    specs = [pl.BlockSpec(memory_space=pltpu.VMEM) for _ in shapes]
    return pl.pallas_call(
        kernel,
        out_shape=shapes[0] if single else shapes,
        in_specs=[pl.BlockSpec(memory_space=pltpu.VMEM)] * len(args),
        out_specs=specs[0] if single else specs,
        scratch_shapes=list(scratch),
        compiler_params=PARAMS,
    )(*args)


def struct(shape, dtype):
    return jax.ShapeDtypeStruct(shape, dtype)


def pick_kernel(tokens, table, out):
    base = lax.axis_index("vocab") * VD
    rows = NC * NQ * 8
    tok = tokens[...]
    part = iota((8, ROWS), 0)
    high = jnp.broadcast_to(tok >> 8, (8, ROWS)).astype(F32)
    low = jnp.broadcast_to(tok & 255, (8, ROWS)).astype(F32)
    codes = jnp.where(part == 0, high, jnp.where(part == 1, low, 0.0)).astype(BF)
    pos = iota((rows, ROWS), 0)
    step, unit, core = pos & 7, (pos >> 3) & (NQ - 1), pos >> 8
    source = (unit * NC + core) * UR + step
    found = dot_nt(ones((iota((rows, ROWS), 1) == source) & (step < UR)), codes)
    local = (found[:, 0:1] * 256.0 + found[:, 1:2]).astype(jnp.int32) - base
    local = jnp.where((iota((rows, 1), 0) & 7) < UR, local, -1)
    for start in range(0, rows, L):
        hot = ones(iota((L, VD), 1) == local[start : start + L])
        out[start : start + L, :] = dot(hot, table[...]).astype(BF)


def share_kernel(ph, pe, out):
    rows = NQ * 8
    both = jnp.concatenate([ph[...], pe[...]], axis=0)
    pos = iota((rows, 2 * CW), 0)
    unit, k, side = pos >> 3, pos & 3, (pos >> 2) & 1
    source = side * CW + (unit >> 1) * PAIR + (unit & 1) * 4 + k
    valid = k < 4 - (unit & 1)
    out[...] = dot(ones((iota((rows, 2 * CW), 1) == source) & valid), both).astype(BF)


def send_kernel(half, share, out):
    for k in range(NQ):
        rows = half[0, k].astype(F32) + half[1, k].astype(F32)
        out[k] = jnp.concatenate([rows, share[k].astype(F32)], axis=0).astype(BF)


def unit_kernel(got, gain, rows, weights):
    total = jnp.zeros((8, FD), F32)
    for k in range(NQ):
        block = got[k].astype(F32)
        total = total + block[0:8]
        weights[k] = block[8:16].astype(BF)
    hi, rest = split(gain[...])
    mid, low = split(rest)
    spare = jnp.concatenate([hi, mid, low, jnp.zeros((1, FD - 3 * L), F32)], axis=1)
    total = jnp.where(iota((8, FD), 0) == UR, spare, total)
    rows[...] = jnp.broadcast_to(total.astype(BF)[None], rows.shape)


def main_kernel(hidden, gain, head, out, squares):
    h = hidden[...].astype(F32)
    squares[...] = place([line(jnp.sum(h * h, axis=1, keepdims=True))], (8, ROWS))
    x = (h * gain[...]).astype(BF)
    for n in range(0, VD, 256):
        acc = dot(x, head[:, n : n + 256]).astype(BF)
        for m in range(2):
            t = n // L + m
            for k in range(NZ):
                out[k, t * RB : (t + 1) * RB, :] = acc[k * RB : (k + 1) * RB, m * L : (m + 1) * L]


def proj_kernel(picked, hidden, hidden_gain, embed_gain, weights, squares, out):
    pos, row = iota((ROWS, NC * NQ * 8), 1), iota((ROWS, NC * NQ * 8), 0)
    step, unit, core = pos & 7, (pos >> 3) & (NQ - 1), pos >> 8
    select = ones((row == (unit * NC + core) * UR + step) & (step < UR))
    e = dot(select, picked[...])
    e_sq = line(jnp.sum(e * e, axis=1, keepdims=True))
    hg = (hidden[...].astype(F32) * hidden_gain[...]).astype(BF)
    eg = (e * embed_gain[...]).astype(BF)
    w = weights[...]
    both = jnp.where((iota((NQ * 8, ROWS), 0) & 4) == 0, dot_nt(w, hg), dot_nt(w, eg)).astype(BF)
    tail = place([*split(squares[0:1, :]), *split(e_sq)], (16, ROWS)).astype(BF)
    for t in range(NY):
        out[t, 0 : NX * 8, :] = both[t * NX * 8 : (t + 1) * NX * 8]
        out[t, NX * 8 :, :] = tail


def join_kernel(parts, out):
    total = parts[0].astype(F32)
    for k in range(1, NZ):
        total = total + parts[k].astype(F32)
    n = NX * 8
    inv_h = lax.rsqrt((total[n : n + 1] + total[n + 1 : n + 2]) / D + EPS)
    inv_e = lax.rsqrt((total[n + 2 : n + 3] + total[n + 3 : n + 4]) / D + EPS)
    body = total[0:n]
    row = iota((16, n), 0)
    first = (row >> 2) * 8 + (row & 3)
    pick_h = (iota((16, n), 1) == first).astype(F32)
    pick_e = (iota((16, n), 1) == first + 4).astype(F32)
    exact = lax.Precision.HIGHEST
    joined = inv_h * jnp.dot(pick_h, body, precision=exact) + inv_e * jnp.dot(pick_e, body, precision=exact)
    out[...] = jnp.broadcast_to(joined.astype(BF)[None], out.shape)


def gained_kernel(picked, head, out, scaled):
    z = lax.axis_index("dp")
    same = iota((CW, L), 0) == iota((CW, L), 1)
    for x in range(NX):
        for c in range(NC):
            start = pl.multiple_of((c * NQ + z * NX + x // 2 * 2) * 8, 16)
            at = x % 2 * 8 + UR
            unit = picked[pl.ds(start, 16), :].astype(F32)[at : at + 1]
            gain = unit[:, 0:L] + unit[:, L : 2 * L] + unit[:, 2 * L : 3 * L]
            col = jnp.sum(jnp.where(same, gain, 0.0), axis=1, keepdims=True)
            j = (x * NC + c) * CW
            scaled[j : j + CW, :] = (head[j : j + CW, :].astype(F32) * col).astype(BF)
    rows = NC * NQ * 16
    pos = iota((rows, FD), 0)
    k, x, unit, core = pos & 3, (pos >> 2) & 3, (pos >> 4) & (NQ - 1), pos >> 9
    source = (x * NC + core) * CW + (unit >> 1) * PAIR + (unit & 1) * 4 + k
    select = ones((iota((rows, FD), 1) == source) & (k < 4 - (unit & 1)))
    for n in range(0, VD, 256):
        out[:, n : n + 256] = dot(select, scaled[:, n : n + 256]).astype(BF)


def head_kernel(columns, head, main, squares, out):
    x = columns[...]
    xf = x.astype(F32)
    d_sq = jnp.sum(xf * xf, axis=0, keepdims=True)
    tail = []
    for v in (*split(d_sq), *split(squares[0:1, :])):
        tail += [v[:, k * L : (k + 1) * L] for k in range(ROWS // L)]
    tail = place(tail, (16, L)).astype(BF)
    n_main = RB * TILES
    for k in range(NZ):
        out[k, 0:n_main, :] = main[k]
        out[k, 2 * n_main :, :] = tail
    xt = xf.T.astype(BF)
    for n in range(0, VD, 256):
        acc = dot(xt, head[:, n : n + 256]).astype(BF)
        for m in range(2):
            t = n_main + (n // L + m) * RB
            for k in range(NZ):
                out[k, t : t + RB, :] = acc[k * RB : (k + 1) * RB, m * L : (m + 1) * L]


def stats_kernel(parts, main_out, draft_out, stats):
    z = lax.axis_index("dp")
    n_main = RB * TILES
    tail = parts[0, 2 * n_main :, :].astype(F32)
    for k in range(1, NZ):
        tail = tail + parts[k, 2 * n_main :, :].astype(F32)
    row, lane = iota((RB, L), 0), iota((RB, L), 1)
    inverse = []
    for n in range(2):
        acc = jnp.zeros((RB, 1), F32)
        for k in range(ROWS // L):
            v = tail[6 * n + k : 6 * n + k + 1] + tail[6 * n + 3 + k : 6 * n + 4 + k]
            acc = acc + jnp.sum(jnp.where(lane + k * L == row + z * RB, v, 0.0), axis=1, keepdims=True)
        inverse.append(lax.rsqrt(acc / D + EPS))
    inv_d, inv_h = inverse
    values = []
    for start, inv, ref in ((0, inv_h, main_out), (n_main, inv_d, draft_out)):
        for t in range(TILES):
            s = start + t * RB
            acc = parts[0, s : s + RB, :].astype(F32)
            for k in range(1, NZ):
                acc = acc + parts[k, s : s + RB, :].astype(F32)
            ref[:, t * L : (t + 1) * L] = acc * inv
        logits = ref[...]
        top = jnp.max(logits, axis=1, keepdims=True)
        total = jnp.sum(jnp.exp(logits - top), axis=1, keepdims=True)
        for v in (top, total):
            values.append(jnp.sum(jnp.where(row == lane, v, 0.0), axis=0, keepdims=True))
    stats[...] = jnp.broadcast_to(place(values, (8, L))[None], stats.shape)


def final_kernel(stats, main, draft, main_out, draft_out):
    diagonal = iota((RB, L), 0) == iota((RB, L), 1)
    every = stats[...]
    for n, (logits, out) in enumerate(((main, main_out), (draft, draft_out))):
        tops, sums = every[:, 2 * n, :], every[:, 2 * n + 1, :]
        top = jnp.max(tops, axis=0, keepdims=True)
        total = jnp.sum(sums * jnp.exp(tops - top), axis=0, keepdims=True)
        top_col = jnp.sum(jnp.where(diagonal, top, 0.0), axis=1, keepdims=True)
        log_col = jnp.log(jnp.sum(jnp.where(diagonal, total, 0.0), axis=1, keepdims=True))
        out[...] = (logits[...] - top_col - log_col).astype(BF)


def exchange(x, groups):
    return lax.all_to_all(x, "vocab", 0, 0, axis_index_groups=groups)


def per_device(
    hidden,
    tokens,
    final_gain,
    hidden_gain,
    embed_gain,
    embed_table,
    proj_hidden,
    proj_embed,
    draft_gain,
    head_weight,
):
    picked = call(pick_kernel, struct((NC * NQ * 8, FD), BF), tokens[None], embed_table)
    share = call(share_kernel, struct((NQ * 8, FD), BF), proj_hidden.T, proj_embed.T)
    half = exchange(picked.reshape(NC, NQ, 8, FD), CORE)
    sent = call(send_kernel, struct((NQ, 16, FD), BF), half, share.reshape(NQ, 8, FD))
    gain = jnp.pad(draft_gain, (0, L - CW))[None]
    unit, weights = call(
        unit_kernel, (struct((NQ, 8, FD), BF), struct((NQ, 8, FD), BF)), exchange(sent, XY), gain
    )
    rows = lax.all_gather(exchange(unit, XY), "vocab", axis_index_groups=CORE).reshape(NC * NQ * 8, FD)

    main, squares = call(
        main_kernel,
        (struct((NZ, RB * TILES, L), BF), struct((8, ROWS), F32)),
        hidden,
        final_gain[None],
        head_weight,
    )
    partial = call(
        proj_kernel,
        struct((NZ, ZR, ROWS), BF),
        rows,
        hidden,
        hidden_gain[None],
        embed_gain[None],
        weights.reshape(NQ * 8, FD),
        squares,
    )
    gained = call(
        gained_kernel,
        struct((NC * NQ * 16, VD), BF),
        rows,
        head_weight,
        scratch=[pltpu.VMEM((FD, VD), BF)],
    )
    joined = call(join_kernel, struct((NQ, 16, ROWS), BF), lax.all_to_all(partial, "dp", 0, 0))
    columns = lax.all_gather(exchange(joined, XY), "vocab", axis_index_groups=CORE)
    blocks = call(
        head_kernel,
        struct((NZ, HR, L), BF),
        columns.reshape(NC * NQ * 16, ROWS),
        gained,
        main,
        squares,
    )
    main_logits, draft_logits, stats = call(
        stats_kernel,
        (struct((RB, VD), F32), struct((RB, VD), F32), struct((NQ * NC, 8, L), F32)),
        lax.all_to_all(blocks, "dp", 0, 0),
    )
    stats = lax.all_to_all(stats, "vocab", 0, 0)
    main_logp, draft_logp = call(
        final_kernel, (struct((RB, VD), BF), struct((RB, VD), BF)), stats, main_logits, draft_logits
    )
    return (main_logp, draft_logp)


def solution(mesh):
    return jax.shard_map(
        per_device,
        mesh=mesh,
        in_specs=(
            P(None, "dp"),
            P(),
            P("dp"),
            P("dp"),
            P("dp"),
            P("vocab", "dp"),
            P("dp", "vocab"),
            P("dp", "vocab"),
            P("vocab"),
            P("dp", "vocab"),
        ),
        out_specs=(P("dp", "vocab"), P("dp", "vocab")),
        check_vma=False,
    )
```

time: 869 us -> 188 us (0.22)
  waiting for transfers between devices: 434 us -> 47 us
  blocking collectives: 396 us -> 94.5 us
  starting transfers between devices: 0.21 us -> 25.3 us
  between operations: 13.9 us -> 0.85 us
  matrix products: 12.9 us -> 0 us
  other arithmetic: 11.4 us -> 0 us
  Pallas kernels: 0 us -> 11.3 us
    psum x2 -> x0, waiting for transfers between devices: 276 us -> none  [the longest x1 201 us: embed_lookup(): return lax.psum(picked, 'vocab')]
    psum x3 -> x0, blocking collectives: 268 us -> none  [the longest x1 129 us: draft_scale(): squares = lax.psum(jnp.sum(projected * projected, axis=1), 'vocab')]
    pmax x1 -> x0, blocking collectives: 128 us -> none  [log_rows(): top = lax.pmax(jnp.max(logits, axis=1), 'vocab')]
    all_to_all x0 -> x3, blocking collectives: none -> 83.4 us  [the longest x1 43.2 us: per_device(): lax.all_to_all(blocks, 'dp', 0, 0)]
    reduce_scatter x2 -> x0, waiting for transfers between devices: 79.7 us -> none  [vocab_head(): lax.psum_scatter(jnp.dot(normed, head_weight, preferred_element_type=jnp....]
    all_gather x1 -> x0, waiting for transfers between devices: 78.3 us -> none  [per_device(): whole = lax.all_gather(slab, 'vocab', axis=1, tiled=True)]
    all_to_all x0 -> x4, waiting for transfers between devices: none -> 47 us  [exchange(): return lax.all_to_all(x, 'vocab', 0, 0, axis_index_groups=groups)]
    all_to_all x0 -> x4, starting transfers between devices: none -> 25.3 us  [exchange(): return lax.all_to_all(x, 'vocab', 0, 0, axis_index_groups=groups)]
  transfers between devices with their start and end apart: 5 -> 4, of which waited for: 5 -> 4; matrix products, arithmetic and copies ran while one was open for 1% -> 0% of each run, Pallas kernels for 0% -> 2%
where the time goes in v2:
time: 188 us; the launch traced here: 187 us
  blocking collectives  94.5 us (50%)
  waiting for transfers between devices  47 us (25%)
  starting transfers between devices  25.3 us (13%)
  Pallas kernels  11.3 us (6%)
  local copies, waits for them, and re-layouts  8.36 us (4%)
    all_to_all x4, waiting for transfers between devices, exchange(): return lax.all_to_all(x, 'vocab', 0, 0, axis_index_groups=groups)  47 us
    all_to_all x1, blocking collectives, per_device(): lax.all_to_all(blocks, 'dp', 0, 0)  43.2 us
    all_to_all x4, starting transfers between devices, exchange(): return lax.all_to_all(x, 'vocab', 0, 0, axis_index_groups=groups)  25.3 us
    all_to_all x1, blocking collectives, per_device(): lax.all_to_all(partial, 'dp', 0, 0)  22 us
    all_to_all x1, blocking collectives, per_device(): stats = lax.all_to_all(stats, 'vocab', 0, 0)  18.2 us
    pallas_call x11, Pallas kernels, call(): pl.pallas_call(kernel, out_shape=shapes[0] if single else shapes, in_spec...  11.3 us
    unnamed x32, local copies, waits for them, and re-layouts  7.66 us
    all_gather x1, blocking collectives, per_device(): lax.all_gather(exchange(unit, XY), 'vocab', axis_index_groups=CORE)  5.62 us
  transfers between devices with their start and end apart: 4, of which 4 were waited for; matrix products, arithmetic and copies ran while one was open for 0% of the time, Pallas kernels for 2%

profile of v2, /device:TPU:1, one launch (start us, length us, event | category | flops | bytes accessed | tf_op | source)
XLA Modules:
  0.0 187.3 jit_solution(17673515476092042097)
XLA Ops:
  0.6 0.7 broadcast_in_dim.15.tokens
  1.3 0.0 copy-start.4
  1.3 1.5 copy-done.4
  2.8 0.0 copy-start.10
  2.8 2.6 %shard_map.113 = bf16[512,896]{1,0:T(8,128)(2,1)} custom-call(s32[1,384]{1,0:T(1,128)S(1)} %broadcast_in_dim.15.tokens, bf16[1024,896]{1,0:T(8,128)(2,1)S(1)} %copy-done.4), custom_call_target="tpu_custom_call" | custom-call | tf_op jit(solution)/shard_map/pallas_call | solution.py:79
  5.4 10.4 %all-to-all-start = ((bf16[2,32,8,896]{3,2,1,0:T(8,128)(2,1)}), bf16[2,32,8,896]{3,2,1,0:T(8,128)(2,1)S(1)}, u32[]{:S(2)}, u32[]{:S(2)}) async-start(bf16[2,32,8,896]{3,2,1,0:T(8,128)(2,1)} %bitcast), calls=%async_computation | async-start | bytes 1835008 | tf_op jit(solution)/shard_map/all_to_all | solution.py:272
  15.8 0.0 copy-done.10
  15.9 0.0 copy-done.11
  15.9 0.3 shard_map.114
  16.2 1.3 all-to-all-done.half
  17.5 0.1 shard_map.115
  17.6 0.0 copy-start.2
  17.6 0.9 copy-done.2
  18.6 0.0 copy-start.3
  18.6 4.4 %all-to-all-start.1 = ((bf16[32,16,896]{2,1,0:T(8,128)(2,1)}), bf16[32,16,896]{2,1,0:T(8,128)(2,1)S(1)}, u32[]{:S(2)}, u32[]{:S(2)}) async-start(bf16[32,16,896]{2,1,0:T(8,128)(2,1)} %copy-done.2), calls=%async_computation.1 | async-start | bytes 1835008 | tf_op jit(solution)/shard_map/all_to_all | solution.py:272
  23.0 0.0 copy-done.15
  23.1 23.9 %all-to-all-done.1.got = bf16[32,16,896]{2,1,0:T(8,128)(2,1)S(1)} async-done(((bf16[32,16,896]{2,1,0:T(8,128)(2,1)}), bf16[32,16,896]{2,1,0:T(8,128)(2,1)S(1)}, u32[]{:S(2)}, u32[]{:S(2)}) %all-to-all-start.1) | async-done | bytes 917536 | tf_op jit(solution)/shard_map/all_to_all | solution.py:272
  47.0 0.1 shard_map.116
  47.1 0.0 copy-start.7
  47.1 0.8 copy-done.7
  47.9 0.8 copy-done.9
  48.6 6.4 %all-to-all-start.2 = ((bf16[32,8,896]{2,1,0:T(8,128)(2,1)}), bf16[32,8,896]{2,1,0:T(8,128)(2,1)}, u32[]{:S(2)}, u32[]{:S(2)}) async-start(bf16[32,8,896]{2,1,0:T(8,128)(2,1)} %copy-done.9), calls=%async_computation.2 | async-start | bytes 917504 | tf_op jit(solution)/shard_map/all_to_all | solution.py:272
  55.0 0.0 copy-done.12
  55.1 0.0 copy-done.13
  55.1 0.0 copy-done.14
  55.1 0.0 copy-done
  55.1 0.0 copy-done.3
  55.1 1.0 shard_map.117
  56.1 0.0 copy-start.5
  56.1 13.2 %all-to-all-done.2 = bf16[32,8,896]{2,1,0:T(8,128)(2,1)} async-done(((bf16[32,8,896]{2,1,0:T(8,128)(2,1)}), bf16[32,8,896]{2,1,0:T(8,128)(2,1)}, u32[]{:S(2)}, u32[]{:S(2)}) %all-to-all-start.2) | async-done | bytes 458784 | tf_op jit(solution)/shard_map/all_to_all | solution.py:272
  69.3 5.6 %all-gather = bf16[64,8,896]{2,1,0:T(8,128)(2,1)S(1)} all-gather(bf16[32,8,896]{2,1,0:T(8,128)(2,1)} %all-to-all-done.2), channel_id=2, replica_groups={{0,1},{2,3},{4,5},{6,7},{8,9},{10,11},{12,13},{14,15},{16,17},{18,19},{..., dimensions={0}, use_global_device_ids=true | all-gather | bytes 1376256 | tf_op jit(solution)/shard_map/all_gather | solution.py:295
  74.9 1.0 copy-done.8
  75.9 1.1 shard_map.118
  77.0 0.0 copy-done.5
  77.0 22.0 %all_to_all.35.parts = bf16[8,48,384]{2,1,0:T(8,128)(2,1)S(1)} all-to-all(bf16[8,48,384]{2,1,0:T(8,128)(2,1)S(1)} %shard_map.118), channel_id=1, replica_groups=mesh['dp'=8,'vocab'=64] {'dp'}, dimensions={0} | all-to-all | bytes 589824 | tf_op jit(solution)/shard_map/all_to_all | solution.py:321
  99.1 1.0 shard_map.119
  100.1 4.1 %all-to-all-start.4 = ((bf16[32,16,384]{2,1,0:T(8,128)(2,1)}), bf16[32,16,384]{2,1,0:T(8,128)(2,1)S(1)}, u32[]{:S(2)}, u32[]{:S(2)}) async-start(bf16[32,16,384]{2,1,0:T(8,128)(2,1)} %shard_map.119), calls=%async_computation.4 | async-start | bytes 786432 | tf_op jit(solution)/shard_map/all_to_all | solution.py:272
  104.2 0.0 copy-start.1
  104.2 1.5 copy-done.1
  105.7 2.7 %shard_map.120.head = bf16[1024,1024]{1,0:T(8,128)(2,1)S(1)} custom-call(bf16[512,896]{1,0:T(8,128)(2,1)S(1)} %bitcast.10, bf16[896,1024]{1,0:T(8,128)(2,1)S(1)} %copy-done.1), custom_call_target="tpu_custom_call" | custom-call | tf_op jit(solution)/shard_map/pallas_call | solution.py:79
  108.4 8.6 %all-to-all-done.4 = bf16[32,16,384]{2,1,0:T(8,128)(2,1)S(1)} async-done(((bf16[32,16,384]{2,1,0:T(8,128)(2,1)}), bf16[32,16,384]{2,1,0:T(8,128)(2,1)S(1)}, u32[]{:S(2)}, u32[]{:S(2)}) %all-to-all-start.4) | async-done | bytes 393248 | tf_op jit(solution)/shard_map/all_to_all | solution.py:272
  117.0 5.4 %all-gather.1 = bf16[64,16,384]{2,1,0:T(8,128)(2,1)S(1)} all-gather(bf16[32,16,384]{2,1,0:T(8,128)(2,1)S(1)} %all-to-all-done.4), channel_id=3, replica_groups={{0,1},{2,3},{4,5},{6,7},{8,9},{10,11},{12,13},{14,15},{16,17},{18,19},{..., dimensions={0}, use_global_device_ids=true | all-gather | bytes 1179648 | tf_op jit(solution)/shard_map/all_gather | solution.py:322
  122.4 1.1 copy-done.6
  123.6 1.0 shard_map.121
  124.6 43.2 %all_to_all.36.parts = bf16[8,784,128]{2,1,0:T(8,128)(2,1)S(1)} all-to-all(bf16[8,784,128]{2,1,0:T(8,128)(2,1)S(1)} %shard_map.121), channel_id=1, replica_groups=mesh['dp'=8,'vocab'=64] {'dp'}, dimensions={0} | all-to-all | bytes 3211264 | tf_op jit(solution)/shard_map/all_to_all | solution.py:334
  167.8 0.4 shard_map.122
  168.2 18.2 %all_to_all.37.stats = f32[64,8,128]{2,1,0:T(8,128)S(1)} all-to-all(f32[64,8,128]{2,1,0:T(8,128)S(1)} %get-tuple-element.13), channel_id=1, replica_groups=mesh['dp'=8,'vocab'=64] {'vocab'}, dimensions={0} | all-to-all | bytes 524288 | tf_op jit(solution)/shard_map/all_to_all | solution.py:336
  186.5 0.9 shard_map.123
  (13 shorter events, 0.0 us)
Async XLA Ops:
  1.3 1.5 copy-start.4
  2.8 13.0 %copy-start.10 = (bf16[896,112]{0,1:T(8,128)(2,1)S(1)}, bf16[896,112]{0,1:T(8,128)(2,1)}, u32[]{:S(2)}) copy-start(bf16[896,112]{0,1:T(8,128)(2,1)} %param.16) | copy-start | bytes 602116
  2.8 13.0 %copy-start.11 = (bf16[896,112]{0,1:T(8,128)(2,1)S(1)}, bf16[896,112]{0,1:T(8,128)(2,1)}, u32[]{:S(2)}) copy-start(bf16[896,112]{0,1:T(8,128)(2,1)} %param.17) | copy-start | bytes 602116
  5.4 12.1 %all-to-all-start = ((bf16[2,32,8,896]{3,2,1,0:T(8,128)(2,1)}), bf16[2,32,8,896]{3,2,1,0:T(8,128)(2,1)S(1)}, u32[]{:S(2)}, u32[]{:S(2)}) async-start(bf16[2,32,8,896]{3,2,1,0:T(8,128)(2,1)} %bitcast), calls=%async_computation | async-start | bytes 1835008 | tf_op jit(solution)/shard_map/all_to_all | solution.py:272
  17.5 5.5 %copy-start.15 = (f32[112]{0:T(128)S(1)}, f32[112]{0:T(128)}, u32[]{:S(2)}) copy-start(f32[112]{0:T(128)} %param.18) | copy-start | bytes 1348
  17.6 0.9 copy-start.2
  18.6 36.5 %copy-start.12 = (f32[896]{0:T(1024)S(1)}, f32[896]{0:T(1024)}, u32[]{:S(2)}) copy-start(f32[896]{0:T(1024)} %param.12) | copy-start | bytes 10756
  18.6 36.5 %copy-start.13 = (f32[896]{0:T(1024)S(1)}, f32[896]{0:T(1024)}, u32[]{:S(2)}) copy-start(f32[896]{0:T(1024)} %param.13) | copy-start | bytes 10756
  18.6 36.5 %copy-start.14 = (f32[896]{0:T(1024)S(1)}, f32[896]{0:T(1024)}, u32[]{:S(2)}) copy-start(f32[896]{0:T(1024)} %param.14) | copy-start | bytes 10756
  18.6 36.5 %copy-start = (bf16[896,1024]{1,0:T(8,128)(2,1)S(1)}, bf16[896,1024]{1,0:T(8,128)(2,1)}, u32[]{:S(2)}) copy-start(bf16[896,1024]{1,0:T(8,128)(2,1)} %head.3) | copy-start | bytes 5505028
  18.6 36.5 %copy-start.3 = (bf16[384,896]{1,0:T(8,128)(2,1)S(1)}, bf16[384,896]{1,0:T(8,128)(2,1)}, u32[]{:S(2)}) copy-start(bf16[384,896]{1,0:T(8,128)(2,1)} %hidden.3) | copy-start | bytes 2064388
  18.6 28.4 %all-to-all-start.1 = ((bf16[32,16,896]{2,1,0:T(8,128)(2,1)}), bf16[32,16,896]{2,1,0:T(8,128)(2,1)S(1)}, u32[]{:S(2)}, u32[]{:S(2)}) async-start(bf16[32,16,896]{2,1,0:T(8,128)(2,1)} %copy-done.2), calls=%async_computation.1 | async-start | bytes 1835008 | tf_op jit(solution)/shard_map/all_to_all | solution.py:272
  47.1 0.8 copy-start.7
  47.9 0.8 copy-start.9
  48.6 20.6 %all-to-all-start.2 = ((bf16[32,8,896]{2,1,0:T(8,128)(2,1)}), bf16[32,8,896]{2,1,0:T(8,128)(2,1)}, u32[]{:S(2)}, u32[]{:S(2)}) async-start(bf16[32,8,896]{2,1,0:T(8,128)(2,1)} %copy-done.9), calls=%async_computation.2 | async-start | bytes 917504 | tf_op jit(solution)/shard_map/all_to_all | solution.py:272
  56.1 20.9 %copy-start.5 = (bf16[8,384,128]{2,1,0:T(8,128)(2,1)}, bf16[8,384,128]{2,1,0:T(8,128)(2,1)S(1)}, u32[]{:S(2)}) copy-start(bf16[8,384,128]{2,1,0:T(8,128)(2,1)S(1)} %get-tuple-element.12.main) | copy-start | bytes 2359300
  74.9 1.0 copy-start.8
  100.1 16.9 %all-to-all-start.4 = ((bf16[32,16,384]{2,1,0:T(8,128)(2,1)}), bf16[32,16,384]{2,1,0:T(8,128)(2,1)S(1)}, u32[]{:S(2)}, u32[]{:S(2)}) async-start(bf16[32,16,384]{2,1,0:T(8,128)(2,1)} %shard_map.119), calls=%async_computation.4 | async-start | bytes 786432 | tf_op jit(solution)/shard_map/all_to_all | solution.py:272
  104.2 1.5 copy-start.1
  122.4 1.1 copy-start.6

commit v3 on v1

--- a/solution.py
+++ b/solution.py
@@ -1,5 +1,3 @@
-import functools
-
 import jax
 import jax.numpy as jnp
 from jax import lax
@@ -11,13 +9,15 @@
 BF, F32 = jnp.bfloat16, jnp.float32
 ROWS, D, V = 384, 7168, 65536
 NZ, NY, NX, NC = 8, 8, 4, 2
+NQ = NY * NX
 FD = D // NZ
-VD = V // (NY * NX * NC)
-CW = D // (NY * NX * NC)
+VD = V // (NQ * NC)
+CW = D // (NQ * NC)
 RB = ROWS // NZ
 UR = RB // (NX * NC)
+XR = NC * UR
 L = 128
-WROWS = 2 * FD + 16
+FT = FD // L
 ZROWS = 2 * RB + 16
 HROWS = RB * (VD // L) + 8
 PARAMS = pltpu.CompilerParams(vmem_limit_bytes=48 * 1024 * 1024)
@@ -42,7 +42,27 @@
     return hi, x - hi
 
 
-def call(kernel, outs, *args):
+def ones(mask):
+    return mask.astype(F32).astype(BF)
+
+
+def dot(a, b):
+    return jnp.dot(a, b, preferred_element_type=F32)
+
+
+def dot_nt(a, b):
+    return lax.dot_general(a, b, (((1,), (1,)), ((), ())), preferred_element_type=F32)
+
+
+def place(rows, shape):
+    row = iota(shape, 0)
+    out = jnp.zeros(shape, F32)
+    for k, v in enumerate(rows):
+        out = jnp.where(row == k, v, out)
+    return out
+
+
+def call(kernel, outs, *args, scratch=()):
     single = not isinstance(outs, (list, tuple))
     shapes = [outs] if single else list(outs)
     specs = [pl.BlockSpec(memory_space=pltpu.VMEM) for _ in shapes]
@@ -51,6 +71,7 @@
         out_shape=shapes[0] if single else shapes,
         in_specs=[pl.BlockSpec(memory_space=pltpu.VMEM)] * len(args),
         out_specs=specs[0] if single else specs,
+        scratch_shapes=list(scratch),
         compiler_params=PARAMS,
     )(*args)
 
@@ -59,44 +80,82 @@
     return jax.ShapeDtypeStruct(shape, dtype)
 
 
-def pack_kernel(ph, pe, gain, out):
-    out[:, CW:] = jnp.zeros((WROWS, L - CW), BF)
-    out[0:FD, 0:CW] = ph[...]
-    out[FD : 2 * FD, 0:CW] = pe[...]
-    hi, rest = split(gain[...])
-    mid, low = split(rest)
-    row = iota((16, CW), 0)
-    out[2 * FD :, 0:CW] = jnp.where(row == 0, hi, jnp.where(row == 1, mid, jnp.where(row == 2, low, 0.0))).astype(BF)
-
-
 def pick_kernel(tokens, table, out):
     base = lax.axis_index("vocab") * VD
-    units = NY * NX
-    rows = NC * units * 8
+    rows = NC * NQ * 8
     tok = tokens[...]
     part = iota((8, ROWS), 0)
     high = jnp.broadcast_to(tok >> 8, (8, ROWS)).astype(F32)
     low = jnp.broadcast_to(tok & 255, (8, ROWS)).astype(F32)
     codes = jnp.where(part == 0, high, jnp.where(part == 1, low, 0.0)).astype(BF)
     pos = iota((rows, ROWS), 0)
-    step, unit, core = pos & 7, (pos >> 3) & (units - 1), pos >> 8
+    step, unit, core = pos & 7, (pos >> 3) & (NQ - 1), pos >> 8
     source = (unit * NC + core) * UR + step
-    select = ((iota((rows, ROWS), 1) == source) & (step < UR)).astype(F32).astype(BF)
-    found = lax.dot_general(select, codes, (((1,), (1,)), ((), ())), preferred_element_type=F32)
+    found = dot_nt(ones((iota((rows, ROWS), 1) == source) & (step < UR)), codes)
     local = (found[:, 0:1] * 256.0 + found[:, 1:2]).astype(jnp.int32) - base
     local = jnp.where((iota((rows, 1), 0) & 7) < UR, local, -1)
-    for start in range(0, rows, 128):
-        hot = (iota((128, VD), 1) == local[start : start + 128]).astype(F32).astype(BF)
-        out[start : start + 128, :] = jnp.dot(hot, table[...], preferred_element_type=F32).astype(BF)
-
-
-def proj_kernel(picked, hidden, hidden_gain, embed_gain, weights, out):
+    for start in range(0, rows, L):
+        hot = ones(iota((L, VD), 1) == local[start : start + L])
+        out[start : start + L, :] = dot(hot, table[...]).astype(BF)
+
+
+def hidden_kernel(hidden, gain, ph, draft_gain, out):
+    pos = iota((ROWS, ROWS), 0)
+    source = (pos % NQ) * XR + pos // NQ
+    select = ones(iota((ROWS, ROWS), 1) == source)
+    x = dot(select, (hidden[...].astype(F32) * gain[...]).astype(BF)).astype(BF)
+    weights = jnp.concatenate([ph[...], jnp.zeros((L - CW, FD), BF)], axis=0)
+    side = dot_nt(x, weights)
+    for i in range(XR):
+        part = slice(i % FT * L, (i % FT + 1) * L)
+        out[i // FT * NQ : (i // FT + 1) * NQ, part] = side[i * NQ : (i + 1) * NQ].astype(BF)
+    for i, v in enumerate(split(draft_gain[...])):
+        n = XR - FT + i
+        out[NQ:, n * L : (n + 1) * L] = jnp.broadcast_to(v.astype(BF), (NQ, L))
+
+
+def send_kernel(half, side, out):
+    row = iota((8, FD), 0)
+    lines = side[...].astype(F32)
+    for k in range(NQ):
+        rows = half[0, k].astype(F32) + half[1, k].astype(F32)
+        rows = jnp.where(row == UR, lines[k : k + 1], rows)
+        out[k] = jnp.where(row == UR + 1, lines[NQ + k : NQ + k + 1], rows).astype(BF)
+
+
+def unit_kernel(got, out):
+    row = iota((8, FD), 0)
+    total = jnp.zeros((8, FD), F32)
+    first = [jnp.zeros((8, FD), F32) for _ in range(NX)]
+    second = [jnp.zeros((8, FD), F32) for _ in range(NX)]
+    for y in range(NY):
+        for x in range(NX):
+            block = got[y * NX + x].astype(F32)
+            total = total + block
+            first[x] = jnp.where(row == y, block[UR : UR + 1], first[x])
+            second[x] = jnp.where(row == y, block[UR + 1 : UR + 2], second[x])
+    for x in range(NX):
+        block = jnp.concatenate([total, first[x], second[x]], axis=0).astype(BF)
+        for c in range(NC):
+            out[x * NC + c] = block
+
+
+def proj_kernel(got, hidden, embed_gain, weights, out, side):
     y = lax.axis_index("vocab") // (NX * NC)
+    core = lax.axis_index("vocab") % NC
+    units = [got[k].astype(F32) for k in range(NX * NC)]
+    picked = jnp.concatenate([u[0:8] for u in units], axis=0).astype(BF)
+    for x in range(NX):
+        lines = jnp.where(core == 0, units[x * NC], units[x * NC + 1])[8:24]
+        for i in range(XR):
+            r, t = i // FT * 8, i % FT * L
+            at = (x * XR + i) * 8
+            side[at : at + 8, :] = lines[r : r + 8, t : t + L]
+    n = (XR - FT) * L
+    gain_hi, gain_low = lines[8:16, n : n + L], lines[8:16, n + L : n + 2 * L]
     h = hidden[pl.ds(pl.multiple_of(y * RB, 16), RB), :].astype(F32)
     row, col = iota((RB, 64), 0), iota((RB, 64), 1)
-    source = (row // UR) * 8 + row % UR
-    select = (col == source).astype(F32).astype(BF)
-    e = jnp.dot(select, picked[...], preferred_element_type=F32)
+    e = dot(ones(col == (row // UR) * 8 + row % UR), picked)
     lane = iota((RB, L), 1)
 
     def extra(x):
@@ -104,14 +163,13 @@
         return jnp.where(lane == CW, hi, jnp.where(lane == CW + 1, low, 0.0))
 
     extra_h, extra_e = extra(h), extra(e)
-    hg = (h * hidden_gain[...]).astype(BF)
     eg = (e * embed_gain[...]).astype(BF)
+    pad = jnp.zeros((L - CW, FD), BF)
     for t in range(NY):
-        out[t, 0:RB, :] = (jnp.dot(hg, weights[t, 0:FD, :], preferred_element_type=F32) + extra_h).astype(BF)
-        out[t, RB : 2 * RB, :] = (
-            jnp.dot(eg, weights[t, FD : 2 * FD, :], preferred_element_type=F32) + extra_e
-        ).astype(BF)
-        out[t, 2 * RB :, :] = weights[t, 2 * FD :, :]
+        w = jnp.concatenate([weights[t], pad], axis=0)
+        out[t, 0:RB, :] = (jnp.where(lane < CW, side[pl.ds(t, RB, stride=8), :], 0.0) + extra_h).astype(BF)
+        out[t, RB : 2 * RB, :] = (dot_nt(eg, w) + extra_e).astype(BF)
+        out[t, 2 * RB :, :] = place([gain_hi[t : t + 1], gain_low[t : t + 1]], (16, L)).astype(BF)
 
 
 def join_kernel(parts, out):
@@ -225,36 +283,42 @@
     draft_gain,
     head_weight,
 ):
-    packed = call(pack_kernel, struct((WROWS, L), BF), proj_hidden, proj_embed, draft_gain[None])
-    weights = lax.all_gather(packed, "vocab", axis_index_groups=YS)
-
-    picked = call(pick_kernel, struct((NC * NY * NX * 8, FD), BF), tokens[None], embed_table)
-    half = exchange(picked.reshape(NC, NY * NX, 8, FD), CORE)
-    half = half[0] + half[1]
-    unit = jnp.sum(exchange(half, XY).astype(F32), axis=0).astype(BF)
-    mine = exchange(jnp.broadcast_to(unit[None], (NX * NC, 8, FD)), XC).reshape(NX * NC * 8, FD)
+    weights = lax.all_gather(proj_embed.T, "vocab", axis_index_groups=YS)
+
+    picked = call(pick_kernel, struct((NC * NQ * 8, FD), BF), tokens[None], embed_table)
+    half = exchange(picked.reshape(NC, NQ, 8, FD), CORE)
+    gain = jnp.pad(draft_gain, (0, L - CW))[None]
+    side = call(hidden_kernel, struct((2 * NQ, FD), BF), hidden, hidden_gain[None], proj_hidden.T, gain)
+    sent = call(send_kernel, struct((NQ, 8, FD), BF), half, side)
+    unit = call(unit_kernel, struct((NX * NC, 24, FD), BF), exchange(sent, XY))
+    got = exchange(unit, XC)
 
     main_in = (hidden.astype(F32) * final_gain).astype(BF)
     main_part = jnp.dot(main_in, head_weight, preferred_element_type=F32)
     main = lax.psum_scatter(main_part, "dp", scatter_dimension=0, tiled=True)
 
     partial = call(
-        proj_kernel, struct((NY, ZROWS, L), BF), mine, hidden, hidden_gain[None], embed_gain[None], weights
-    )
-    joined = call(join_kernel, struct((NY * NX, RB, L), BF), lax.all_to_all(partial, "dp", 0, 0))
+        proj_kernel,
+        struct((NY, ZROWS, L), BF),
+        got,
+        hidden,
+        embed_gain[None],
+        weights,
+        scratch=[pltpu.VMEM((RB * 8, L), F32)],
+    )
+    joined = call(join_kernel, struct((NQ, RB, L), BF), lax.all_to_all(partial, "dp", 0, 0))
     rows = lax.all_gather(exchange(joined, XY), "vocab", axis_index_groups=CORE)
-    blocks = pl.pallas_call(
+    blocks = call(
         head_kernel,
-        out_shape=struct((NZ, HROWS, L), BF),
-        in_specs=[pl.BlockSpec(memory_space=pltpu.VMEM)] * 2,
-        out_specs=pl.BlockSpec(memory_space=pltpu.VMEM),
-        scratch_shapes=[pltpu.VMEM((ROWS, FD), BF)],
-        compiler_params=PARAMS,
-    )(rows, head_weight)
+        struct((NZ, HROWS, L), BF),
+        rows,
+        head_weight,
+        scratch=[pltpu.VMEM((ROWS, FD), BF)],
+    )
     parts = lax.all_to_all(blocks, "dp", 0, 0)
     main_logits, draft_logits, stats = call(
         stats_kernel,
-        (struct((RB, VD), F32), struct((RB, VD), F32), struct((NY * NX * NC, 8, L), F32)),
+        (struct((RB, VD), F32), struct((RB, VD), F32), struct((NQ * NC, 8, L), F32)),
         parts,
         main,
     )

time: 182 us -> 168 us (0.923)
  waiting for transfers between devices: 63.5 us -> 48.9 us
  blocking collectives: 71.1 us -> 60.5 us
  starting transfers between devices: 14.3 us -> 24.6 us
  Pallas kernels: 6.86 us -> 9.74 us
  local copies, waits for them, and re-layouts: 7.33 us -> 5.49 us
    all_gather x1, waiting for transfers between devices: 17.2 us -> 0.01 us  [per_device(): weights = lax.all_gather(proj_embed.T, 'vocab', axis_index_groups=YS)]
    all_to_all x2 -> x1, blocking collectives: 29.6 us -> 17.6 us  [exchange(): return lax.all_to_all(x, 'vocab', 0, 0, axis_index_groups=groups)]
    all_to_all x2 -> x3, starting transfers between devices: 10.7 us -> 21 us  [exchange(): return lax.all_to_all(x, 'vocab', 0, 0, axis_index_groups=groups)]
    pallas_call x6 -> x9, Pallas kernels: 4.82 us -> 9.74 us  [call(): pl.pallas_call(kernel, out_shape=shapes[0] if single else shapes, in_spec...]
    all_to_all x1, blocking collectives: 17.1 us -> 19.3 us  [per_device(): lax.all_to_all(partial, 'dp', 0, 0)]
    pallas_call x1 -> x0, Pallas kernels: 2.04 us -> none  [per_device(): pl.pallas_call(head_kernel, out_shape=struct((NZ, HROWS, L), BF), in_spec...]
    all_to_all x2 -> x3, waiting for transfers between devices: 22.4 us -> 24.4 us  [exchange(): return lax.all_to_all(x, 'vocab', 0, 0, axis_index_groups=groups)]
    unnamed x20 -> x18, local copies, waits for them, and re-layouts: 5.97 us -> 4.8 us
  transfers between devices with their start and end apart: 5 -> 6, of which waited for: 4 -> 3; matrix products, arithmetic and copies ran while one was open for 2% -> 2% of each run, Pallas kernels for 3% -> 5%
where the time goes in v3:
time: 168 us
  blocking collectives  60.5 us (36%)
  waiting for transfers between devices  48.9 us (29%)
  starting transfers between devices  24.6 us (15%)
  between operations  15.6 us (9%)
  Pallas kernels  9.74 us (6%)
  local copies, waits for them, and re-layouts  5.49 us (3%)
  matrix products  2.8 us (2%)
    all_to_all x3, waiting for transfers between devices, exchange(): return lax.all_to_all(x, 'vocab', 0, 0, axis_index_groups=groups)  24.4 us
    all_to_all x1, waiting for transfers between devices, per_device(): parts = lax.all_to_all(blocks, 'dp', 0, 0)  23.8 us
    all_to_all x3, starting transfers between devices, exchange(): return lax.all_to_all(x, 'vocab', 0, 0, axis_index_groups=groups)  21 us
    all_to_all x1, blocking collectives, per_device(): lax.all_to_all(partial, 'dp', 0, 0)  19.3 us
    all_to_all x1, blocking collectives, per_device(): stats = lax.all_to_all(stats, 'vocab', 0, 0)  17.9 us
    all_to_all x1, blocking collectives, exchange(): return lax.all_to_all(x, 'vocab', 0, 0, axis_index_groups=groups)  17.6 us
    pallas_call x9, Pallas kernels, call(): pl.pallas_call(kernel, out_shape=shapes[0] if single else shapes, in_spec...  9.74 us
    all_gather x1, blocking collectives, per_device(): rows = lax.all_gather(exchange(joined, XY), 'vocab', axis_index_groups=CORE)  5.64 us
  transfers between devices with their start and end apart: 6, of which 3 were waited for; matrix products, arithmetic and copies ran while one was open for 2% of the time, Pallas kernels for 5%

profile of v3, /device:TPU:1, one launch (start us, length us, event | category | flops | bytes accessed | tf_op | source)
XLA Modules:
  0.0 167.7 jit_solution(14883554314766787582)
XLA Ops:
  8.0 0.0 all-gather.4.cloned.1.call-start
  8.0 0.7 all-gather.4.cloned.1.call-update
  8.7 0.7 broadcast_in_dim.13.tokens
  9.4 0.0 copy-start.1
  9.4 1.5 copy-done.1
  10.9 2.7 %shard_map.113 = bf16[512,896]{1,0:T(8,128)(2,1)} custom-call(s32[1,384]{1,0:T(1,128)S(1)} %broadcast_in_dim.13.tokens, bf16[1024,896]{1,0:T(8,128)(2,1)S(1)} %copy-done.1), custom_call_target="tpu_custom_call" | custom-call | tf_op jit(solution)/shard_map/pallas_call | solution.py:69
  13.6 0.0 copy-start.6
  13.6 0.0 copy-start.8
  13.6 0.0 copy-start
  13.6 10.6 %all-to-all-start = ((bf16[2,32,8,896]{3,2,1,0:T(8,128)(2,1)}), bf16[2,32,8,896]{3,2,1,0:T(8,128)(2,1)S(1)}, u32[]{:S(2)}, u32[]{:S(2)}) async-start(bf16[2,32,8,896]{3,2,1,0:T(8,128)(2,1)} %bitcast), calls=%async_computation | async-start | bytes 1835008 | tf_op jit(solution)/shard_map/all_to_all | solution.py:271
  24.1 0.0 copy-done.6
  24.1 0.0 copy-done.8
  24.2 0.0 copy-done
  24.2 0.0 copy-start.4
  24.2 0.9 copy-done.4
  25.1 0.0 copy-start.2
  25.1 0.8 shard_map.114.side
  25.9 0.0 all-to-all-done.half
  25.9 1.0 shard_map.115
  26.9 4.3 %all-to-all-start.1 = ((bf16[32,8,896]{2,1,0:T(8,128)(2,1)}), bf16[32,8,896]{2,1,0:T(8,128)(2,1)S(1)}, u32[]{:S(2)}, u32[]{:S(2)}) async-start(bf16[32,8,896]{2,1,0:T(8,128)(2,1)} %shard_map.115), calls=%async_computation.1 | async-start | bytes 917504 | tf_op jit(solution)/shard_map/all_to_all | solution.py:271
  31.2 0.0 reduce-scatter.2.cloned.1.call-start
  31.3 0.0 copy-done.2
  31.3 2.8 %fusion = f32[384,1024]{1,0:T(8,128)} fusion(bf16[896,1024]{1,0:T(8,128)(2,1)S(1)} %copy-done.2, bf16[384,896]{1,0:T(8,128)(2,1)S(1)} %copy-done, f32[896]{0:T(1024)} %param.12), kind=kOutput, calls=%fused_computation.1 | convolution fusion | flops 705675264 | bytes 4099584 | tf_op jit(solution)/shard_map/dot_general | solution.py:297
  34.1 0.0 copy-start.7
  34.1 0.0 reduce-scatter.2.cloned.1.call-update
  34.1 17.1 %all-to-all-done.1.got = bf16[32,8,896]{2,1,0:T(8,128)(2,1)S(1)} async-done(((bf16[32,8,896]{2,1,0:T(8,128)(2,1)}), bf16[32,8,896]{2,1,0:T(8,128)(2,1)S(1)}, u32[]{:S(2)}, u32[]{:S(2)}) %all-to-all-start.1) | async-done | bytes 458784 | tf_op jit(solution)/shard_map/all_to_all | solution.py:271
  51.2 0.9 shard_map.116
  52.2 6.1 %all-to-all-start.2 = ((bf16[8,24,896]{2,1,0:T(8,128)(2,1)}), bf16[8,24,896]{2,1,0:T(8,128)(2,1)S(1)}, u32[]{:S(2)}, u32[]{:S(2)}) async-start(bf16[8,24,896]{2,1,0:T(8,128)(2,1)} %shard_map.116), calls=%async_computation.2 | async-start | bytes 688128 | tf_op jit(solution)/shard_map/all_to_all | solution.py:271
  58.3 0.0 copy-done.7
  58.3 7.3 %all-to-all-done.2.got = bf16[8,24,896]{2,1,0:T(8,128)(2,1)S(1)} async-done(((bf16[8,24,896]{2,1,0:T(8,128)(2,1)}), bf16[8,24,896]{2,1,0:T(8,128)(2,1)S(1)}, u32[]{:S(2)}, u32[]{:S(2)}) %all-to-all-start.2) | async-done | bytes 344096 | tf_op jit(solution)/shard_map/all_to_all | solution.py:271
  65.6 0.0 all-gather.4.cloned.1.call-done
  65.6 0.0 copy-start.3
  65.6 1.4 copy-done.3
  67.0 0.9 shard_map.117
  67.9 19.3 %all_to_all.35.parts = bf16[8,112,128]{2,1,0:T(8,128)(2,1)S(1)} all-to-all(bf16[8,112,128]{2,1,0:T(8,128)(2,1)S(1)} %shard_map.117), channel_id=1, replica_groups=mesh['dp'=8,'vocab'=64] {'dp'}, dimensions={0} | all-to-all | bytes 458752 | tf_op jit(solution)/shard_map/all_to_all | solution.py:309
  87.2 0.2 shard_map.118
  87.4 17.6 %all_to_all.36 = bf16[32,48,128]{2,1,0:T(8,128)(2,1)S(1)} all-to-all(bf16[32,48,128]{2,1,0:T(8,128)(2,1)S(1)} %shard_map.118), channel_id=1, replica_groups={{0,2,4,6,8,10,12,14,16,18,20,22,24,26,28,30,32,34,36,38,40,42,44,46,48,..., dimensions={0} | all-to-all | bytes 786432 | tf_op jit(solution)/shard_map/all_to_all | solution.py:271
  105.0 5.6 %all-gather.1 = bf16[64,48,128]{2,1,0:T(8,128)(2,1)S(1)} all-gather(bf16[32,48,128]{2,1,0:T(8,128)(2,1)S(1)} %all_to_all.36), channel_id=3, replica_groups={{0,1},{2,3},{4,5},{6,7},{8,9},{10,11},{12,13},{14,15},{16,17},{18,19},{..., dimensions={0}, use_global_device_ids=true | all-gather | bytes 1179648 | tf_op jit(solution)/shard_map/all_gather | solution.py:310
  110.7 2.0 %shard_map.119 = bf16[8,392,128]{2,1,0:T(8,128)(2,1)} custom-call(bf16[2,32,48,128]{3,2,1,0:T(8,128)(2,1)S(1)} %bitcast.8, bf16[896,1024]{1,0:T(8,128)(2,1)S(1)} %copy-done.2), custom_call_target="tpu_custom_call" | custom-call | tf_op jit(solution)/shard_map/pallas_call | solution.py:69
  112.7 3.5 %all-to-all-start.5 = ((bf16[8,392,128]{2,1,0:T(8,128)(2,1)}), bf16[8,392,128]{2,1,0:T(8,128)(2,1)S(1)}, u32[]{:S(2)}, u32[]{:S(2)}) async-start(bf16[8,392,128]{2,1,0:T(8,128)(2,1)} %shard_map.119), calls=%async_computation.5 | async-start | bytes 1605632 | tf_op jit(solution)/shard_map/all_to_all | solution.py:318
  116.3 0.0 reduce-scatter.2.cloned.1.call-done.main
  116.3 23.8 %all-to-all-done.5.parts = bf16[8,392,128]{2,1,0:T(8,128)(2,1)S(1)} async-done(((bf16[8,392,128]{2,1,0:T(8,128)(2,1)}), bf16[8,392,128]{2,1,0:T(8,128)(2,1)S(1)}, u32[]{:S(2)}, u32[]{:S(2)}) %all-to-all-start.5) | async-done | bytes 802848 | tf_op jit(solution)/shard_map/all_to_all | solution.py:318
  140.1 0.0 copy-start.5
  140.1 0.9 copy-done.5
  141.1 0.4 shard_map.120
  141.4 17.9 %all_to_all.37.stats = f32[64,8,128]{2,1,0:T(8,128)S(1)} all-to-all(f32[64,8,128]{2,1,0:T(8,128)S(1)} %get-tuple-element.5), channel_id=1, replica_groups=mesh['dp'=8,'vocab'=64] {'vocab'}, dimensions={0} | all-to-all | bytes 524288 | tf_op jit(solution)/shard_map/all_to_all | solution.py:325
  159.4 0.9 shard_map.121
  (3 shorter events, 0.0 us)
Async XLA Ops:
  8.0 57.6 %all-gather.4.cloned.1.call-start = ((), (), s32[]{:S(2)}) async-start(), calls=%async_computation.9 | async-start | bytes 1806336 | tf_op jit(solution)/shard_map/all_gather | solution.py:286
  9.4 1.5 copy-start.1
  13.6 10.6 %copy-start.6 = (f32[896]{0:T(1024)S(1)}, f32[896]{0:T(1024)}, u32[]{:S(2)}) copy-start(f32[896]{0:T(1024)} %param.13) | copy-start | bytes 10756
  13.6 10.6 %copy-start.8 = (f32[112]{0:T(128)S(1)}, f32[112]{0:T(128)}, u32[]{:S(2)}) copy-start(f32[112]{0:T(128)} %param.18) | copy-start | bytes 1348
  13.6 10.6 %copy-start = (bf16[384,896]{1,0:T(8,128)(2,1)S(1)}, bf16[384,896]{1,0:T(8,128)(2,1)}, u32[]{:S(2)}) copy-start(bf16[384,896]{1,0:T(8,128)(2,1)} %hidden.3) | copy-start | bytes 2064388
  13.6 12.3 %all-to-all-start = ((bf16[2,32,8,896]{3,2,1,0:T(8,128)(2,1)}), bf16[2,32,8,896]{3,2,1,0:T(8,128)(2,1)S(1)}, u32[]{:S(2)}, u32[]{:S(2)}) async-start(bf16[2,32,8,896]{3,2,1,0:T(8,128)(2,1)} %bitcast), calls=%async_computation | async-start | bytes 1835008 | tf_op jit(solution)/shard_map/all_to_all | solution.py:271
  24.2 0.9 copy-start.4
  25.1 6.2 %copy-start.2 = (bf16[896,1024]{1,0:T(8,128)(2,1)S(1)}, bf16[896,1024]{1,0:T(8,128)(2,1)}, u32[]{:S(2)}) copy-start(bf16[896,1024]{1,0:T(8,128)(2,1)} %head.1) | copy-start | bytes 5505028
  26.9 24.3 %all-to-all-start.1 = ((bf16[32,8,896]{2,1,0:T(8,128)(2,1)}), bf16[32,8,896]{2,1,0:T(8,128)(2,1)S(1)}, u32[]{:S(2)}, u32[]{:S(2)}) async-start(bf16[32,8,896]{2,1,0:T(8,128)(2,1)} %shard_map.115), calls=%async_computation.1 | async-start | bytes 917504 | tf_op jit(solution)/shard_map/all_to_all | solution.py:271
  31.2 85.1 %reduce-scatter.2.cloned.1.call-start = ((), (), s32[]{:S(2)}) async-start(), calls=%async_computation.8 | async-start | bytes 1769472 | tf_op jit(solution)/shard_map/reduce_scatter | solution.py:298
  34.1 24.2 %copy-start.7 = (f32[896]{0:T(1024)S(1)}, f32[896]{0:T(1024)}, u32[]{:S(2)}) copy-start(f32[896]{0:T(1024)} %param.14) | copy-start | bytes 10756
  52.2 13.4 %all-to-all-start.2 = ((bf16[8,24,896]{2,1,0:T(8,128)(2,1)}), bf16[8,24,896]{2,1,0:T(8,128)(2,1)S(1)}, u32[]{:S(2)}, u32[]{:S(2)}) async-start(bf16[8,24,896]{2,1,0:T(8,128)(2,1)} %shard_map.116), calls=%async_computation.2 | async-start | bytes 688128 | tf_op jit(solution)/shard_map/all_to_all | solution.py:271
  65.6 1.4 copy-start.3
  112.7 27.4 %all-to-all-start.5 = ((bf16[8,392,128]{2,1,0:T(8,128)(2,1)}), bf16[8,392,128]{2,1,0:T(8,128)(2,1)S(1)}, u32[]{:S(2)}, u32[]{:S(2)}) async-start(bf16[8,392,128]{2,1,0:T(8,128)(2,1)} %shard_map.119), calls=%async_computation.5 | async-start | bytes 1605632 | tf_op jit(solution)/shard_map/all_to_all | solution.py:318
  140.1 0.9 copy-start.5
Sparse Core Ops, SparseCore 0:
  10.9 51.4 all-gather.3
Sparse Core Ops, SparseCore 1:
  34.6 44.4 reduce-scatter.1

commit v4 on v3

--- a/solution.py
+++ b/solution.py
@@ -20,7 +20,6 @@
 FT = FD // L
 ZROWS = 2 * RB + 16
 HROWS = RB * (VD // L) + 8
-PARAMS = pltpu.CompilerParams(vmem_limit_bytes=48 * 1024 * 1024)
 
 
 def vid(y, x, c):
@@ -62,17 +61,17 @@
     return out
 
 
-def call(kernel, outs, *args, scratch=()):
+def call(kernel, outs, *args, scratch=(), far=(), room=48 * 1024):
     single = not isinstance(outs, (list, tuple))
     shapes = [outs] if single else list(outs)
     specs = [pl.BlockSpec(memory_space=pltpu.VMEM) for _ in shapes]
     return pl.pallas_call(
         kernel,
         out_shape=shapes[0] if single else shapes,
-        in_specs=[pl.BlockSpec(memory_space=pltpu.VMEM)] * len(args),
+        in_specs=[pl.BlockSpec(memory_space=pltpu.HBM if k in far else pltpu.VMEM) for k in range(len(args))],
         out_specs=specs[0] if single else specs,
         scratch_shapes=list(scratch),
-        compiler_params=PARAMS,
+        compiler_params=pltpu.CompilerParams(vmem_limit_bytes=room * 1024),
     )(*args)
 
 
@@ -80,7 +79,16 @@
     return jax.ShapeDtypeStruct(shape, dtype)
 
 
-def pick_kernel(tokens, table, out):
+def front_kernel(tokens, gain, draft_gain, hidden, ph, table, out, side, hidden_v, ph_v, table_v, sems):
+    copies = [
+        pltpu.make_async_copy(src, dst, sems.at[k])
+        for k, (src, dst) in enumerate(((hidden, hidden_v), (ph, ph_v), (table, table_v)))
+    ]
+    for copy in copies:
+        copy.start()
+    pos = iota((ROWS, ROWS), 0)
+    source = (pos % NQ) * XR + pos // NQ
+    select = ones(iota((ROWS, ROWS), 1) == source)
     base = lax.axis_index("vocab") * VD
     rows = NC * NQ * 8
     tok = tokens[...]
@@ -94,24 +102,21 @@
     found = dot_nt(ones((iota((rows, ROWS), 1) == source) & (step < UR)), codes)
     local = (found[:, 0:1] * 256.0 + found[:, 1:2]).astype(jnp.int32) - base
     local = jnp.where((iota((rows, 1), 0) & 7) < UR, local, -1)
+    copies[0].wait()
+    x = dot(select, (hidden_v[...].astype(F32) * gain[...]).astype(BF)).astype(BF)
+    copies[1].wait()
+    weights = jnp.concatenate([ph_v[...], jnp.zeros((L - CW, FD), BF)], axis=0)
+    lines = dot_nt(x, weights)
+    for i in range(XR):
+        part = slice(i % FT * L, (i % FT + 1) * L)
+        side[i // FT * NQ : (i // FT + 1) * NQ, part] = lines[i * NQ : (i + 1) * NQ].astype(BF)
+    for i, v in enumerate(split(draft_gain[...])):
+        n = XR - FT + i
+        side[NQ:, n * L : (n + 1) * L] = jnp.broadcast_to(v.astype(BF), (NQ, L))
+    copies[2].wait()
     for start in range(0, rows, L):
         hot = ones(iota((L, VD), 1) == local[start : start + L])
-        out[start : start + L, :] = dot(hot, table[...]).astype(BF)
-
-
-def hidden_kernel(hidden, gain, ph, draft_gain, out):
-    pos = iota((ROWS, ROWS), 0)
-    source = (pos % NQ) * XR + pos // NQ
-    select = ones(iota((ROWS, ROWS), 1) == source)
-    x = dot(select, (hidden[...].astype(F32) * gain[...]).astype(BF)).astype(BF)
-    weights = jnp.concatenate([ph[...], jnp.zeros((L - CW, FD), BF)], axis=0)
-    side = dot_nt(x, weights)
-    for i in range(XR):
-        part = slice(i % FT * L, (i % FT + 1) * L)
-        out[i // FT * NQ : (i // FT + 1) * NQ, part] = side[i * NQ : (i + 1) * NQ].astype(BF)
-    for i, v in enumerate(split(draft_gain[...])):
-        n = XR - FT + i
-        out[NQ:, n * L : (n + 1) * L] = jnp.broadcast_to(v.astype(BF), (NQ, L))
+        out[start : start + L, :] = dot(hot, table_v[...]).astype(BF)
 
 
 def send_kernel(half, side, out):
@@ -140,8 +145,15 @@
             out[x * NC + c] = block
 
 
-def proj_kernel(got, hidden, embed_gain, weights, out, side):
+def proj_kernel(got, hidden, embed_gain, weights, out, side, hidden_v, weights_v, sems):
     y = lax.axis_index("vocab") // (NX * NC)
+    mine = hidden.at[pl.ds(pl.multiple_of(y * RB, 16), RB), :]
+    copies = [
+        pltpu.make_async_copy(mine, hidden_v, sems.at[0]),
+        pltpu.make_async_copy(weights, weights_v, sems.at[1]),
+    ]
+    for copy in copies:
+        copy.start()
     core = lax.axis_index("vocab") % NC
     units = [got[k].astype(F32) for k in range(NX * NC)]
     picked = jnp.concatenate([u[0:8] for u in units], axis=0).astype(BF)
@@ -153,7 +165,8 @@
             side[at : at + 8, :] = lines[r : r + 8, t : t + L]
     n = (XR - FT) * L
     gain_hi, gain_low = lines[8:16, n : n + L], lines[8:16, n + L : n + 2 * L]
-    h = hidden[pl.ds(pl.multiple_of(y * RB, 16), RB), :].astype(F32)
+    copies[0].wait()
+    h = hidden_v[...].astype(F32)
     row, col = iota((RB, 64), 0), iota((RB, 64), 1)
     e = dot(ones(col == (row // UR) * 8 + row % UR), picked)
     lane = iota((RB, L), 1)
@@ -165,8 +178,9 @@
     extra_h, extra_e = extra(h), extra(e)
     eg = (e * embed_gain[...]).astype(BF)
     pad = jnp.zeros((L - CW, FD), BF)
+    copies[1].wait()
     for t in range(NY):
-        w = jnp.concatenate([weights[t], pad], axis=0)
+        w = jnp.concatenate([weights_v[t], pad], axis=0)
         out[t, 0:RB, :] = (jnp.where(lane < CW, side[pl.ds(t, RB, stride=8), :], 0.0) + extra_h).astype(BF)
         out[t, RB : 2 * RB, :] = (dot_nt(eg, w) + extra_e).astype(BF)
         out[t, 2 * RB :, :] = place([gain_hi[t : t + 1], gain_low[t : t + 1]], (16, L)).astype(BF)
@@ -202,20 +216,13 @@
             j = x * NC + c
             x_ref[:, j * CW : (j + 1) * CW] = a[:, 0:CW]
             squares = squares + a.astype(F32)
-            if j == 0:
-                scales = a.astype(F32)
     lane = iota((ROWS, L), 1)
     sq = jnp.sum(jnp.where((lane == CW) | (lane == CW + 1), squares, 0.0), axis=1, keepdims=True)
-    inv_h = jnp.sum(jnp.where((lane == CW + 2) | (lane == CW + 3), scales, 0.0), axis=1, keepdims=True)
     diagonal = iota((RB, L), 0) == iota((RB, L), 1)
     part = iota((8, L), 0)
     for k in range(NZ):
-        tail = jnp.zeros((8, L), F32)
-        for n, col in enumerate((sq, inv_h)):
-            line = jnp.sum(jnp.where(diagonal, col[k * RB : (k + 1) * RB], 0.0), axis=0, keepdims=True)
-            hi, low = split(line)
-            tail = jnp.where(part == 2 * n, hi, jnp.where(part == 2 * n + 1, low, tail))
-        out[k, HROWS - 8 :, :] = tail.astype(BF)
+        line = jnp.sum(jnp.where(diagonal, sq[k * RB : (k + 1) * RB], 0.0), axis=0, keepdims=True)
+        out[k, HROWS - 8 :, :] = place(split(line), (8, L)).astype(BF)
     for n in range(0, VD, 256):
         acc = jnp.dot(x_ref[...], head[:, n : n + 256], preferred_element_type=F32).astype(BF)
         for m in range(2):
@@ -224,47 +231,55 @@
                 out[k, tile * RB : (tile + 1) * RB, :] = acc[k * RB : (k + 1) * RB, m * L : (m + 1) * L]
 
 
-def stats_kernel(parts, main, main_out, draft_out, stats):
+def summary(logits):
     diagonal = iota((RB, L), 0) == iota((RB, L), 1)
-
-    def column(line):
-        return jnp.sum(jnp.where(diagonal, line, 0.0), axis=1, keepdims=True)
-
-    def line(col):
-        return jnp.sum(jnp.where(diagonal, col, 0.0), axis=0, keepdims=True)
-
+    top = jnp.max(logits, axis=1, keepdims=True)
+    total = jnp.sum(jnp.exp(logits - top), axis=1, keepdims=True)
+    return [jnp.sum(jnp.where(diagonal, v, 0.0), axis=0, keepdims=True) for v in (top, total)]
+
+
+def main_kernel(rows, sums, out, stats):
+    z = lax.axis_index("dp")
+    lane = iota((RB, L), 1)
+    block = rows[0, z * NX].astype(F32)
+    scale = jnp.sum(jnp.where((lane == CW + 2) | (lane == CW + 3), block, 0.0), axis=1, keepdims=True)
+    logits = sums[...] * scale
+    out[...] = logits
+    stats[...] = place(summary(logits), (8, L))
+
+
+def stats_kernel(parts, main_stats, out, stats):
+    diagonal = iota((RB, L), 0) == iota((RB, L), 1)
     tail = parts[0, HROWS - 8 :, :].astype(F32)
-    inv_h = column(tail[2:3] + tail[3:4])
     for k in range(1, NZ):
         tail = tail + parts[k, HROWS - 8 :, :].astype(F32)
-    inv_d = lax.rsqrt(column(tail[0:1] + tail[1:2]) / D + EPS)
-    main_logits = main[...] * inv_h
-    main_out[...] = main_logits
+    squares = jnp.sum(jnp.where(diagonal, tail[0:1] + tail[1:2], 0.0), axis=1, keepdims=True)
+    scale = lax.rsqrt(squares / D + EPS)
     for t in range(VD // L):
         acc = parts[0, t * RB : (t + 1) * RB, :].astype(F32)
         for k in range(1, NZ):
             acc = acc + parts[k, t * RB : (t + 1) * RB, :].astype(F32)
-        draft_out[:, t * L : (t + 1) * L] = acc * inv_d
-    draft_logits = draft_out[...]
-    part = iota((8, L), 0)
-    value = jnp.zeros((8, L), F32)
-    for n, logits in enumerate((main_logits, draft_logits)):
-        top = jnp.max(logits, axis=1, keepdims=True)
-        total = jnp.sum(jnp.exp(logits - top), axis=1, keepdims=True)
-        value = jnp.where(part == 2 * n, line(top), jnp.where(part == 2 * n + 1, line(total), value))
-    stats[...] = jnp.broadcast_to(value[None], stats.shape)
+        out[:, t * L : (t + 1) * L] = acc * scale
+    both = place([main_stats[0:1, :], main_stats[1:2, :], *summary(out[...])], (8, L))
+    stats[...] = jnp.broadcast_to(both[None], stats.shape)
 
 
 def final_kernel(stats, main, draft, main_out, draft_out):
+    top = stats[0]
+    for k in range(1, NQ * NC):
+        top = jnp.maximum(top, stats[k])
+    total = jnp.zeros((8, L), F32)
+    for k in range(NQ * NC):
+        total = total + stats[k] * pltpu.roll(jnp.exp(stats[k] - top), 1, 0)
     diagonal = iota((RB, L), 0) == iota((RB, L), 1)
-    every = stats[...]
+
+    def column(line):
+        return jnp.sum(jnp.where(diagonal, line, 0.0), axis=1, keepdims=True)
+
     for n, (logits, out) in enumerate(((main, main_out), (draft, draft_out))):
-        tops, sums = every[:, 2 * n, :], every[:, 2 * n + 1, :]
-        top = jnp.max(tops, axis=0, keepdims=True)
-        total = jnp.sum(sums * jnp.exp(tops - top), axis=0, keepdims=True)
-        top_col = jnp.sum(jnp.where(diagonal, top, 0.0), axis=1, keepdims=True)
-        log_col = jnp.log(jnp.sum(jnp.where(diagonal, total, 0.0), axis=1, keepdims=True))
-        out[...] = (logits[...] - top_col - log_col).astype(BF)
+        shift = column(top[2 * n : 2 * n + 1])
+        log_total = jnp.log(column(total[2 * n + 1 : 2 * n + 2]))
+        out[...] = (logits[...] - shift - log_total).astype(BF)
 
 
 def exchange(x, groups):
@@ -285,10 +300,26 @@
 ):
     weights = lax.all_gather(proj_embed.T, "vocab", axis_index_groups=YS)
 
-    picked = call(pick_kernel, struct((NC * NQ * 8, FD), BF), tokens[None], embed_table)
+    gain = jnp.pad(draft_gain, (0, L - CW))[None]
+    picked, side = call(
+        front_kernel,
+        (struct((NC * NQ * 8, FD), BF), struct((2 * NQ, FD), BF)),
+        tokens[None],
+        hidden_gain[None],
+        gain,
+        hidden,
+        proj_hidden.T,
+        embed_table,
+        far=(3, 4, 5),
+        room=63 * 1024,
+        scratch=[
+            pltpu.VMEM((ROWS, FD), BF),
+            pltpu.VMEM((CW, FD), BF),
+            pltpu.VMEM((VD, FD), BF),
+            pltpu.SemaphoreType.DMA((3,)),
+        ],
+    )
     half = exchange(picked.reshape(NC, NQ, 8, FD), CORE)
-    gain = jnp.pad(draft_gain, (0, L - CW))[None]
-    side = call(hidden_kernel, struct((2 * NQ, FD), BF), hidden, hidden_gain[None], proj_hidden.T, gain)
     sent = call(send_kernel, struct((NQ, 8, FD), BF), half, side)
     unit = call(unit_kernel, struct((NX * NC, 24, FD), BF), exchange(sent, XY))
     got = exchange(unit, XC)
@@ -304,7 +335,14 @@
         hidden,
         embed_gain[None],
         weights,
-        scratch=[pltpu.VMEM((RB * 8, L), F32)],
+        far=(1, 3),
+        room=64000,
+        scratch=[
+            pltpu.VMEM((RB * 8, L), F32),
+            pltpu.VMEM((RB, FD), BF),
+            pltpu.VMEM((NY, CW, FD), BF),
+            pltpu.SemaphoreType.DMA((2,)),
+        ],
     )
     joined = call(join_kernel, struct((NQ, RB, L), BF), lax.all_to_all(partial, "dp", 0, 0))
     rows = lax.all_gather(exchange(joined, XY), "vocab", axis_index_groups=CORE)
@@ -316,11 +354,9 @@
         scratch=[pltpu.VMEM((ROWS, FD), BF)],
     )
     parts = lax.all_to_all(blocks, "dp", 0, 0)
-    main_logits, draft_logits, stats = call(
-        stats_kernel,
-        (struct((RB, VD), F32), struct((RB, VD), F32), struct((NQ * NC, 8, L), F32)),
-        parts,
-        main,
+    main_logits, main_stats = call(main_kernel, (struct((RB, VD), F32), struct((8, L), F32)), rows, main)
+    draft_logits, stats = call(
+        stats_kernel, (struct((RB, VD), F32), struct((NQ * NC, 8, L), F32)), parts, main_stats
     )
     stats = lax.all_to_all(stats, "vocab", 0, 0)
     main_logp, draft_logp = call(

time: 168 us -> 174 us (1.036)
  blocking collectives: 60.5 us -> 74.5 us
  starting transfers between devices: 24.6 us -> 14 us
  Pallas kernels: 9.74 us -> 14.9 us
  waiting for transfers between devices: 48.9 us -> 45.9 us
    all_to_all x1 -> x2, blocking collectives: 17.6 us -> 29.4 us  [exchange(): return lax.all_to_all(x, 'vocab', 0, 0, axis_index_groups=groups)]
    all_to_all x3 -> x2, starting transfers between devices: 21 us -> 10.4 us  [exchange(): return lax.all_to_all(x, 'vocab', 0, 0, axis_index_groups=groups)]
    pallas_call x9, Pallas kernels: 9.74 us -> 14.9 us  [call(): pl.pallas_call(kernel, out_shape=shapes[0] if single else shapes, in_spec...]
    unnamed x18 -> x16, local copies, waits for them, and re-layouts: 4.8 us -> 1.7 us
    all_to_all x1, blocking collectives: 19.3 us -> 21.5 us  [per_device(): lax.all_to_all(partial, 'dp', 0, 0)]
    all_to_all x3 -> x2, waiting for transfers between devices: 24.4 us -> 22.5 us  [exchange(): return lax.all_to_all(x, 'vocab', 0, 0, axis_index_groups=groups)]
  transfers between devices with their start and end apart: 6 -> 5, of which waited for: 3 -> 3; matrix products, arithmetic and copies ran while one was open for 2% -> 4% of each run, Pallas kernels for 5% -> 8%
where the time goes in v4:
time: 174 us; the launch traced here: 173 us
  blocking collectives  74.5 us (43%)
  waiting for transfers between devices  45.9 us (26%)
  between operations  15.6 us (9%)
  Pallas kernels  14.9 us (9%)
  starting transfers between devices  14 us (8%)
  local copies, waits for them, and re-layouts  5.93 us (3%)
  matrix products  2.12 us (1%)
    all_to_all x2, blocking collectives, exchange(): return lax.all_to_all(x, 'vocab', 0, 0, axis_index_groups=groups)  29.4 us
    all_to_all x1, waiting for transfers between devices, per_device(): parts = lax.all_to_all(blocks, 'dp', 0, 0)  22.7 us
    all_to_all x2, waiting for transfers between devices, exchange(): return lax.all_to_all(x, 'vocab', 0, 0, axis_index_groups=groups)  22.5 us
    all_to_all x1, blocking collectives, per_device(): lax.all_to_all(partial, 'dp', 0, 0)  21.5 us
    all_to_all x1, blocking collectives, per_device(): stats = lax.all_to_all(stats, 'vocab', 0, 0)  17.9 us
    pallas_call x9, Pallas kernels, call(): pl.pallas_call(kernel, out_shape=shapes[0] if single else shapes, in_spec...  14.9 us
    all_to_all x2, starting transfers between devices, exchange(): return lax.all_to_all(x, 'vocab', 0, 0, axis_index_groups=groups)  10.4 us
    all_gather x1, blocking collectives, per_device(): rows = lax.all_gather(exchange(joined, XY), 'vocab', axis_index_groups=CORE)  5.62 us
  transfers between devices with their start and end apart: 5, of which 3 were waited for; matrix products, arithmetic and copies ran while one was open for 4% of the time, Pallas kernels for 8%

profile of v4, /device:TPU:1, one launch (start us, length us, event | category | flops | bytes accessed | tf_op | source)
XLA Modules:
  0.0 172.9 jit_solution(7256306229288144569)
XLA Ops:
  8.0 0.0 all-gather.4.cloned.1.call-start
  8.0 0.7 all-gather.4.cloned.1.call-update
  8.7 1.3 broadcast_in_dim.14.gain
  10.0 1.2 broadcast_in_dim.13.tokens
  11.2 1.1 pad_bitcast_fusion.draft_gain
  12.4 5.3 %shard_map.113 = (bf16[512,896]{1,0:T(8,128)(2,1)}, bf16[64,896]{1,0:T(8,128)(2,1)}) custom-call(s32[1,384]{1,0:T(1,128)} %broadcast_in_dim.13.tokens, f32[1,896]{1,0:T(1,128)} %broadcast_in_dim.14.gain, f32[1,128]{1,0:T(1,128)} %pad_bitcast_fusion.draft_gain, bf16[384,896]{1,0:T(8,128)(2,1)} %hidden.3, bf16[112,896]{1,0:T(8,128)(2,1)} %bitcast.13, ...), custom_call_target="tpu_custom_call" | custom-call | tf_op jit(solution)/shard_map/pallas_call | solution.py:68
  17.6 0.0 copy-start.3
  17.7 0.0 copy-start.4
  17.7 12.2 %all_to_all.35.half = bf16[2,32,8,896]{3,2,1,0:T(8,128)(2,1)S(1)} all-to-all(bf16[2,32,8,896]{3,2,1,0:T(8,128)(2,1)} %bitcast.11), channel_id=1, replica_groups={{0,1},{2,3},{4,5},{6,7},{8,9},{10,11},{12,13},{14,15},{16,17},{18,19},{..., dimensions={0} | all-to-all | bytes 1835008 | tf_op jit(solution)/shard_map/all_to_all | solution.py:286
  29.9 0.0 copy-start
  29.9 0.0 copy-start.7
  29.9 0.0 copy-done.3
  29.9 1.0 shard_map.114
  30.9 4.3 %all-to-all-start.1 = ((bf16[32,8,896]{2,1,0:T(8,128)(2,1)}), bf16[32,8,896]{2,1,0:T(8,128)(2,1)S(1)}, u32[]{:S(2)}, u32[]{:S(2)}) async-start(bf16[32,8,896]{2,1,0:T(8,128)(2,1)} %shard_map.114), calls=%async_computation.1 | async-start | bytes 917504 | tf_op jit(solution)/shard_map/all_to_all | solution.py:286
  35.2 0.0 reduce-scatter.2.cloned.1.call-start
  35.2 0.0 copy-done.4
  35.3 0.0 copy-done
  35.3 0.0 copy-done.7
  35.3 2.1 %fusion = f32[384,1024]{1,0:T(8,128)} fusion(bf16[896,1024]{1,0:T(8,128)(2,1)S(1)} %copy-done, bf16[384,896]{1,0:T(8,128)(2,1)S(1)} %copy-done.4, f32[896]{0:T(1024)S(1)} %copy-done.7), kind=kOutput, calls=%fused_computation.1 | convolution fusion | flops 705675264 | bytes 4099584 | tf_op jit(solution)/shard_map/dot_general | solution.py:328
  37.4 0.0 copy-start.6
  37.4 0.0 reduce-scatter.2.cloned.1.call-update
  37.4 15.8 %all-to-all-done.1.got = bf16[32,8,896]{2,1,0:T(8,128)(2,1)S(1)} async-done(((bf16[32,8,896]{2,1,0:T(8,128)(2,1)}), bf16[32,8,896]{2,1,0:T(8,128)(2,1)S(1)}, u32[]{:S(2)}, u32[]{:S(2)}) %all-to-all-start.1) | async-done | bytes 458784 | tf_op jit(solution)/shard_map/all_to_all | solution.py:286
  53.2 1.0 shard_map.115
  54.2 6.1 %all-to-all-start.2 = ((bf16[8,24,896]{2,1,0:T(8,128)(2,1)}), bf16[8,24,896]{2,1,0:T(8,128)(2,1)S(1)}, u32[]{:S(2)}, u32[]{:S(2)}) async-start(bf16[8,24,896]{2,1,0:T(8,128)(2,1)} %shard_map.115), calls=%async_computation.2 | async-start | bytes 688128 | tf_op jit(solution)/shard_map/all_to_all | solution.py:286
  60.3 0.0 copy-done.6
  60.3 0.6 broadcast_in_dim.16.embed_gain
  60.8 6.7 %all-to-all-done.2.got = bf16[8,24,896]{2,1,0:T(8,128)(2,1)S(1)} async-done(((bf16[8,24,896]{2,1,0:T(8,128)(2,1)}), bf16[8,24,896]{2,1,0:T(8,128)(2,1)S(1)}, u32[]{:S(2)}, u32[]{:S(2)}) %all-to-all-start.2) | async-done | bytes 344096 | tf_op jit(solution)/shard_map/all_to_all | solution.py:286
  67.5 0.0 copy-start.5
  67.5 0.0 all-gather.4.cloned.1.call-done
  67.5 0.8 copy-done.5
  68.3 3.9 %shard_map.116 = bf16[8,112,128]{2,1,0:T(8,128)(2,1)} custom-call(bf16[8,24,896]{2,1,0:T(8,128)(2,1)} %copy-done.5, bf16[384,896]{1,0:T(8,128)(2,1)} %hidden.3, f32[1,896]{1,0:T(1,128)} %broadcast_in_dim.16.embed_gain, bf16[8,112,896]{2,1,0:T(8,128)(2,1)} %bitcast.10), custom_call_target="tpu_custom_call" | custom-call | tf_op jit(solution)/shard_map/pallas_call | solution.py:68
  72.2 0.0 copy-start.1
  72.2 21.5 %all_to_all.36.parts = bf16[8,112,128]{2,1,0:T(8,128)(2,1)S(1)} all-to-all(bf16[8,112,128]{2,1,0:T(8,128)(2,1)} %shard_map.116), channel_id=1, replica_groups=mesh['dp'=8,'vocab'=64] {'dp'}, dimensions={0} | all-to-all | bytes 458752 | tf_op jit(solution)/shard_map/all_to_all | solution.py:347
  93.7 0.2 shard_map.117
  93.9 17.2 %all_to_all.37 = bf16[32,48,128]{2,1,0:T(8,128)(2,1)S(1)} all-to-all(bf16[32,48,128]{2,1,0:T(8,128)(2,1)S(1)} %shard_map.117), channel_id=1, replica_groups={{0,2,4,6,8,10,12,14,16,18,20,22,24,26,28,30,32,34,36,38,40,42,44,46,48,..., dimensions={0} | all-to-all | bytes 786432 | tf_op jit(solution)/shard_map/all_to_all | solution.py:286
  111.1 5.6 %all-gather.1 = bf16[64,48,128]{2,1,0:T(8,128)(2,1)S(1)} all-gather(bf16[32,48,128]{2,1,0:T(8,128)(2,1)S(1)} %all_to_all.37), channel_id=3, replica_groups={{0,1},{2,3},{4,5},{6,7},{8,9},{10,11},{12,13},{14,15},{16,17},{18,19},{..., dimensions={0}, use_global_device_ids=true | all-gather | bytes 1179648 | tf_op jit(solution)/shard_map/all_gather | solution.py:348
  116.8 0.0 copy-done.1
  116.8 2.0 %shard_map.118 = bf16[8,392,128]{2,1,0:T(8,128)(2,1)} custom-call(bf16[2,32,48,128]{3,2,1,0:T(8,128)(2,1)S(1)} %bitcast.8, bf16[896,1024]{1,0:T(8,128)(2,1)S(1)} %copy-done.1), custom_call_target="tpu_custom_call" | custom-call | tf_op jit(solution)/shard_map/pallas_call | solution.py:68
  118.8 3.5 %all-to-all-start.5 = ((bf16[8,392,128]{2,1,0:T(8,128)(2,1)}), bf16[8,392,128]{2,1,0:T(8,128)(2,1)S(1)}, u32[]{:S(2)}, u32[]{:S(2)}) async-start(bf16[8,392,128]{2,1,0:T(8,128)(2,1)} %shard_map.118), calls=%async_computation.5 | async-start | bytes 1605632 | tf_op jit(solution)/shard_map/all_to_all | solution.py:356
  122.3 0.0 reduce-scatter.2.cloned.1.call-done.sums
  122.4 0.0 copy-start.2
  122.4 0.9 copy-done.2
  123.3 0.3 shard_map.119
  123.6 22.7 %all-to-all-done.5.parts = bf16[8,392,128]{2,1,0:T(8,128)(2,1)S(1)} async-done(((bf16[8,392,128]{2,1,0:T(8,128)(2,1)}), bf16[8,392,128]{2,1,0:T(8,128)(2,1)S(1)}, u32[]{:S(2)}, u32[]{:S(2)}) %all-to-all-start.5) | async-done | bytes 802848 | tf_op jit(solution)/shard_map/all_to_all | solution.py:356
  146.2 0.3 shard_map.120
  146.6 17.9 %all_to_all.38.stats = f32[64,8,128]{2,1,0:T(8,128)S(1)} all-to-all(f32[64,8,128]{2,1,0:T(8,128)S(1)} %get-tuple-element.11), channel_id=1, replica_groups=mesh['dp'=8,'vocab'=64] {'vocab'}, dimensions={0} | all-to-all | bytes 524288 | tf_op jit(solution)/shard_map/all_to_all | solution.py:361
  164.5 0.9 shard_map.121
Async XLA Ops:
  8.0 59.5 %all-gather.4.cloned.1.call-start = ((), (), s32[]{:S(2)}) async-start(), calls=%async_computation.9 | async-start | bytes 1806336 | tf_op jit(solution)/shard_map/all_gather | solution.py:301
  17.6 12.2 %copy-start.3 = (bf16[64,896]{1,0:T(8,128)(2,1)S(1)}, bf16[64,896]{1,0:T(8,128)(2,1)}, u32[]{:S(2)}) copy-start(bf16[64,896]{1,0:T(8,128)(2,1)} %get-tuple-element.9.side) | copy-start | bytes 344068
  17.7 17.6 %copy-start.4 = (bf16[384,896]{1,0:T(8,128)(2,1)S(1)}, bf16[384,896]{1,0:T(8,128)(2,1)}, u32[]{:S(2)}) copy-start(bf16[384,896]{1,0:T(8,128)(2,1)} %hidden.3) | copy-start | bytes 2064388
  29.9 5.4 %copy-start = (bf16[896,1024]{1,0:T(8,128)(2,1)S(1)}, bf16[896,1024]{1,0:T(8,128)(2,1)}, u32[]{:S(2)}) copy-start(bf16[896,1024]{1,0:T(8,128)(2,1)} %head.1) | copy-start | bytes 5505028
  29.9 5.4 %copy-start.7 = (f32[896]{0:T(1024)S(1)}, f32[896]{0:T(1024)}, u32[]{:S(2)}) copy-start(f32[896]{0:T(1024)} %param.12) | copy-start | bytes 10756
  30.9 22.4 %all-to-all-start.1 = ((bf16[32,8,896]{2,1,0:T(8,128)(2,1)}), bf16[32,8,896]{2,1,0:T(8,128)(2,1)S(1)}, u32[]{:S(2)}, u32[]{:S(2)}) async-start(bf16[32,8,896]{2,1,0:T(8,128)(2,1)} %shard_map.114), calls=%async_computation.1 | async-start | bytes 917504 | tf_op jit(solution)/shard_map/all_to_all | solution.py:286
  35.2 87.2 %reduce-scatter.2.cloned.1.call-start = ((), (), s32[]{:S(2)}) async-start(), calls=%async_computation.8 | async-start | bytes 1769472 | tf_op jit(solution)/shard_map/reduce_scatter | solution.py:329
  37.4 22.9 %copy-start.6 = (f32[896]{0:T(1024)S(1)}, f32[896]{0:T(1024)}, u32[]{:S(2)}) copy-start(f32[896]{0:T(1024)} %param.14) | copy-start | bytes 10756
  54.2 13.3 %all-to-all-start.2 = ((bf16[8,24,896]{2,1,0:T(8,128)(2,1)}), bf16[8,24,896]{2,1,0:T(8,128)(2,1)S(1)}, u32[]{:S(2)}, u32[]{:S(2)}) async-start(bf16[8,24,896]{2,1,0:T(8,128)(2,1)} %shard_map.115), calls=%async_computation.2 | async-start | bytes 688128 | tf_op jit(solution)/shard_map/all_to_all | solution.py:286
  67.5 0.8 copy-start.5
  72.2 44.6 %copy-start.1 = (bf16[896,1024]{1,0:T(8,128)(2,1)S(1)}, bf16[896,1024]{1,0:T(8,128)(2,1)}, u32[]{:S(2)}) copy-start(bf16[896,1024]{1,0:T(8,128)(2,1)} %head.1) | copy-start | bytes 5505028
  118.8 27.5 %all-to-all-start.5 = ((bf16[8,392,128]{2,1,0:T(8,128)(2,1)}), bf16[8,392,128]{2,1,0:T(8,128)(2,1)S(1)}, u32[]{:S(2)}, u32[]{:S(2)}) async-start(bf16[8,392,128]{2,1,0:T(8,128)(2,1)} %shard_map.118), calls=%async_computation.5 | async-start | bytes 1605632 | tf_op jit(solution)/shard_map/all_to_all | solution.py:356
  122.4 0.9 copy-start.2
Sparse Core Ops, SparseCore 0:
  10.9 51.8 all-gather.3
Sparse Core Ops, SparseCore 1:
  38.5 43.8 reduce-scatter.1

commit v5 on v4

--- a/solution.py
+++ b/solution.py
@@ -20,6 +20,7 @@
 FT = FD // L
 ZROWS = 2 * RB + 16
 HROWS = RB * (VD // L) + 8
+PARAMS = pltpu.CompilerParams(vmem_limit_bytes=48 * 1024 * 1024)
 
 
 def vid(y, x, c):
@@ -29,7 +30,7 @@
 CORE = [[vid(y, x, c) for c in range(NC)] for y in range(NY) for x in range(NX)]
 YS = [[vid(y, x, c) for y in range(NY)] for x in range(NX) for c in range(NC)]
 XY = [[vid(y, x, c) for y in range(NY) for x in range(NX)] for c in range(NC)]
-XC = [[vid(y, x, c) for x in range(NX) for c in range(NC)] for y in range(NY)]
+XS = [[vid(y, x, c) for x in range(NX)] for y in range(NY) for c in range(NC)]
 
 
 def iota(shape, dim):
@@ -61,17 +62,17 @@
     return out
 
 
-def call(kernel, outs, *args, scratch=(), far=(), room=48 * 1024):
+def call(kernel, outs, *args, scratch=(), space=pltpu.VMEM):
     single = not isinstance(outs, (list, tuple))
     shapes = [outs] if single else list(outs)
-    specs = [pl.BlockSpec(memory_space=pltpu.VMEM) for _ in shapes]
+    specs = [pl.BlockSpec(memory_space=space) for _ in shapes]
     return pl.pallas_call(
         kernel,
         out_shape=shapes[0] if single else shapes,
-        in_specs=[pl.BlockSpec(memory_space=pltpu.HBM if k in far else pltpu.VMEM) for k in range(len(args))],
+        in_specs=[pl.BlockSpec(memory_space=pltpu.VMEM)] * len(args),
         out_specs=specs[0] if single else specs,
         scratch_shapes=list(scratch),
-        compiler_params=pltpu.CompilerParams(vmem_limit_bytes=room * 1024),
+        compiler_params=PARAMS,
     )(*args)
 
 
@@ -79,19 +80,10 @@
     return jax.ShapeDtypeStruct(shape, dtype)
 
 
-def front_kernel(tokens, gain, draft_gain, hidden, ph, table, out, side, hidden_v, ph_v, table_v, sems):
-    copies = [
-        pltpu.make_async_copy(src, dst, sems.at[k])
-        for k, (src, dst) in enumerate(((hidden, hidden_v), (ph, ph_v), (table, table_v)))
-    ]
-    for copy in copies:
-        copy.start()
-    pos = iota((ROWS, ROWS), 0)
-    source = (pos % NQ) * XR + pos // NQ
-    select = ones(iota((ROWS, ROWS), 1) == source)
+def pick_kernel(tokens, table, out, buf, sems):
     base = lax.axis_index("vocab") * VD
     rows = NC * NQ * 8
-    tok = tokens[...]
+    tok = tokens[...].reshape(1, ROWS)
     part = iota((8, ROWS), 0)
     high = jnp.broadcast_to(tok >> 8, (8, ROWS)).astype(F32)
     low = jnp.broadcast_to(tok & 255, (8, ROWS)).astype(F32)
@@ -102,30 +94,46 @@
     found = dot_nt(ones((iota((rows, ROWS), 1) == source) & (step < UR)), codes)
     local = (found[:, 0:1] * 256.0 + found[:, 1:2]).astype(jnp.int32) - base
     local = jnp.where((iota((rows, 1), 0) & 7) < UR, local, -1)
-    copies[0].wait()
-    x = dot(select, (hidden_v[...].astype(F32) * gain[...]).astype(BF)).astype(BF)
-    copies[1].wait()
-    weights = jnp.concatenate([ph_v[...], jnp.zeros((L - CW, FD), BF)], axis=0)
-    lines = dot_nt(x, weights)
+    copies = []
+    for start in range(0, rows, L):
+        hot = ones(iota((L, VD), 1) == local[start : start + L])
+        buf[start : start + L, :] = dot(hot, table[...]).astype(BF)
+        part = pl.ds(start, L)
+        copies.append(pltpu.make_async_copy(buf.at[part], out.at[part], sems.at[start // L]))
+        copies[-1].start()
+    for copy in copies:
+        copy.wait()
+
+
+def hidden_kernel(hidden, gain, ph, draft_gain, out):
+    pos = iota((ROWS, ROWS), 0)
+    source = (pos % NQ) * XR + pos // NQ
+    select = ones(iota((ROWS, ROWS), 1) == source)
+    x = dot(select, (hidden[...].astype(F32) * gain[...]).astype(BF)).astype(BF)
+    weights = jnp.concatenate([ph[...], jnp.zeros((L - CW, FD), BF)], axis=0)
+    side = dot_nt(x, weights)
     for i in range(XR):
         part = slice(i % FT * L, (i % FT + 1) * L)
-        side[i // FT * NQ : (i // FT + 1) * NQ, part] = lines[i * NQ : (i + 1) * NQ].astype(BF)
+        out[i // FT * NQ : (i // FT + 1) * NQ, part] = side[i * NQ : (i + 1) * NQ].astype(BF)
     for i, v in enumerate(split(draft_gain[...])):
         n = XR - FT + i
-        side[NQ:, n * L : (n + 1) * L] = jnp.broadcast_to(v.astype(BF), (NQ, L))
-    copies[2].wait()
-    for start in range(0, rows, L):
-        hot = ones(iota((L, VD), 1) == local[start : start + L])
-        out[start : start + L, :] = dot(hot, table_v[...]).astype(BF)
-
-
-def send_kernel(half, side, out):
+        out[NQ:, n * L : (n + 1) * L] = jnp.broadcast_to(v.astype(BF), (NQ, L))
+
+
+def send_kernel(half, side, out, buf, sems):
     row = iota((8, FD), 0)
     lines = side[...].astype(F32)
+    copies = []
     for k in range(NQ):
         rows = half[0, k].astype(F32) + half[1, k].astype(F32)
         rows = jnp.where(row == UR, lines[k : k + 1], rows)
-        out[k] = jnp.where(row == UR + 1, lines[NQ + k : NQ + k + 1], rows).astype(BF)
+        buf[k] = jnp.where(row == UR + 1, lines[NQ + k : NQ + k + 1], rows).astype(BF)
+        if k % 8 == 7:
+            part = pl.ds(k - 7, 8)
+            copies.append(pltpu.make_async_copy(buf.at[part], out.at[part], sems.at[k // 8]))
+            copies[-1].start()
+    for copy in copies:
+        copy.wait()
 
 
 def unit_kernel(got, out):
@@ -140,22 +148,13 @@
             first[x] = jnp.where(row == y, block[UR : UR + 1], first[x])
             second[x] = jnp.where(row == y, block[UR + 1 : UR + 2], second[x])
     for x in range(NX):
-        block = jnp.concatenate([total, first[x], second[x]], axis=0).astype(BF)
-        for c in range(NC):
-            out[x * NC + c] = block
-
-
-def proj_kernel(got, hidden, embed_gain, weights, out, side, hidden_v, weights_v, sems):
+        out[x] = jnp.concatenate([total, first[x], second[x]], axis=0).astype(BF)
+
+
+def proj_kernel(got, hidden, embed_gain, weights, out, side):
     y = lax.axis_index("vocab") // (NX * NC)
-    mine = hidden.at[pl.ds(pl.multiple_of(y * RB, 16), RB), :]
-    copies = [
-        pltpu.make_async_copy(mine, hidden_v, sems.at[0]),
-        pltpu.make_async_copy(weights, weights_v, sems.at[1]),
-    ]
-    for copy in copies:
-        copy.start()
     core = lax.axis_index("vocab") % NC
-    units = [got[k].astype(F32) for k in range(NX * NC)]
+    units = [got[c, x].astype(F32) for x in range(NX) for c in range(NC)]
     picked = jnp.concatenate([u[0:8] for u in units], axis=0).astype(BF)
     for x in range(NX):
         lines = jnp.where(core == 0, units[x * NC], units[x * NC + 1])[8:24]
@@ -165,8 +164,7 @@
             side[at : at + 8, :] = lines[r : r + 8, t : t + L]
     n = (XR - FT) * L
     gain_hi, gain_low = lines[8:16, n : n + L], lines[8:16, n + L : n + 2 * L]
-    copies[0].wait()
-    h = hidden_v[...].astype(F32)
+    h = hidden[pl.ds(pl.multiple_of(y * RB, 16), RB), :].astype(F32)
     row, col = iota((RB, 64), 0), iota((RB, 64), 1)
     e = dot(ones(col == (row // UR) * 8 + row % UR), picked)
     lane = iota((RB, L), 1)
@@ -178,9 +176,8 @@
     extra_h, extra_e = extra(h), extra(e)
     eg = (e * embed_gain[...]).astype(BF)
     pad = jnp.zeros((L - CW, FD), BF)
-    copies[1].wait()
     for t in range(NY):
-        w = jnp.concatenate([weights_v[t], pad], axis=0)
+        w = jnp.concatenate([weights[t], pad], axis=0)
         out[t, 0:RB, :] = (jnp.where(lane < CW, side[pl.ds(t, RB, stride=8), :], 0.0) + extra_h).astype(BF)
         out[t, RB : 2 * RB, :] = (dot_nt(eg, w) + extra_e).astype(BF)
         out[t, 2 * RB :, :] = place([gain_hi[t : t + 1], gain_low[t : t + 1]], (16, L)).astype(BF)
@@ -300,29 +297,27 @@
 ):
     weights = lax.all_gather(proj_embed.T, "vocab", axis_index_groups=YS)
 
+    picked = call(
+        pick_kernel,
+        struct((NC * NQ * 8, FD), BF),
+        tokens,
+        embed_table,
+        scratch=[pltpu.VMEM((NC * NQ * 8, FD), BF), pltpu.SemaphoreType.DMA((NC * NQ * 8 // L,))],
+        space=pltpu.HBM,
+    )
+    half = exchange(picked.reshape(NC, NQ, 8, FD), CORE)
     gain = jnp.pad(draft_gain, (0, L - CW))[None]
-    picked, side = call(
-        front_kernel,
-        (struct((NC * NQ * 8, FD), BF), struct((2 * NQ, FD), BF)),
-        tokens[None],
-        hidden_gain[None],
-        gain,
-        hidden,
-        proj_hidden.T,
-        embed_table,
-        far=(3, 4, 5),
-        room=63 * 1024,
-        scratch=[
-            pltpu.VMEM((ROWS, FD), BF),
-            pltpu.VMEM((CW, FD), BF),
-            pltpu.VMEM((VD, FD), BF),
-            pltpu.SemaphoreType.DMA((3,)),
-        ],
-    )
-    half = exchange(picked.reshape(NC, NQ, 8, FD), CORE)
-    sent = call(send_kernel, struct((NQ, 8, FD), BF), half, side)
-    unit = call(unit_kernel, struct((NX * NC, 24, FD), BF), exchange(sent, XY))
-    got = exchange(unit, XC)
+    side = call(hidden_kernel, struct((2 * NQ, FD), BF), hidden, hidden_gain[None], proj_hidden.T, gain)
+    sent = call(
+        send_kernel,
+        struct((NQ, 8, FD), BF),
+        half,
+        side,
+        scratch=[pltpu.VMEM((NQ, 8, FD), BF), pltpu.SemaphoreType.DMA((NQ // 8,))],
+        space=pltpu.HBM,
+    )
+    unit = call(unit_kernel, struct((NX, 24, FD), BF), exchange(sent, XY))
+    got = lax.all_gather(exchange(unit, XS), "vocab", axis_index_groups=CORE)
 
     main_in = (hidden.astype(F32) * final_gain).astype(BF)
     main_part = jnp.dot(main_in, head_weight, preferred_element_type=F32)
@@ -335,14 +330,7 @@
         hidden,
         embed_gain[None],
         weights,
-        far=(1, 3),
-        room=64000,
-        scratch=[
-            pltpu.VMEM((RB * 8, L), F32),
-            pltpu.VMEM((RB, FD), BF),
-            pltpu.VMEM((NY, CW, FD), BF),
-            pltpu.SemaphoreType.DMA((2,)),
-        ],
+        scratch=[pltpu.VMEM((RB * 8, L), F32)],
     )
     joined = call(join_kernel, struct((NQ, RB, L), BF), lax.all_to_all(partial, "dp", 0, 0))
     rows = lax.all_gather(exchange(joined, XY), "vocab", axis_index_groups=CORE)

time: 174 us -> 168 us (0.966)
  blocking collectives: 74.5 us -> 65.6 us
  starting transfers between devices: 14 us -> 22.6 us
  Pallas kernels: 14.9 us -> 9.61 us
    all_to_all x2 -> x1, blocking collectives: 29.4 us -> 18 us  [exchange(): return lax.all_to_all(x, 'vocab', 0, 0, axis_index_groups=groups)]
    all_to_all x2 -> x3, starting transfers between devices: 10.4 us -> 19 us  [exchange(): return lax.all_to_all(x, 'vocab', 0, 0, axis_index_groups=groups)]
    pallas_call x9 -> x10, Pallas kernels: 14.9 us -> 9.61 us  [call(): pl.pallas_call(kernel, out_shape=shapes[0] if single else shapes, in_spec...]
    all_gather x0 -> x1, blocking collectives: none -> 4.81 us  [per_device(): got = lax.all_gather(exchange(unit, XS), 'vocab', axis_index_groups=CORE)]
    unnamed x16 -> x20, local copies, waits for them, and re-layouts: 1.7 us -> 5.48 us
    all_to_all x1, blocking collectives: 21.5 us -> 19.5 us  [per_device(): lax.all_to_all(partial, 'dp', 0, 0)]
    all_to_all x2 -> x3, waiting for transfers between devices: 22.5 us -> 22.1 us  [exchange(): return lax.all_to_all(x, 'vocab', 0, 0, axis_index_groups=groups)]
  transfers between devices with their start and end apart: 5 -> 6, of which waited for: 3 -> 3; matrix products, arithmetic and copies ran while one was open for 4% -> 2% of each run, Pallas kernels for 8% -> 5%
where the time goes in v5:
time: 168 us; the launch traced here: 167 us
  blocking collectives  65.6 us (39%)
  waiting for transfers between devices  45.5 us (27%)
  starting transfers between devices  22.6 us (13%)
  between operations  15.6 us (9%)
  Pallas kernels  9.61 us (6%)
  local copies, waits for them, and re-layouts  5.49 us (3%)
  matrix products  2.81 us (2%)
    all_to_all x1, waiting for transfers between devices, per_device(): parts = lax.all_to_all(blocks, 'dp', 0, 0)  22.7 us
    all_to_all x3, waiting for transfers between devices, exchange(): return lax.all_to_all(x, 'vocab', 0, 0, axis_index_groups=groups)  22.1 us
    all_to_all x1, blocking collectives, per_device(): lax.all_to_all(partial, 'dp', 0, 0)  19.5 us
    all_to_all x3, starting transfers between devices, exchange(): return lax.all_to_all(x, 'vocab', 0, 0, axis_index_groups=groups)  19 us
    all_to_all x1, blocking collectives, exchange(): return lax.all_to_all(x, 'vocab', 0, 0, axis_index_groups=groups)  18 us
    all_to_all x1, blocking collectives, per_device(): stats = lax.all_to_all(stats, 'vocab', 0, 0)  17.9 us
    pallas_call x10, Pallas kernels, call(): pl.pallas_call(kernel, out_shape=shapes[0] if single else shapes, in_spec...  9.61 us
    unnamed x20, local copies, waits for them, and re-layouts  5.48 us
  transfers between devices with their start and end apart: 6, of which 3 were waited for; matrix products, arithmetic and copies ran while one was open for 2% of the time, Pallas kernels for 5%

profile of v5, /device:TPU:1, one launch (start us, length us, event | category | flops | bytes accessed | tf_op | source)
XLA Modules:
  0.0 167.2 jit_solution(4486141751509580250)
XLA Ops:
  8.0 0.0 all-gather.5.cloned.1.call-start
  8.0 0.7 all-gather.5.cloned.1.call-update
  8.7 0.0 copy-start.1
  8.7 1.5 copy-done.1
  10.2 0.0 copy-start.6
  10.2 0.7 copy-done.6
  10.9 2.4 %shard_map.113 = bf16[512,896]{1,0:T(8,128)(2,1)} custom-call(s32[384]{0:T(512)S(1)} %copy-done.6, bf16[1024,896]{1,0:T(8,128)(2,1)S(1)} %copy-done.1), custom_call_target="tpu_custom_call" | custom-call | tf_op jit(solution)/shard_map/pallas_call | solution.py:69
  13.3 0.0 copy-start.7
  13.3 0.0 copy-start.9
  13.3 0.0 copy-start
  13.3 10.6 %all-to-all-start = ((bf16[2,32,8,896]{3,2,1,0:T(8,128)(2,1)}), bf16[2,32,8,896]{3,2,1,0:T(8,128)(2,1)S(1)}, u32[]{:S(2)}, u32[]{:S(2)}) async-start(bf16[2,32,8,896]{3,2,1,0:T(8,128)(2,1)} %bitcast), calls=%async_computation | async-start | bytes 1835008 | tf_op jit(solution)/shard_map/all_to_all | solution.py:283
  23.9 0.0 copy-done.7
  23.9 0.0 copy-done.9
  23.9 0.0 copy-done
  23.9 0.0 copy-start.4
  24.0 0.9 copy-done.4
  24.9 0.0 copy-start.2
  24.9 0.8 shard_map.114.side
  25.7 0.0 all-to-all-done.half
  25.7 0.9 shard_map.115
  26.6 4.3 %all-to-all-start.1 = ((bf16[32,8,896]{2,1,0:T(8,128)(2,1)}), bf16[32,8,896]{2,1,0:T(8,128)(2,1)S(1)}, u32[]{:S(2)}, u32[]{:S(2)}) async-start(bf16[32,8,896]{2,1,0:T(8,128)(2,1)} %shard_map.115), calls=%async_computation.1 | async-start | bytes 917504 | tf_op jit(solution)/shard_map/all_to_all | solution.py:283
  30.9 0.0 reduce-scatter.2.cloned.1.call-start
  31.0 0.0 copy-done.2
  31.0 2.8 %fusion = f32[384,1024]{1,0:T(8,128)} fusion(bf16[896,1024]{1,0:T(8,128)(2,1)S(1)} %copy-done.2, bf16[384,896]{1,0:T(8,128)(2,1)S(1)} %copy-done, f32[896]{0:T(1024)} %param.12), kind=kOutput, calls=%fused_computation.1 | convolution fusion | flops 705675264 | bytes 4099584 | tf_op jit(solution)/shard_map/dot_general | solution.py:323
  33.8 0.0 copy-start.8
  33.8 0.0 reduce-scatter.2.cloned.1.call-update
  33.8 17.0 %all-to-all-done.1.got = bf16[32,8,896]{2,1,0:T(8,128)(2,1)S(1)} async-done(((bf16[32,8,896]{2,1,0:T(8,128)(2,1)}), bf16[32,8,896]{2,1,0:T(8,128)(2,1)S(1)}, u32[]{:S(2)}, u32[]{:S(2)}) %all-to-all-start.1) | async-done | bytes 458784 | tf_op jit(solution)/shard_map/all_to_all | solution.py:283
  50.9 0.9 shard_map.116
  51.8 4.1 %all-to-all-start.2 = ((bf16[4,24,896]{2,1,0:T(8,128)(2,1)}), bf16[4,24,896]{2,1,0:T(8,128)(2,1)S(1)}, u32[]{:S(2)}, u32[]{:S(2)}) async-start(bf16[4,24,896]{2,1,0:T(8,128)(2,1)} %shard_map.116), calls=%async_computation.2 | async-start | bytes 344064 | tf_op jit(solution)/shard_map/all_to_all | solution.py:283
  55.9 0.0 copy-done.8
  55.9 5.0 %all-to-all-done.2 = bf16[4,24,896]{2,1,0:T(8,128)(2,1)S(1)} async-done(((bf16[4,24,896]{2,1,0:T(8,128)(2,1)}), bf16[4,24,896]{2,1,0:T(8,128)(2,1)S(1)}, u32[]{:S(2)}, u32[]{:S(2)}) %all-to-all-start.2) | async-done | bytes 172064 | tf_op jit(solution)/shard_map/all_to_all | solution.py:283
  60.9 4.8 %all-gather = bf16[8,24,896]{2,1,0:T(8,128)(2,1)S(1)} all-gather(bf16[4,24,896]{2,1,0:T(8,128)(2,1)S(1)} %all-to-all-done.2), channel_id=2, replica_groups={{0,1},{2,3},{4,5},{6,7},{8,9},{10,11},{12,13},{14,15},{16,17},{18,19},{..., dimensions={0}, use_global_device_ids=true | all-gather | bytes 516096 | tf_op jit(solution)/shard_map/all_gather | solution.py:320
  65.7 1.4 copy-done.3
  67.2 0.9 shard_map.117
  68.0 19.5 %all_to_all.35.parts = bf16[8,112,128]{2,1,0:T(8,128)(2,1)S(1)} all-to-all(bf16[8,112,128]{2,1,0:T(8,128)(2,1)S(1)} %shard_map.117), channel_id=1, replica_groups=mesh['dp'=8,'vocab'=64] {'dp'}, dimensions={0} | all-to-all | bytes 458752 | tf_op jit(solution)/shard_map/all_to_all | solution.py:335
  87.5 0.2 shard_map.118
  87.7 18.0 %all_to_all.36 = bf16[32,48,128]{2,1,0:T(8,128)(2,1)S(1)} all-to-all(bf16[32,48,128]{2,1,0:T(8,128)(2,1)S(1)} %shard_map.118), channel_id=1, replica_groups={{0,2,4,6,8,10,12,14,16,18,20,22,24,26,28,30,32,34,36,38,40,42,44,46,48,..., dimensions={0} | all-to-all | bytes 786432 | tf_op jit(solution)/shard_map/all_to_all | solution.py:283
  105.8 5.3 %all-gather.2 = bf16[64,48,128]{2,1,0:T(8,128)(2,1)S(1)} all-gather(bf16[32,48,128]{2,1,0:T(8,128)(2,1)S(1)} %all_to_all.36), channel_id=4, replica_groups={{0,1},{2,3},{4,5},{6,7},{8,9},{10,11},{12,13},{14,15},{16,17},{18,19},{..., dimensions={0}, use_global_device_ids=true | all-gather | bytes 1179648 | tf_op jit(solution)/shard_map/all_gather | solution.py:336
  111.1 2.0 %shard_map.119 = bf16[8,392,128]{2,1,0:T(8,128)(2,1)} custom-call(bf16[2,32,48,128]{3,2,1,0:T(8,128)(2,1)S(1)} %bitcast.9, bf16[896,1024]{1,0:T(8,128)(2,1)S(1)} %copy-done.2), custom_call_target="tpu_custom_call" | custom-call | tf_op jit(solution)/shard_map/pallas_call | solution.py:69
  113.1 3.5 %all-to-all-start.5 = ((bf16[8,392,128]{2,1,0:T(8,128)(2,1)}), bf16[8,392,128]{2,1,0:T(8,128)(2,1)S(1)}, u32[]{:S(2)}, u32[]{:S(2)}) async-start(bf16[8,392,128]{2,1,0:T(8,128)(2,1)} %shard_map.119), calls=%async_computation.5 | async-start | bytes 1605632 | tf_op jit(solution)/shard_map/all_to_all | solution.py:344
  116.7 0.0 reduce-scatter.2.cloned.1.call-done.sums
  116.7 0.0 copy-start.5
  116.7 0.9 copy-done.5
  117.6 0.3 shard_map.120
  117.9 22.7 %all-to-all-done.5.parts = bf16[8,392,128]{2,1,0:T(8,128)(2,1)S(1)} async-done(((bf16[8,392,128]{2,1,0:T(8,128)(2,1)}), bf16[8,392,128]{2,1,0:T(8,128)(2,1)S(1)}, u32[]{:S(2)}, u32[]{:S(2)}) %all-to-all-start.5) | async-done | bytes 802848 | tf_op jit(solution)/shard_map/all_to_all | solution.py:344
  140.6 0.3 shard_map.121
  140.9 17.9 %all_to_all.37.stats = f32[64,8,128]{2,1,0:T(8,128)S(1)} all-to-all(f32[64,8,128]{2,1,0:T(8,128)S(1)} %get-tuple-element.7), channel_id=1, replica_groups=mesh['dp'=8,'vocab'=64] {'vocab'}, dimensions={0} | all-to-all | bytes 524288 | tf_op jit(solution)/shard_map/all_to_all | solution.py:349
  158.8 0.9 shard_map.122
  (5 shorter events, 0.0 us)
Async XLA Ops:
  8.0 57.7 %all-gather.5.cloned.1.call-start = ((), (), s32[]{:S(2)}) async-start(), calls=%async_computation.9 | async-start | bytes 1806336 | tf_op jit(solution)/shard_map/all_gather | solution.py:298
  8.7 1.5 copy-start.1
  10.2 0.7 copy-start.6
  13.3 10.6 %copy-start.7 = (f32[896]{0:T(1024)S(1)}, f32[896]{0:T(1024)}, u32[]{:S(2)}) copy-start(f32[896]{0:T(1024)} %param.13) | copy-start | bytes 10756
  13.3 10.6 %copy-start.9 = (f32[112]{0:T(128)S(1)}, f32[112]{0:T(128)}, u32[]{:S(2)}) copy-start(f32[112]{0:T(128)} %param.18) | copy-start | bytes 1348
  13.3 10.6 %copy-start = (bf16[384,896]{1,0:T(8,128)(2,1)S(1)}, bf16[384,896]{1,0:T(8,128)(2,1)}, u32[]{:S(2)}) copy-start(bf16[384,896]{1,0:T(8,128)(2,1)} %hidden.3) | copy-start | bytes 2064388
  13.3 12.4 %all-to-all-start = ((bf16[2,32,8,896]{3,2,1,0:T(8,128)(2,1)}), bf16[2,32,8,896]{3,2,1,0:T(8,128)(2,1)S(1)}, u32[]{:S(2)}, u32[]{:S(2)}) async-start(bf16[2,32,8,896]{3,2,1,0:T(8,128)(2,1)} %bitcast), calls=%async_computation | async-start | bytes 1835008 | tf_op jit(solution)/shard_map/all_to_all | solution.py:283
  23.9 0.9 copy-start.4
  24.9 6.1 %copy-start.2 = (bf16[896,1024]{1,0:T(8,128)(2,1)S(1)}, bf16[896,1024]{1,0:T(8,128)(2,1)}, u32[]{:S(2)}) copy-start(bf16[896,1024]{1,0:T(8,128)(2,1)} %head.1) | copy-start | bytes 5505028
  26.6 24.3 %all-to-all-start.1 = ((bf16[32,8,896]{2,1,0:T(8,128)(2,1)}), bf16[32,8,896]{2,1,0:T(8,128)(2,1)S(1)}, u32[]{:S(2)}, u32[]{:S(2)}) async-start(bf16[32,8,896]{2,1,0:T(8,128)(2,1)} %shard_map.115), calls=%async_computation.1 | async-start | bytes 917504 | tf_op jit(solution)/shard_map/all_to_all | solution.py:283
  30.9 85.8 %reduce-scatter.2.cloned.1.call-start = ((), (), s32[]{:S(2)}) async-start(), calls=%async_computation.8 | async-start | bytes 1769472 | tf_op jit(solution)/shard_map/reduce_scatter | solution.py:324
  33.8 22.1 %copy-start.8 = (f32[896]{0:T(1024)S(1)}, f32[896]{0:T(1024)}, u32[]{:S(2)}) copy-start(f32[896]{0:T(1024)} %param.14) | copy-start | bytes 10756
  51.8 9.2 %all-to-all-start.2 = ((bf16[4,24,896]{2,1,0:T(8,128)(2,1)}), bf16[4,24,896]{2,1,0:T(8,128)(2,1)S(1)}, u32[]{:S(2)}, u32[]{:S(2)}) async-start(bf16[4,24,896]{2,1,0:T(8,128)(2,1)} %shard_map.116), calls=%async_computation.2 | async-start | bytes 344064 | tf_op jit(solution)/shard_map/all_to_all | solution.py:283
  65.7 1.4 copy-start.3
  113.1 27.5 %all-to-all-start.5 = ((bf16[8,392,128]{2,1,0:T(8,128)(2,1)}), bf16[8,392,128]{2,1,0:T(8,128)(2,1)S(1)}, u32[]{:S(2)}, u32[]{:S(2)}) async-start(bf16[8,392,128]{2,1,0:T(8,128)(2,1)} %shard_map.119), calls=%async_computation.5 | async-start | bytes 1605632 | tf_op jit(solution)/shard_map/all_to_all | solution.py:344
  116.7 0.9 copy-start.5
Sparse Core Ops, SparseCore 0:
  10.9 51.5 all-gather.4
Sparse Core Ops, SparseCore 1:
  34.3 44.0 reduce-scatter.1

commit v6 on v5

--- a/solution.py
+++ b/solution.py
@@ -14,10 +14,8 @@
 VD = V // (NQ * NC)
 CW = D // (NQ * NC)
 RB = ROWS // NZ
-UR = RB // (NX * NC)
-XR = NC * UR
+HB = RB // NC
 L = 128
-FT = FD // L
 ZROWS = 2 * RB + 16
 HROWS = RB * (VD // L) + 8
 PARAMS = pltpu.CompilerParams(vmem_limit_bytes=48 * 1024 * 1024)
@@ -82,20 +80,18 @@
 
 def pick_kernel(tokens, table, out, buf, sems):
     base = lax.axis_index("vocab") * VD
-    rows = NC * NQ * 8
     tok = tokens[...].reshape(1, ROWS)
     part = iota((8, ROWS), 0)
     high = jnp.broadcast_to(tok >> 8, (8, ROWS)).astype(F32)
     low = jnp.broadcast_to(tok & 255, (8, ROWS)).astype(F32)
     codes = jnp.where(part == 0, high, jnp.where(part == 1, low, 0.0)).astype(BF)
-    pos = iota((rows, ROWS), 0)
-    step, unit, core = pos & 7, (pos >> 3) & (NQ - 1), pos >> 8
-    source = (unit * NC + core) * UR + step
-    found = dot_nt(ones((iota((rows, ROWS), 1) == source) & (step < UR)), codes)
+    row = iota((ROWS, ROWS), 1)
+    y, rest = row // RB, row % RB
+    place_of = (rest // HB) * (NY * HB) + y * HB + rest % HB
+    found = dot_nt(ones(iota((ROWS, ROWS), 0) == place_of), codes)
     local = (found[:, 0:1] * 256.0 + found[:, 1:2]).astype(jnp.int32) - base
-    local = jnp.where((iota((rows, 1), 0) & 7) < UR, local, -1)
     copies = []
-    for start in range(0, rows, L):
+    for start in range(0, ROWS, L):
         hot = ones(iota((L, VD), 1) == local[start : start + L])
         buf[start : start + L, :] = dot(hot, table[...]).astype(BF)
         part = pl.ds(start, L)
@@ -106,67 +102,45 @@
 
 
 def hidden_kernel(hidden, gain, ph, draft_gain, out):
-    pos = iota((ROWS, ROWS), 0)
-    source = (pos % NQ) * XR + pos // NQ
-    select = ones(iota((ROWS, ROWS), 1) == source)
-    x = dot(select, (hidden[...].astype(F32) * gain[...]).astype(BF)).astype(BF)
+    x = (hidden[...].astype(F32) * gain[...]).astype(BF)
     weights = jnp.concatenate([ph[...], jnp.zeros((L - CW, FD), BF)], axis=0)
     side = dot_nt(x, weights)
-    for i in range(XR):
-        part = slice(i % FT * L, (i % FT + 1) * L)
-        out[i // FT * NQ : (i // FT + 1) * NQ, part] = side[i * NQ : (i + 1) * NQ].astype(BF)
-    for i, v in enumerate(split(draft_gain[...])):
-        n = XR - FT + i
-        out[NQ:, n * L : (n + 1) * L] = jnp.broadcast_to(v.astype(BF), (NQ, L))
+    last = place(split(draft_gain[...]), (8, L))
+    for y in range(NY):
+        tiles = [side[y * RB + i : y * RB + i + 8] for i in range(0, RB, 8)]
+        out[y] = jnp.concatenate([*tiles, last], axis=1)
 
 
 def send_kernel(half, side, out, buf, sems):
-    row = iota((8, FD), 0)
-    lines = side[...].astype(F32)
     copies = []
-    for k in range(NQ):
+    for k in range(NY):
         rows = half[0, k].astype(F32) + half[1, k].astype(F32)
-        rows = jnp.where(row == UR, lines[k : k + 1], rows)
-        buf[k] = jnp.where(row == UR + 1, lines[NQ + k : NQ + k + 1], rows).astype(BF)
-        if k % 8 == 7:
-            part = pl.ds(k - 7, 8)
-            copies.append(pltpu.make_async_copy(buf.at[part], out.at[part], sems.at[k // 8]))
+        buf[k] = jnp.concatenate([rows, side[k]], axis=0).astype(BF)
+        if k % 2 == 1:
+            part = pl.ds(k - 1, 2)
+            copies.append(pltpu.make_async_copy(buf.at[part], out.at[part], sems.at[k // 2]))
             copies[-1].start()
     for copy in copies:
         copy.wait()
 
 
 def unit_kernel(got, out):
-    row = iota((8, FD), 0)
-    total = jnp.zeros((8, FD), F32)
-    first = [jnp.zeros((8, FD), F32) for _ in range(NX)]
-    second = [jnp.zeros((8, FD), F32) for _ in range(NX)]
+    total = jnp.zeros((HB, FD), F32)
     for y in range(NY):
-        for x in range(NX):
-            block = got[y * NX + x].astype(F32)
-            total = total + block
-            first[x] = jnp.where(row == y, block[UR : UR + 1], first[x])
-            second[x] = jnp.where(row == y, block[UR + 1 : UR + 2], second[x])
-    for x in range(NX):
-        out[x] = jnp.concatenate([total, first[x], second[x]], axis=0).astype(BF)
-
-
-def proj_kernel(got, hidden, embed_gain, weights, out, side):
+        total = total + got[y].astype(F32)[0:HB]
+    out[...] = jnp.broadcast_to(total.astype(BF)[None], out.shape)
+
+
+def proj_kernel(picked, lines, hidden, embed_gain, weights, out):
     y = lax.axis_index("vocab") // (NX * NC)
-    core = lax.axis_index("vocab") % NC
-    units = [got[c, x].astype(F32) for x in range(NX) for c in range(NC)]
-    picked = jnp.concatenate([u[0:8] for u in units], axis=0).astype(BF)
-    for x in range(NX):
-        lines = jnp.where(core == 0, units[x * NC], units[x * NC + 1])[8:24]
-        for i in range(XR):
-            r, t = i // FT * 8, i % FT * L
-            at = (x * XR + i) * 8
-            side[at : at + 8, :] = lines[r : r + 8, t : t + L]
-    n = (XR - FT) * L
-    gain_hi, gain_low = lines[8:16, n : n + L], lines[8:16, n + L : n + 2 * L]
     h = hidden[pl.ds(pl.multiple_of(y * RB, 16), RB), :].astype(F32)
-    row, col = iota((RB, 64), 0), iota((RB, 64), 1)
-    e = dot(ones(col == (row // UR) * 8 + row % UR), picked)
+    halves = []
+    for c in range(NC):
+        half = picked[c, 0].astype(F32)
+        for x in range(1, NX):
+            half = half + picked[c, x].astype(F32)
+        halves.append(half)
+    e = jnp.concatenate(halves, axis=0)
     lane = iota((RB, L), 1)
 
     def extra(x):
@@ -178,9 +152,12 @@
     pad = jnp.zeros((L - CW, FD), BF)
     for t in range(NY):
         w = jnp.concatenate([weights[t], pad], axis=0)
-        out[t, 0:RB, :] = (jnp.where(lane < CW, side[pl.ds(t, RB, stride=8), :], 0.0) + extra_h).astype(BF)
+        block = lines[t].astype(F32)[HB : HB + 8]
+        side = jnp.concatenate([block[:, i * L : (i + 1) * L] for i in range(RB // 8)], axis=0)
+        gain = block[:, RB // 8 * L :]
+        out[t, 0:RB, :] = (side + extra_h).astype(BF)
         out[t, RB : 2 * RB, :] = (dot_nt(eg, w) + extra_e).astype(BF)
-        out[t, 2 * RB :, :] = place([gain_hi[t : t + 1], gain_low[t : t + 1]], (16, L)).astype(BF)
+        out[t, 2 * RB :, :] = place([gain[0:1], gain[1:2]], (16, L)).astype(BF)
 
 
 def join_kernel(parts, out):
@@ -299,24 +276,25 @@
 
     picked = call(
         pick_kernel,
-        struct((NC * NQ * 8, FD), BF),
+        struct((ROWS, FD), BF),
         tokens,
         embed_table,
-        scratch=[pltpu.VMEM((NC * NQ * 8, FD), BF), pltpu.SemaphoreType.DMA((NC * NQ * 8 // L,))],
+        scratch=[pltpu.VMEM((ROWS, FD), BF), pltpu.SemaphoreType.DMA((ROWS // L,))],
         space=pltpu.HBM,
     )
-    half = exchange(picked.reshape(NC, NQ, 8, FD), CORE)
+    half = exchange(picked.reshape(NC, NY, HB, FD), CORE)
     gain = jnp.pad(draft_gain, (0, L - CW))[None]
-    side = call(hidden_kernel, struct((2 * NQ, FD), BF), hidden, hidden_gain[None], proj_hidden.T, gain)
+    side = call(hidden_kernel, struct((NY, 8, FD), F32), hidden, hidden_gain[None], proj_hidden.T, gain)
     sent = call(
         send_kernel,
-        struct((NQ, 8, FD), BF),
+        struct((NY, HB + 8, FD), BF),
         half,
         side,
-        scratch=[pltpu.VMEM((NQ, 8, FD), BF), pltpu.SemaphoreType.DMA((NQ // 8,))],
+        scratch=[pltpu.VMEM((NY, HB + 8, FD), BF), pltpu.SemaphoreType.DMA((NY // 2,))],
         space=pltpu.HBM,
     )
-    unit = call(unit_kernel, struct((NX, 24, FD), BF), exchange(sent, XY))
+    lines = exchange(sent, YS)
+    unit = call(unit_kernel, struct((NX, HB, FD), BF), lines)
     got = lax.all_gather(exchange(unit, XS), "vocab", axis_index_groups=CORE)
 
     main_in = (hidden.astype(F32) * final_gain).astype(BF)
@@ -327,10 +305,10 @@
         proj_kernel,
         struct((NY, ZROWS, L), BF),
         got,
+        lines,
         hidden,
         embed_gain[None],
         weights,
-        scratch=[pltpu.VMEM((RB * 8, L), F32)],
     )
     joined = call(join_kernel, struct((NQ, RB, L), BF), lax.all_to_all(partial, "dp", 0, 0))
     rows = lax.all_gather(exchange(joined, XY), "vocab", axis_index_groups=CORE)

time: 168 us -> 165 us (0.982)
  blocking collectives: 65.6 us -> 63.2 us
  waiting for transfers between devices: 45.5 us -> 47.7 us
  starting transfers between devices: 22.6 us -> 20.8 us
    all_to_all x1, blocking collectives: 18 us -> 14.7 us  [exchange(): return lax.all_to_all(x, 'vocab', 0, 0, axis_index_groups=groups)]
    all_gather x1, blocking collectives: 5.32 us -> 7.84 us  [per_device(): rows = lax.all_gather(exchange(joined, XY), 'vocab', axis_index_groups=CORE)]
    all_to_all x3, waiting for transfers between devices: 22.1 us -> 24.3 us  [exchange(): return lax.all_to_all(x, 'vocab', 0, 0, axis_index_groups=groups)]
    all_to_all x3, starting transfers between devices: 19 us -> 17.2 us  [exchange(): return lax.all_to_all(x, 'vocab', 0, 0, axis_index_groups=groups)]
    unnamed x20 -> x24, local copies, waits for them, and re-layouts: 5.48 us -> 6.22 us
  transfers between devices with their start and end apart: 6 -> 6, of which waited for: 3 -> 4; matrix products, arithmetic and copies ran while one was open for 2% -> 1% of each run, Pallas kernels for 5% -> 4%
where the time goes in v6:
time: 165 us; the launch traced here: 164 us
  blocking collectives  63.2 us (38%)
  waiting for transfers between devices  47.7 us (29%)
  starting transfers between devices  20.8 us (13%)
  between operations  15.6 us (9%)
  Pallas kernels  8.39 us (5%)
  local copies, waits for them, and re-layouts  6.23 us (4%)
  matrix products  2.13 us (1%)
    all_to_all x3, waiting for transfers between devices, exchange(): return lax.all_to_all(x, 'vocab', 0, 0, axis_index_groups=groups)  24.3 us
    all_to_all x1, waiting for transfers between devices, per_device(): parts = lax.all_to_all(blocks, 'dp', 0, 0)  22.7 us
    all_to_all x1, blocking collectives, per_device(): lax.all_to_all(partial, 'dp', 0, 0)  19.7 us
    all_to_all x1, blocking collectives, per_device(): stats = lax.all_to_all(stats, 'vocab', 0, 0)  17.7 us
    all_to_all x3, starting transfers between devices, exchange(): return lax.all_to_all(x, 'vocab', 0, 0, axis_index_groups=groups)  17.2 us
    all_to_all x1, blocking collectives, exchange(): return lax.all_to_all(x, 'vocab', 0, 0, axis_index_groups=groups)  14.7 us
    pallas_call x10, Pallas kernels, call(): pl.pallas_call(kernel, out_shape=shapes[0] if single else shapes, in_spec...  8.39 us
    all_gather x1, blocking collectives, per_device(): rows = lax.all_gather(exchange(joined, XY), 'vocab', axis_index_groups=CORE)  7.84 us
  transfers between devices with their start and end apart: 6, of which 4 were waited for; matrix products, arithmetic and copies ran while one was open for 1% of the time, Pallas kernels for 4%

profile of v6, /device:TPU:1, one launch (start us, length us, event | category | flops | bytes accessed | tf_op | source)
XLA Modules:
  0.0 164.1 jit_solution(17244728548389512924)
XLA Ops:
  8.0 0.0 all-gather.5.cloned.1.call-start
  8.0 0.7 all-gather.5.cloned.1.call-update
  8.7 0.0 copy-start.1
  8.7 1.5 copy-done.1
  10.2 0.0 copy-start.7
  10.2 0.7 copy-done.7
  10.9 0.0 copy-start.8
  10.9 0.0 copy-start.11
  10.9 2.1 %shard_map.113 = bf16[384,896]{1,0:T(8,128)(2,1)} custom-call(s32[384]{0:T(512)S(1)} %copy-done.7, bf16[1024,896]{1,0:T(8,128)(2,1)S(1)} %copy-done.1), custom_call_target="tpu_custom_call" | custom-call | tf_op jit(solution)/shard_map/pallas_call | solution.py:67
  13.0 10.4 %all-to-all-start = ((bf16[2,8,24,896]{3,2,1,0:T(8,128)(2,1)}), bf16[2,8,24,896]{3,2,1,0:T(8,128)(2,1)S(1)}, u32[]{:S(2)}, u32[]{:S(2)}) async-start(bf16[2,8,24,896]{3,2,1,0:T(8,128)(2,1)} %bitcast), calls=%async_computation | async-start | bytes 1376256 | tf_op jit(solution)/shard_map/all_to_all | solution.py:260
  23.4 0.0 copy-done.8
  23.4 0.0 copy-done.11
  23.4 0.0 copy-done
  23.4 0.0 copy-start.5
  23.4 0.9 copy-done.5
  24.4 0.4 shard_map.114.side
  24.7 0.1 all-to-all-done.half
  24.9 0.7 shard_map.115
  25.6 0.0 copy-start.3
  25.6 0.8 copy-done.3
  26.4 3.5 %all-to-all-start.1 = ((bf16[8,32,896]{2,1,0:T(8,128)(2,1)}), bf16[8,32,896]{2,1,0:T(8,128)(2,1)S(1)}, u32[]{:S(2)}, u32[]{:S(2)}) async-start(bf16[8,32,896]{2,1,0:T(8,128)(2,1)} %copy-done.3), calls=%async_computation.1 | async-start | bytes 917504 | tf_op jit(solution)/shard_map/all_to_all | solution.py:260
  29.8 0.0 reduce-scatter.2.cloned.1.call-start
  29.9 0.0 copy-done.2
  29.9 0.0 copy-done.10
  29.9 2.1 %fusion = f32[384,1024]{1,0:T(8,128)} fusion(bf16[896,1024]{1,0:T(8,128)(2,1)S(1)} %copy-done.2, bf16[384,896]{1,0:T(8,128)(2,1)S(1)} %copy-done, f32[896]{0:T(1024)S(1)} %copy-done.10), kind=kOutput, calls=%fused_computation.1 | convolution fusion | flops 705675264 | bytes 4099584 | tf_op jit(solution)/shard_map/dot_general | solution.py:301
  32.0 0.0 reduce-scatter.2.cloned.1.call-update
  32.1 19.2 %all-to-all-done.1.got.lines = bf16[8,32,896]{2,1,0:T(8,128)(2,1)S(1)} async-done(((bf16[8,32,896]{2,1,0:T(8,128)(2,1)}), bf16[8,32,896]{2,1,0:T(8,128)(2,1)S(1)}, u32[]{:S(2)}, u32[]{:S(2)}) %all-to-all-start.1) | async-done | bytes 458784 | tf_op jit(solution)/shard_map/all_to_all | solution.py:260
  51.2 0.7 shard_map.116
  51.9 3.4 %all-to-all-start.2 = ((bf16[4,24,896]{2,1,0:T(8,128)(2,1)}), bf16[4,24,896]{2,1,0:T(8,128)(2,1)S(1)}, u32[]{:S(2)}, u32[]{:S(2)}) async-start(bf16[4,24,896]{2,1,0:T(8,128)(2,1)} %shard_map.116), calls=%async_computation.2 | async-start | bytes 344064 | tf_op jit(solution)/shard_map/all_to_all | solution.py:260
  55.3 0.0 copy-done.9
  55.3 5.0 %all-to-all-done.2 = bf16[4,24,896]{2,1,0:T(8,128)(2,1)S(1)} async-done(((bf16[4,24,896]{2,1,0:T(8,128)(2,1)}), bf16[4,24,896]{2,1,0:T(8,128)(2,1)S(1)}, u32[]{:S(2)}, u32[]{:S(2)}) %all-to-all-start.2) | async-done | bytes 172064 | tf_op jit(solution)/shard_map/all_to_all | solution.py:260
  60.4 3.2 %all-gather = bf16[8,24,896]{2,1,0:T(8,128)(2,1)S(1)} all-gather(bf16[4,24,896]{2,1,0:T(8,128)(2,1)S(1)} %all-to-all-done.2), channel_id=2, replica_groups={{0,1},{2,3},{4,5},{6,7},{8,9},{10,11},{12,13},{14,15},{16,17},{18,19},{..., dimensions={0}, use_global_device_ids=true | all-gather | bytes 516096 | tf_op jit(solution)/shard_map/all_gather | solution.py:298
  63.6 1.4 copy-done.4
  65.0 0.7 shard_map.117
  65.8 19.7 %all_to_all.35.parts = bf16[8,112,128]{2,1,0:T(8,128)(2,1)S(1)} all-to-all(bf16[8,112,128]{2,1,0:T(8,128)(2,1)S(1)} %shard_map.117), channel_id=1, replica_groups=mesh['dp'=8,'vocab'=64] {'dp'}, dimensions={0} | all-to-all | bytes 458752 | tf_op jit(solution)/shard_map/all_to_all | solution.py:313
  85.5 0.2 shard_map.118
  85.7 14.7 %all_to_all.36 = bf16[32,48,128]{2,1,0:T(8,128)(2,1)S(1)} all-to-all(bf16[32,48,128]{2,1,0:T(8,128)(2,1)S(1)} %shard_map.118), channel_id=1, replica_groups={{0,2,4,6,8,10,12,14,16,18,20,22,24,26,28,30,32,34,36,38,40,42,44,46,48,..., dimensions={0} | all-to-all | bytes 786432 | tf_op jit(solution)/shard_map/all_to_all | solution.py:260
  100.4 7.8 %all-gather.2 = bf16[64,48,128]{2,1,0:T(8,128)(2,1)S(1)} all-gather(bf16[32,48,128]{2,1,0:T(8,128)(2,1)S(1)} %all_to_all.36), channel_id=4, replica_groups={{0,1},{2,3},{4,5},{6,7},{8,9},{10,11},{12,13},{14,15},{16,17},{18,19},{..., dimensions={0}, use_global_device_ids=true | all-gather | bytes 1179648 | tf_op jit(solution)/shard_map/all_gather | solution.py:314
  108.3 2.0 %shard_map.119 = bf16[8,392,128]{2,1,0:T(8,128)(2,1)} custom-call(bf16[2,32,48,128]{3,2,1,0:T(8,128)(2,1)S(1)} %bitcast.9, bf16[896,1024]{1,0:T(8,128)(2,1)S(1)} %copy-done.2), custom_call_target="tpu_custom_call" | custom-call | tf_op jit(solution)/shard_map/pallas_call | solution.py:67
  110.3 3.5 %all-to-all-start.5 = ((bf16[8,392,128]{2,1,0:T(8,128)(2,1)}), bf16[8,392,128]{2,1,0:T(8,128)(2,1)S(1)}, u32[]{:S(2)}, u32[]{:S(2)}) async-start(bf16[8,392,128]{2,1,0:T(8,128)(2,1)} %shard_map.119), calls=%async_computation.5 | async-start | bytes 1605632 | tf_op jit(solution)/shard_map/all_to_all | solution.py:322
  113.9 0.0 reduce-scatter.2.cloned.1.call-done.sums
  113.9 0.0 copy-start.6
  113.9 0.9 copy-done.6
  114.8 0.3 shard_map.120
  115.1 22.7 %all-to-all-done.5.parts = bf16[8,392,128]{2,1,0:T(8,128)(2,1)S(1)} async-done(((bf16[8,392,128]{2,1,0:T(8,128)(2,1)}), bf16[8,392,128]{2,1,0:T(8,128)(2,1)S(1)}, u32[]{:S(2)}, u32[]{:S(2)}) %all-to-all-start.5) | async-done | bytes 802848 | tf_op jit(solution)/shard_map/all_to_all | solution.py:322
  137.8 0.3 shard_map.121
  138.1 17.7 %all_to_all.37.stats = f32[64,8,128]{2,1,0:T(8,128)S(1)} all-to-all(f32[64,8,128]{2,1,0:T(8,128)S(1)} %get-tuple-element.7), channel_id=1, replica_groups=mesh['dp'=8,'vocab'=64] {'vocab'}, dimensions={0} | all-to-all | bytes 524288 | tf_op jit(solution)/shard_map/all_to_all | solution.py:327
  155.8 0.9 shard_map.122
  (9 shorter events, 0.0 us)
Async XLA Ops:
  8.0 55.6 %all-gather.5.cloned.1.call-start = ((), (), s32[]{:S(2)}) async-start(), calls=%async_computation.9 | async-start | bytes 1806336 | tf_op jit(solution)/shard_map/all_gather | solution.py:275
  8.7 1.5 copy-start.1
  10.2 0.7 copy-start.7
  10.9 12.5 %copy-start.8 = (f32[896]{0:T(1024)S(1)}, f32[896]{0:T(1024)}, u32[]{:S(2)}) copy-start(f32[896]{0:T(1024)} %param.13) | copy-start | bytes 10756
  10.9 12.5 %copy-start.11 = (f32[112]{0:T(128)S(1)}, f32[112]{0:T(128)}, u32[]{:S(2)}) copy-start(f32[112]{0:T(128)} %param.18) | copy-start | bytes 1348
  10.9 12.5 %copy-start = (bf16[384,896]{1,0:T(8,128)(2,1)S(1)}, bf16[384,896]{1,0:T(8,128)(2,1)}, u32[]{:S(2)}) copy-start(bf16[384,896]{1,0:T(8,128)(2,1)} %hidden.3) | copy-start | bytes 2064388
  13.0 11.9 %all-to-all-start = ((bf16[2,8,24,896]{3,2,1,0:T(8,128)(2,1)}), bf16[2,8,24,896]{3,2,1,0:T(8,128)(2,1)S(1)}, u32[]{:S(2)}, u32[]{:S(2)}) async-start(bf16[2,8,24,896]{3,2,1,0:T(8,128)(2,1)} %bitcast), calls=%async_computation | async-start | bytes 1376256 | tf_op jit(solution)/shard_map/all_to_all | solution.py:260
  23.4 0.9 copy-start.5
  24.3 5.5 %copy-start.2 = (bf16[896,1024]{1,0:T(8,128)(2,1)S(1)}, bf16[896,1024]{1,0:T(8,128)(2,1)}, u32[]{:S(2)}) copy-start(bf16[896,1024]{1,0:T(8,128)(2,1)} %head.1) | copy-start | bytes 5505028
  24.3 5.6 %copy-start.10 = (f32[896]{0:T(1024)S(1)}, f32[896]{0:T(1024)}, u32[]{:S(2)}) copy-start(f32[896]{0:T(1024)} %param.12) | copy-start | bytes 10756
  25.6 0.8 copy-start.3
  26.4 24.9 %all-to-all-start.1 = ((bf16[8,32,896]{2,1,0:T(8,128)(2,1)}), bf16[8,32,896]{2,1,0:T(8,128)(2,1)S(1)}, u32[]{:S(2)}, u32[]{:S(2)}) async-start(bf16[8,32,896]{2,1,0:T(8,128)(2,1)} %copy-done.3), calls=%async_computation.1 | async-start | bytes 917504 | tf_op jit(solution)/shard_map/all_to_all | solution.py:260
  29.8 84.1 %reduce-scatter.2.cloned.1.call-start = ((), (), s32[]{:S(2)}) async-start(), calls=%async_computation.8 | async-start | bytes 1769472 | tf_op jit(solution)/shard_map/reduce_scatter | solution.py:302
  32.0 23.3 %copy-start.9 = (f32[896]{0:T(1024)S(1)}, f32[896]{0:T(1024)}, u32[]{:S(2)}) copy-start(f32[896]{0:T(1024)} %param.14) | copy-start | bytes 10756
  51.9 8.4 %all-to-all-start.2 = ((bf16[4,24,896]{2,1,0:T(8,128)(2,1)}), bf16[4,24,896]{2,1,0:T(8,128)(2,1)S(1)}, u32[]{:S(2)}, u32[]{:S(2)}) async-start(bf16[4,24,896]{2,1,0:T(8,128)(2,1)} %shard_map.116), calls=%async_computation.2 | async-start | bytes 344064 | tf_op jit(solution)/shard_map/all_to_all | solution.py:260
  63.6 1.4 copy-start.4
  110.3 27.5 %all-to-all-start.5 = ((bf16[8,392,128]{2,1,0:T(8,128)(2,1)}), bf16[8,392,128]{2,1,0:T(8,128)(2,1)S(1)}, u32[]{:S(2)}, u32[]{:S(2)}) async-start(bf16[8,392,128]{2,1,0:T(8,128)(2,1)} %shard_map.119), calls=%async_computation.5 | async-start | bytes 1605632 | tf_op jit(solution)/shard_map/all_to_all | solution.py:322
  113.9 0.9 copy-start.6
Sparse Core Ops, SparseCore 0:
  10.9 52.4 all-gather.4
Sparse Core Ops, SparseCore 1:
  33.2 42.3 reduce-scatter.1

commit v7 on v6

--- a/solution.py
+++ b/solution.py
@@ -16,8 +16,8 @@
 RB = ROWS // NZ
 HB = RB // NC
 L = 128
-ZROWS = 2 * RB + 16
-HROWS = RB * (VD // L) + 8
+ZROWS = 2 * RB
+HROWS = RB * (VD // L) + 16
 PARAMS = pltpu.CompilerParams(vmem_limit_bytes=48 * 1024 * 1024)
 
 
@@ -154,15 +154,14 @@
         w = jnp.concatenate([weights[t], pad], axis=0)
         block = lines[t].astype(F32)[HB : HB + 8]
         side = jnp.concatenate([block[:, i * L : (i + 1) * L] for i in range(RB // 8)], axis=0)
-        gain = block[:, RB // 8 * L :]
         out[t, 0:RB, :] = (side + extra_h).astype(BF)
         out[t, RB : 2 * RB, :] = (dot_nt(eg, w) + extra_e).astype(BF)
-        out[t, 2 * RB :, :] = place([gain[0:1], gain[1:2]], (16, L)).astype(BF)
-
-
-def join_kernel(parts, out):
+
+
+def join_kernel(parts, lines, out):
     total = parts[0].astype(F32)
-    gain = jnp.sum(total[2 * RB :, :], axis=0, keepdims=True)
+    gain = lines[lax.axis_index("dp")].astype(F32)[HB : HB + 2, RB // 8 * L :]
+    gain = gain[0:1] + gain[1:2]
     for k in range(1, NZ):
         total = total + parts[k].astype(F32)
     lane = iota((RB, L), 1)
@@ -182,7 +181,7 @@
     out[...] = jnp.broadcast_to(x.astype(BF)[None], out.shape)
 
 
-def head_kernel(rows, head, out, x_ref):
+def head_kernel(rows, head, out, x_ref, buf, sems):
     squares = jnp.zeros((ROWS, L), F32)
     for x in range(NX):
         for c in range(NC):
@@ -193,16 +192,22 @@
     lane = iota((ROWS, L), 1)
     sq = jnp.sum(jnp.where((lane == CW) | (lane == CW + 1), squares, 0.0), axis=1, keepdims=True)
     diagonal = iota((RB, L), 0) == iota((RB, L), 1)
-    part = iota((8, L), 0)
     for k in range(NZ):
         line = jnp.sum(jnp.where(diagonal, sq[k * RB : (k + 1) * RB], 0.0), axis=0, keepdims=True)
-        out[k, HROWS - 8 :, :] = place(split(line), (8, L)).astype(BF)
+        buf[k, HROWS - 16 :, :] = place(split(line), (16, L)).astype(BF)
+    copies = []
     for n in range(0, VD, 256):
-        acc = jnp.dot(x_ref[...], head[:, n : n + 256], preferred_element_type=F32).astype(BF)
+        acc = dot(x_ref[...], head[:, n : n + 256]).astype(BF)
+        first, last = n // L * RB, (n // L + 2) * RB
         for m in range(2):
-            tile = n // L + m
             for k in range(NZ):
-                out[k, tile * RB : (tile + 1) * RB, :] = acc[k * RB : (k + 1) * RB, m * L : (m + 1) * L]
+                at = first + m * RB
+                buf[k, at : at + RB, :] = acc[k * RB : (k + 1) * RB, m * L : (m + 1) * L]
+        part = pl.ds(first, (last if n + 256 < VD else HROWS) - first)
+        copies.append(pltpu.make_async_copy(buf.at[:, part, :], out.at[:, part, :], sems.at[n // 256]))
+        copies[-1].start()
+    for copy in copies:
+        copy.wait()
 
 
 def summary(logits):
@@ -224,9 +229,9 @@
 
 def stats_kernel(parts, main_stats, out, stats):
     diagonal = iota((RB, L), 0) == iota((RB, L), 1)
-    tail = parts[0, HROWS - 8 :, :].astype(F32)
+    tail = parts[0, HROWS - 16 :, :].astype(F32)
     for k in range(1, NZ):
-        tail = tail + parts[k, HROWS - 8 :, :].astype(F32)
+        tail = tail + parts[k, HROWS - 16 :, :].astype(F32)
     squares = jnp.sum(jnp.where(diagonal, tail[0:1] + tail[1:2], 0.0), axis=1, keepdims=True)
     scale = lax.rsqrt(squares / D + EPS)
     for t in range(VD // L):
@@ -310,14 +315,19 @@
         embed_gain[None],
         weights,
     )
-    joined = call(join_kernel, struct((NQ, RB, L), BF), lax.all_to_all(partial, "dp", 0, 0))
+    joined = call(join_kernel, struct((NQ, RB, L), BF), lax.all_to_all(partial, "dp", 0, 0), lines)
     rows = lax.all_gather(exchange(joined, XY), "vocab", axis_index_groups=CORE)
     blocks = call(
         head_kernel,
         struct((NZ, HROWS, L), BF),
         rows,
         head_weight,
-        scratch=[pltpu.VMEM((ROWS, FD), BF)],
+        scratch=[
+            pltpu.VMEM((ROWS, FD), BF),
+            pltpu.VMEM((NZ, HROWS, L), BF),
+            pltpu.SemaphoreType.DMA((VD // 256,)),
+        ],
+        space=pltpu.HBM,
     )
     parts = lax.all_to_all(blocks, "dp", 0, 0)
     main_logits, main_stats = call(main_kernel, (struct((RB, VD), F32), struct((8, L), F32)), rows, main)

time: 165 us -> 165 us (level)
  no operation moved by 1% of the time
where the time goes in v7:
time: 165 us; the launch traced here: 164 us
  blocking collectives  62.6 us (38%)
  waiting for transfers between devices  48.1 us (29%)
  starting transfers between devices  20.8 us (13%)
  between operations  15.6 us (9%)
  Pallas kernels  8.34 us (5%)
  local copies, waits for them, and re-layouts  6.23 us (4%)
  matrix products  2.13 us (1%)
    all_to_all x3, waiting for transfers between devices, exchange(): return lax.all_to_all(x, 'vocab', 0, 0, axis_index_groups=groups)  24.3 us
    all_to_all x1, waiting for transfers between devices, per_device(): parts = lax.all_to_all(blocks, 'dp', 0, 0)  23 us
    all_to_all x1, blocking collectives, per_device(): lax.all_to_all(partial, 'dp', 0, 0)  18.9 us
    all_to_all x1, blocking collectives, per_device(): stats = lax.all_to_all(stats, 'vocab', 0, 0)  17.7 us
    all_to_all x3, starting transfers between devices, exchange(): return lax.all_to_all(x, 'vocab', 0, 0, axis_index_groups=groups)  17.2 us
    all_to_all x1, blocking collectives, exchange(): return lax.all_to_all(x, 'vocab', 0, 0, axis_index_groups=groups)  14.8 us
    pallas_call x10, Pallas kernels, call(): pl.pallas_call(kernel, out_shape=shapes[0] if single else shapes, in_spec...  8.34 us
    all_gather x1, blocking collectives, per_device(): rows = lax.all_gather(exchange(joined, XY), 'vocab', axis_index_groups=CORE)  7.97 us
  transfers between devices with their start and end apart: 6, of which 4 were waited for; matrix products, arithmetic and copies ran while one was open for 1% of the time, Pallas kernels for 4%

profile of v7, /device:TPU:1, one launch (start us, length us, event | category | flops | bytes accessed | tf_op | source)
XLA Modules:
  0.0 163.8 jit_solution(5686076023322110600)
XLA Ops:
  8.0 0.0 all-gather.5.cloned.1.call-start
  8.0 0.7 all-gather.5.cloned.1.call-update
  8.7 0.0 copy-start.1
  8.7 1.5 copy-done.1
  10.2 0.0 copy-start.7
  10.2 0.7 copy-done.7
  10.9 0.0 copy-start.8
  10.9 0.0 copy-start.11
  10.9 2.1 %shard_map.113 = bf16[384,896]{1,0:T(8,128)(2,1)} custom-call(s32[384]{0:T(512)S(1)} %copy-done.7, bf16[1024,896]{1,0:T(8,128)(2,1)S(1)} %copy-done.1), custom_call_target="tpu_custom_call" | custom-call | tf_op jit(solution)/shard_map/pallas_call | solution.py:67
  13.0 10.4 %all-to-all-start = ((bf16[2,8,24,896]{3,2,1,0:T(8,128)(2,1)}), bf16[2,8,24,896]{3,2,1,0:T(8,128)(2,1)S(1)}, u32[]{:S(2)}, u32[]{:S(2)}) async-start(bf16[2,8,24,896]{3,2,1,0:T(8,128)(2,1)} %bitcast), calls=%async_computation | async-start | bytes 1376256 | tf_op jit(solution)/shard_map/all_to_all | solution.py:265
  23.4 0.0 copy-done.8
  23.4 0.0 copy-done.11
  23.4 0.0 copy-done
  23.4 0.0 copy-start.5
  23.4 0.9 copy-done.5
  24.4 0.4 shard_map.114.side
  24.7 0.1 all-to-all-done.half
  24.9 0.7 shard_map.115
  25.6 0.0 copy-start.3
  25.6 0.8 copy-done.3
  26.4 3.5 %all-to-all-start.1 = ((bf16[8,32,896]{2,1,0:T(8,128)(2,1)}), bf16[8,32,896]{2,1,0:T(8,128)(2,1)S(1)}, u32[]{:S(2)}, u32[]{:S(2)}) async-start(bf16[8,32,896]{2,1,0:T(8,128)(2,1)} %copy-done.3), calls=%async_computation.1 | async-start | bytes 917504 | tf_op jit(solution)/shard_map/all_to_all | solution.py:265
  29.8 0.0 reduce-scatter.2.cloned.1.call-start
  29.9 0.0 copy-done.2
  29.9 0.0 copy-done.10
  29.9 2.1 %fusion = f32[384,1024]{1,0:T(8,128)} fusion(bf16[896,1024]{1,0:T(8,128)(2,1)S(1)} %copy-done.2, bf16[384,896]{1,0:T(8,128)(2,1)S(1)} %copy-done, f32[896]{0:T(1024)S(1)} %copy-done.10), kind=kOutput, calls=%fused_computation.1 | convolution fusion | flops 705675264 | bytes 4099584 | tf_op jit(solution)/shard_map/dot_general | solution.py:306
  32.0 0.0 reduce-scatter.2.cloned.1.call-update
  32.1 19.2 %all-to-all-done.1.got.lines = bf16[8,32,896]{2,1,0:T(8,128)(2,1)S(1)} async-done(((bf16[8,32,896]{2,1,0:T(8,128)(2,1)}), bf16[8,32,896]{2,1,0:T(8,128)(2,1)S(1)}, u32[]{:S(2)}, u32[]{:S(2)}) %all-to-all-start.1) | async-done | bytes 458784 | tf_op jit(solution)/shard_map/all_to_all | solution.py:265
  51.2 0.7 shard_map.116
  51.9 3.4 %all-to-all-start.2 = ((bf16[4,24,896]{2,1,0:T(8,128)(2,1)}), bf16[4,24,896]{2,1,0:T(8,128)(2,1)S(1)}, u32[]{:S(2)}, u32[]{:S(2)}) async-start(bf16[4,24,896]{2,1,0:T(8,128)(2,1)} %shard_map.116), calls=%async_computation.2 | async-start | bytes 344064 | tf_op jit(solution)/shard_map/all_to_all | solution.py:265
  55.3 0.0 copy-done.9
  55.3 5.0 %all-to-all-done.2 = bf16[4,24,896]{2,1,0:T(8,128)(2,1)S(1)} async-done(((bf16[4,24,896]{2,1,0:T(8,128)(2,1)}), bf16[4,24,896]{2,1,0:T(8,128)(2,1)S(1)}, u32[]{:S(2)}, u32[]{:S(2)}) %all-to-all-start.2) | async-done | bytes 172064 | tf_op jit(solution)/shard_map/all_to_all | solution.py:265
  60.4 3.2 %all-gather = bf16[8,24,896]{2,1,0:T(8,128)(2,1)S(1)} all-gather(bf16[4,24,896]{2,1,0:T(8,128)(2,1)S(1)} %all-to-all-done.2), channel_id=2, replica_groups={{0,1},{2,3},{4,5},{6,7},{8,9},{10,11},{12,13},{14,15},{16,17},{18,19},{..., dimensions={0}, use_global_device_ids=true | all-gather | bytes 516096 | tf_op jit(solution)/shard_map/all_gather | solution.py:303
  63.6 1.4 copy-done.4
  65.0 0.7 shard_map.117
  65.8 18.9 %all_to_all.35.parts = bf16[8,96,128]{2,1,0:T(8,128)(2,1)S(1)} all-to-all(bf16[8,96,128]{2,1,0:T(8,128)(2,1)S(1)} %shard_map.117), channel_id=1, replica_groups=mesh['dp'=8,'vocab'=64] {'dp'}, dimensions={0} | all-to-all | bytes 393216 | tf_op jit(solution)/shard_map/all_to_all | solution.py:318
  84.7 0.2 shard_map.118
  84.9 14.8 %all_to_all.36 = bf16[32,48,128]{2,1,0:T(8,128)(2,1)S(1)} all-to-all(bf16[32,48,128]{2,1,0:T(8,128)(2,1)S(1)} %shard_map.118), channel_id=1, replica_groups={{0,2,4,6,8,10,12,14,16,18,20,22,24,26,28,30,32,34,36,38,40,42,44,46,48,..., dimensions={0} | all-to-all | bytes 786432 | tf_op jit(solution)/shard_map/all_to_all | solution.py:265
  99.7 8.0 %all-gather.2 = bf16[64,48,128]{2,1,0:T(8,128)(2,1)S(1)} all-gather(bf16[32,48,128]{2,1,0:T(8,128)(2,1)S(1)} %all_to_all.36), channel_id=4, replica_groups={{0,1},{2,3},{4,5},{6,7},{8,9},{10,11},{12,13},{14,15},{16,17},{18,19},{..., dimensions={0}, use_global_device_ids=true | all-gather | bytes 1179648 | tf_op jit(solution)/shard_map/all_gather | solution.py:319
  107.6 2.0 %shard_map.119 = bf16[8,400,128]{2,1,0:T(8,128)(2,1)} custom-call(bf16[2,32,48,128]{3,2,1,0:T(8,128)(2,1)S(1)} %bitcast.9, bf16[896,1024]{1,0:T(8,128)(2,1)S(1)} %copy-done.2), custom_call_target="tpu_custom_call" | custom-call | tf_op jit(solution)/shard_map/pallas_call | solution.py:67
  109.6 3.6 %all-to-all-start.5 = ((bf16[8,400,128]{2,1,0:T(8,128)(2,1)}), bf16[8,400,128]{2,1,0:T(8,128)(2,1)S(1)}, u32[]{:S(2)}, u32[]{:S(2)}) async-start(bf16[8,400,128]{2,1,0:T(8,128)(2,1)} %shard_map.119), calls=%async_computation.5 | async-start | bytes 1638400 | tf_op jit(solution)/shard_map/all_to_all | solution.py:332
  113.2 0.0 reduce-scatter.2.cloned.1.call-done.sums
  113.2 0.0 copy-start.6
  113.3 0.9 copy-done.6
  114.2 0.3 shard_map.120
  114.5 23.0 %all-to-all-done.5.parts = bf16[8,400,128]{2,1,0:T(8,128)(2,1)S(1)} async-done(((bf16[8,400,128]{2,1,0:T(8,128)(2,1)}), bf16[8,400,128]{2,1,0:T(8,128)(2,1)S(1)}, u32[]{:S(2)}, u32[]{:S(2)}) %all-to-all-start.5) | async-done | bytes 819232 | tf_op jit(solution)/shard_map/all_to_all | solution.py:332
  137.5 0.3 shard_map.121
  137.8 17.7 %all_to_all.37.stats = f32[64,8,128]{2,1,0:T(8,128)S(1)} all-to-all(f32[64,8,128]{2,1,0:T(8,128)S(1)} %get-tuple-element.7), channel_id=1, replica_groups=mesh['dp'=8,'vocab'=64] {'vocab'}, dimensions={0} | all-to-all | bytes 524288 | tf_op jit(solution)/shard_map/all_to_all | solution.py:337
  155.5 0.9 shard_map.122
  (9 shorter events, 0.0 us)
Async XLA Ops:
  8.0 55.6 %all-gather.5.cloned.1.call-start = ((), (), s32[]{:S(2)}) async-start(), calls=%async_computation.9 | async-start | bytes 1806336 | tf_op jit(solution)/shard_map/all_gather | solution.py:280
  8.7 1.5 copy-start.1
  10.2 0.7 copy-start.7
  10.9 12.5 %copy-start.8 = (f32[896]{0:T(1024)S(1)}, f32[896]{0:T(1024)}, u32[]{:S(2)}) copy-start(f32[896]{0:T(1024)} %param.13) | copy-start | bytes 10756
  10.9 12.5 %copy-start.11 = (f32[112]{0:T(128)S(1)}, f32[112]{0:T(128)}, u32[]{:S(2)}) copy-start(f32[112]{0:T(128)} %param.18) | copy-start | bytes 1348
  10.9 12.5 %copy-start = (bf16[384,896]{1,0:T(8,128)(2,1)S(1)}, bf16[384,896]{1,0:T(8,128)(2,1)}, u32[]{:S(2)}) copy-start(bf16[384,896]{1,0:T(8,128)(2,1)} %hidden.3) | copy-start | bytes 2064388
  13.0 11.9 %all-to-all-start = ((bf16[2,8,24,896]{3,2,1,0:T(8,128)(2,1)}), bf16[2,8,24,896]{3,2,1,0:T(8,128)(2,1)S(1)}, u32[]{:S(2)}, u32[]{:S(2)}) async-start(bf16[2,8,24,896]{3,2,1,0:T(8,128)(2,1)} %bitcast), calls=%async_computation | async-start | bytes 1376256 | tf_op jit(solution)/shard_map/all_to_all | solution.py:265
  23.4 0.9 copy-start.5
  24.3 5.5 %copy-start.2 = (bf16[896,1024]{1,0:T(8,128)(2,1)S(1)}, bf16[896,1024]{1,0:T(8,128)(2,1)}, u32[]{:S(2)}) copy-start(bf16[896,1024]{1,0:T(8,128)(2,1)} %head.1) | copy-start | bytes 5505028
  24.3 5.6 %copy-start.10 = (f32[896]{0:T(1024)S(1)}, f32[896]{0:T(1024)}, u32[]{:S(2)}) copy-start(f32[896]{0:T(1024)} %param.12) | copy-start | bytes 10756
  25.6 0.8 copy-start.3
  26.4 24.9 %all-to-all-start.1 = ((bf16[8,32,896]{2,1,0:T(8,128)(2,1)}), bf16[8,32,896]{2,1,0:T(8,128)(2,1)S(1)}, u32[]{:S(2)}, u32[]{:S(2)}) async-start(bf16[8,32,896]{2,1,0:T(8,128)(2,1)} %copy-done.3), calls=%async_computation.1 | async-start | bytes 917504 | tf_op jit(solution)/shard_map/all_to_all | solution.py:265
  29.8 83.4 %reduce-scatter.2.cloned.1.call-start = ((), (), s32[]{:S(2)}) async-start(), calls=%async_computation.8 | async-start | bytes 1769472 | tf_op jit(solution)/shard_map/reduce_scatter | solution.py:307
  32.0 23.3 %copy-start.9 = (f32[896]{0:T(1024)S(1)}, f32[896]{0:T(1024)}, u32[]{:S(2)}) copy-start(f32[896]{0:T(1024)} %param.14) | copy-start | bytes 10756
  51.9 8.4 %all-to-all-start.2 = ((bf16[4,24,896]{2,1,0:T(8,128)(2,1)}), bf16[4,24,896]{2,1,0:T(8,128)(2,1)S(1)}, u32[]{:S(2)}, u32[]{:S(2)}) async-start(bf16[4,24,896]{2,1,0:T(8,128)(2,1)} %shard_map.116), calls=%async_computation.2 | async-start | bytes 344064 | tf_op jit(solution)/shard_map/all_to_all | solution.py:265
  63.6 1.4 copy-start.4
  109.6 27.8 %all-to-all-start.5 = ((bf16[8,400,128]{2,1,0:T(8,128)(2,1)}), bf16[8,400,128]{2,1,0:T(8,128)(2,1)S(1)}, u32[]{:S(2)}, u32[]{:S(2)}) async-start(bf16[8,400,128]{2,1,0:T(8,128)(2,1)} %shard_map.119), calls=%async_computation.5 | async-start | bytes 1638400 | tf_op jit(solution)/shard_map/all_to_all | solution.py:332
  113.2 0.9 copy-start.6
Sparse Core Ops, SparseCore 0:
  10.9 52.4 all-gather.4
Sparse Core Ops, SparseCore 1:
  33.2 42.3 reduce-scatter.1

commit v8 on v7

--- a/solution.py
+++ b/solution.py
@@ -63,6 +63,8 @@
 def call(kernel, outs, *args, scratch=(), space=pltpu.VMEM):
     single = not isinstance(outs, (list, tuple))
     shapes = [outs] if single else list(outs)
+    if space is pltpu.HBM:
+        shapes = [pltpu.HBM(s.shape, s.dtype) for s in shapes]
     specs = [pl.BlockSpec(memory_space=space) for _ in shapes]
     return pl.pallas_call(
         kernel,
@@ -181,14 +183,20 @@
     out[...] = jnp.broadcast_to(x.astype(BF)[None], out.shape)
 
 
+def pad_kernel(head, out):
+    for j in range(NX * NC):
+        out[j * L : j * L + CW, :] = head[j * CW : (j + 1) * CW, :]
+        out[j * L + CW : (j + 1) * L, :] = jnp.zeros((L - CW, VD), BF)
+
+
 def head_kernel(rows, head, out, x_ref, buf, sems):
     squares = jnp.zeros((ROWS, L), F32)
     for x in range(NX):
         for c in range(NC):
-            a = jnp.concatenate([rows[c, y * NX + x] for y in range(NY)], axis=0)
             j = x * NC + c
-            x_ref[:, j * CW : (j + 1) * CW] = a[:, 0:CW]
-            squares = squares + a.astype(F32)
+            for y in range(NY):
+                x_ref[y * RB : (y + 1) * RB, j * L : (j + 1) * L] = rows[c, y * NX + x]
+            squares = squares + x_ref[:, j * L : (j + 1) * L].astype(F32)
     lane = iota((ROWS, L), 1)
     sq = jnp.sum(jnp.where((lane == CW) | (lane == CW + 1), squares, 0.0), axis=1, keepdims=True)
     diagonal = iota((RB, L), 0) == iota((RB, L), 1)
@@ -317,13 +325,14 @@
     )
     joined = call(join_kernel, struct((NQ, RB, L), BF), lax.all_to_all(partial, "dp", 0, 0), lines)
     rows = lax.all_gather(exchange(joined, XY), "vocab", axis_index_groups=CORE)
+    padded = call(pad_kernel, struct((NX * NC * L, VD), BF), head_weight)
     blocks = call(
         head_kernel,
         struct((NZ, HROWS, L), BF),
         rows,
-        head_weight,
+        padded,
         scratch=[
-            pltpu.VMEM((ROWS, FD), BF),
+            pltpu.VMEM((ROWS, NX * NC * L), BF),
             pltpu.VMEM((NZ, HROWS, L), BF),
             pltpu.SemaphoreType.DMA((VD // 256,)),
         ],

time: 165 us -> 166 us (level)
  blocking collectives: 62.6 us -> 47.4 us
  waiting for transfers between devices: 48.1 us -> 57.3 us
  starting transfers between devices: 20.8 us -> 26.1 us
    all_to_all x1 -> x0, blocking collectives: 14.8 us -> none  [exchange(): return lax.all_to_all(x, 'vocab', 0, 0, axis_index_groups=groups)]
    all_to_all x3 -> x4, waiting for transfers between devices: 24.3 us -> 33.5 us  [exchange(): return lax.all_to_all(x, 'vocab', 0, 0, axis_index_groups=groups)]
    all_to_all x3 -> x4, starting transfers between devices: 17.2 us -> 22.4 us  [exchange(): return lax.all_to_all(x, 'vocab', 0, 0, axis_index_groups=groups)]
    pallas_call x10 -> x11, Pallas kernels: 8.34 us -> 9.17 us  [call(): pl.pallas_call(kernel, out_shape=shapes[0] if single else shapes, in_spec...]
  transfers between devices with their start and end apart: 6 -> 7, of which waited for: 4 -> 4; matrix products, arithmetic and copies ran while one was open for 1% -> 1% of each run, Pallas kernels for 4% -> 5%
where the time goes in v8:
time: 166 us; the launch traced here: 165 us
  waiting for transfers between devices  57.3 us (35%)
  blocking collectives  47.4 us (29%)
  starting transfers between devices  26.1 us (16%)
  between operations  15.7 us (9%)
  Pallas kernels  9.17 us (6%)
  local copies, waits for them, and re-layouts  7.1 us (4%)
  matrix products  2.12 us (1%)
    all_to_all x4, waiting for transfers between devices, exchange(): return lax.all_to_all(x, 'vocab', 0, 0, axis_index_groups=groups)  33.5 us
    all_to_all x1, waiting for transfers between devices, per_device(): parts = lax.all_to_all(blocks, 'dp', 0, 0)  23 us
    all_to_all x4, starting transfers between devices, exchange(): return lax.all_to_all(x, 'vocab', 0, 0, axis_index_groups=groups)  22.4 us
    all_to_all x1, blocking collectives, per_device(): stats = lax.all_to_all(stats, 'vocab', 0, 0)  17.7 us
    all_to_all x1, blocking collectives, per_device(): lax.all_to_all(partial, 'dp', 0, 0)  17.6 us
    pallas_call x11, Pallas kernels, call(): pl.pallas_call(kernel, out_shape=shapes[0] if single else shapes, in_spec...  9.17 us
    all_gather x1, blocking collectives, per_device(): rows = lax.all_gather(exchange(joined, XY), 'vocab', axis_index_groups=CORE)  8.45 us
    unnamed x24, local copies, waits for them, and re-layouts  7.09 us
  transfers between devices with their start and end apart: 7, of which 4 were waited for; matrix products, arithmetic and copies ran while one was open for 1% of the time, Pallas kernels for 5%

profile of v8, /device:TPU:1, one launch (start us, length us, event | category | flops | bytes accessed | tf_op | source)
XLA Modules:
  0.0 164.9 jit_solution(16374624362743306904)
XLA Ops:
  8.0 0.0 all-gather.5.cloned.1.call-start
  8.0 0.7 all-gather.5.cloned.1.call-update
  8.7 0.0 copy-start.1
  8.7 1.5 copy-done.1
  10.2 0.7 copy-done.7
  10.9 2.1 %shard_map.113 = bf16[384,896]{1,0:T(8,128)(2,1)} custom-call(s32[384]{0:T(512)S(1)} %copy-done.7, bf16[1024,896]{1,0:T(8,128)(2,1)S(1)} %copy-done.1), custom_call_target="tpu_custom_call" | custom-call | tf_op jit(solution)/shard_map/pallas_call | solution.py:69
  13.0 0.0 copy-start.10
  13.0 10.4 %all-to-all-start = ((bf16[2,8,24,896]{3,2,1,0:T(8,128)(2,1)}), bf16[2,8,24,896]{3,2,1,0:T(8,128)(2,1)S(1)}, u32[]{:S(2)}, u32[]{:S(2)}) async-start(bf16[2,8,24,896]{3,2,1,0:T(8,128)(2,1)} %bitcast.14), calls=%async_computation | async-start | bytes 1376256 | tf_op jit(solution)/shard_map/all_to_all | solution.py:273
  23.4 0.0 copy-done.8
  23.4 0.0 copy-done.11
  23.4 0.0 copy-done
  23.4 0.0 copy-start.5
  23.5 1.0 copy-done.5
  24.5 0.4 shard_map.114.side
  24.9 0.0 all-to-all-done.half
  24.9 0.8 shard_map.115
  25.7 3.5 %all-to-all-start.1 = ((bf16[8,32,896]{2,1,0:T(8,128)(2,1)}), bf16[8,32,896]{2,1,0:T(8,128)(2,1)S(1)}, u32[]{:S(2)}, u32[]{:S(2)}) async-start(bf16[8,32,896]{2,1,0:T(8,128)(2,1)} %shard_map.115), calls=%async_computation.1 | async-start | bytes 917504 | tf_op jit(solution)/shard_map/all_to_all | solution.py:273
  29.2 0.0 reduce-scatter.2.cloned.1.call-start
  29.3 0.0 copy-done.10
  29.3 0.0 copy-done.2
  29.3 2.1 %fusion = f32[384,1024]{1,0:T(8,128)} fusion(bf16[896,1024]{1,0:T(8,128)(2,1)S(1)} %copy-done.2, bf16[384,896]{1,0:T(8,128)(2,1)S(1)} %copy-done, f32[896]{0:T(1024)S(1)} %copy-done.10), kind=kOutput, calls=%fused_computation.1 | convolution fusion | flops 705675264 | bytes 4099584 | tf_op jit(solution)/shard_map/dot_general | solution.py:314
  31.4 0.0 reduce-scatter.2.cloned.1.call-update
  31.4 18.7 %all-to-all-done.1.got.lines = bf16[8,32,896]{2,1,0:T(8,128)(2,1)S(1)} async-done(((bf16[8,32,896]{2,1,0:T(8,128)(2,1)}), bf16[8,32,896]{2,1,0:T(8,128)(2,1)S(1)}, u32[]{:S(2)}, u32[]{:S(2)}) %all-to-all-start.1) | async-done | bytes 458784 | tf_op jit(solution)/shard_map/all_to_all | solution.py:273
  50.1 0.7 shard_map.116
  50.8 3.3 %all-to-all-start.2 = ((bf16[4,24,896]{2,1,0:T(8,128)(2,1)}), bf16[4,24,896]{2,1,0:T(8,128)(2,1)S(1)}, u32[]{:S(2)}, u32[]{:S(2)}) async-start(bf16[4,24,896]{2,1,0:T(8,128)(2,1)} %shard_map.116), calls=%async_computation.2 | async-start | bytes 344064 | tf_op jit(solution)/shard_map/all_to_all | solution.py:273
  54.2 0.0 copy-done.9
  54.2 5.0 %all-to-all-done.2 = bf16[4,24,896]{2,1,0:T(8,128)(2,1)S(1)} async-done(((bf16[4,24,896]{2,1,0:T(8,128)(2,1)}), bf16[4,24,896]{2,1,0:T(8,128)(2,1)S(1)}, u32[]{:S(2)}, u32[]{:S(2)}) %all-to-all-start.2) | async-done | bytes 172064 | tf_op jit(solution)/shard_map/all_to_all | solution.py:273
  59.3 3.7 %all-gather = bf16[8,24,896]{2,1,0:T(8,128)(2,1)S(1)} all-gather(bf16[4,24,896]{2,1,0:T(8,128)(2,1)S(1)} %all-to-all-done.2), channel_id=2, replica_groups={{0,1},{2,3},{4,5},{6,7},{8,9},{10,11},{12,13},{14,15},{16,17},{18,19},{..., dimensions={0}, use_global_device_ids=true | all-gather | bytes 516096 | tf_op jit(solution)/shard_map/all_gather | solution.py:311
  63.0 1.4 copy-done.4
  64.4 0.7 shard_map.117
  65.2 17.6 %all_to_all.35.parts = bf16[8,96,128]{2,1,0:T(8,128)(2,1)S(1)} all-to-all(bf16[8,96,128]{2,1,0:T(8,128)(2,1)S(1)} %shard_map.117), channel_id=1, replica_groups=mesh['dp'=8,'vocab'=64] {'dp'}, dimensions={0} | all-to-all | bytes 393216 | tf_op jit(solution)/shard_map/all_to_all | solution.py:326
  82.8 1.0 shard_map.118
  83.7 5.2 %all-to-all-start.4 = ((bf16[32,48,128]{2,1,0:T(8,128)(2,1)}), bf16[32,48,128]{2,1,0:T(8,128)(2,1)S(1)}, u32[]{:S(2)}, u32[]{:S(2)}) async-start(bf16[32,48,128]{2,1,0:T(8,128)(2,1)} %shard_map.118), calls=%async_computation.4 | async-start | bytes 786432 | tf_op jit(solution)/shard_map/all_to_all | solution.py:273
  89.0 0.0 copy-start.3
  89.0 1.5 copy-done.3
  90.5 0.1 shard_map.119.head
  90.6 9.8 %all-to-all-done.4 = bf16[32,48,128]{2,1,0:T(8,128)(2,1)S(1)} async-done(((bf16[32,48,128]{2,1,0:T(8,128)(2,1)}), bf16[32,48,128]{2,1,0:T(8,128)(2,1)S(1)}, u32[]{:S(2)}, u32[]{:S(2)}) %all-to-all-start.4) | async-done | bytes 393248 | tf_op jit(solution)/shard_map/all_to_all | solution.py:273
  100.4 8.5 %all-gather.2 = bf16[64,48,128]{2,1,0:T(8,128)(2,1)S(1)} all-gather(bf16[32,48,128]{2,1,0:T(8,128)(2,1)S(1)} %all-to-all-done.4), channel_id=4, replica_groups={{0,1},{2,3},{4,5},{6,7},{8,9},{10,11},{12,13},{14,15},{16,17},{18,19},{..., dimensions={0}, use_global_device_ids=true | all-gather | bytes 1179648 | tf_op jit(solution)/shard_map/all_gather | solution.py:327
  108.9 1.8 %shard_map.120 = bf16[8,400,128]{2,1,0:T(8,128)(2,1)} custom-call(bf16[2,32,48,128]{3,2,1,0:T(8,128)(2,1)S(1)} %bitcast.9, bf16[1024,1024]{1,0:T(8,128)(2,1)S(1)} %shard_map.119.head), custom_call_target="tpu_custom_call" | custom-call | tf_op jit(solution)/shard_map/pallas_call | solution.py:69
  110.7 3.6 %all-to-all-start.5 = ((bf16[8,400,128]{2,1,0:T(8,128)(2,1)}), bf16[8,400,128]{2,1,0:T(8,128)(2,1)S(1)}, u32[]{:S(2)}, u32[]{:S(2)}) async-start(bf16[8,400,128]{2,1,0:T(8,128)(2,1)} %shard_map.120), calls=%async_computation.5 | async-start | bytes 1638400 | tf_op jit(solution)/shard_map/all_to_all | solution.py:341
  114.2 0.0 reduce-scatter.2.cloned.1.call-done.sums
  114.3 0.0 copy-start.6
  114.3 0.9 copy-done.6
  115.2 0.3 shard_map.121
  115.5 23.0 %all-to-all-done.5.parts = bf16[8,400,128]{2,1,0:T(8,128)(2,1)S(1)} async-done(((bf16[8,400,128]{2,1,0:T(8,128)(2,1)}), bf16[8,400,128]{2,1,0:T(8,128)(2,1)S(1)}, u32[]{:S(2)}, u32[]{:S(2)}) %all-to-all-start.5) | async-done | bytes 819232 | tf_op jit(solution)/shard_map/all_to_all | solution.py:341
  138.5 0.3 shard_map.122
  138.8 17.7 %all_to_all.36.stats = f32[64,8,128]{2,1,0:T(8,128)S(1)} all-to-all(f32[64,8,128]{2,1,0:T(8,128)S(1)} %get-tuple-element.7), channel_id=1, replica_groups=mesh['dp'=8,'vocab'=64] {'vocab'}, dimensions={0} | all-to-all | bytes 524288 | tf_op jit(solution)/shard_map/all_to_all | solution.py:346
  156.5 0.9 shard_map.123
  (11 shorter events, 0.0 us)
Async XLA Ops:
  8.0 55.0 %all-gather.5.cloned.1.call-start = ((), (), s32[]{:S(2)}) async-start(), calls=%async_computation.9 | async-start | bytes 1806336 | tf_op jit(solution)/shard_map/all_gather | solution.py:288
  8.7 1.5 copy-start.1
  10.2 0.7 copy-start.7
  10.9 12.5 %copy-start.8 = (f32[896]{0:T(1024)S(1)}, f32[896]{0:T(1024)}, u32[]{:S(2)}) copy-start(f32[896]{0:T(1024)} %param.13) | copy-start | bytes 10756
  10.9 12.5 %copy-start.11 = (f32[112]{0:T(128)S(1)}, f32[112]{0:T(128)}, u32[]{:S(2)}) copy-start(f32[112]{0:T(128)} %param.18) | copy-start | bytes 1348
  10.9 12.5 %copy-start = (bf16[384,896]{1,0:T(8,128)(2,1)S(1)}, bf16[384,896]{1,0:T(8,128)(2,1)}, u32[]{:S(2)}) copy-start(bf16[384,896]{1,0:T(8,128)(2,1)} %hidden.3) | copy-start | bytes 2064388
  13.0 16.3 %copy-start.10 = (f32[896]{0:T(1024)S(1)}, f32[896]{0:T(1024)}, u32[]{:S(2)}) copy-start(f32[896]{0:T(1024)} %param.12) | copy-start | bytes 10756
  13.0 11.9 %all-to-all-start = ((bf16[2,8,24,896]{3,2,1,0:T(8,128)(2,1)}), bf16[2,8,24,896]{3,2,1,0:T(8,128)(2,1)S(1)}, u32[]{:S(2)}, u32[]{:S(2)}) async-start(bf16[2,8,24,896]{3,2,1,0:T(8,128)(2,1)} %bitcast.14), calls=%async_computation | async-start | bytes 1376256 | tf_op jit(solution)/shard_map/all_to_all | solution.py:273
  23.4 5.9 %copy-start.2 = (bf16[896,1024]{1,0:T(8,128)(2,1)S(1)}, bf16[896,1024]{1,0:T(8,128)(2,1)}, u32[]{:S(2)}) copy-start(bf16[896,1024]{1,0:T(8,128)(2,1)} %head.1) | copy-start | bytes 5505028
  23.4 1.1 copy-start.5
  25.7 24.4 %all-to-all-start.1 = ((bf16[8,32,896]{2,1,0:T(8,128)(2,1)}), bf16[8,32,896]{2,1,0:T(8,128)(2,1)S(1)}, u32[]{:S(2)}, u32[]{:S(2)}) async-start(bf16[8,32,896]{2,1,0:T(8,128)(2,1)} %shard_map.115), calls=%async_computation.1 | async-start | bytes 917504 | tf_op jit(solution)/shard_map/all_to_all | solution.py:273
  29.2 85.0 %reduce-scatter.2.cloned.1.call-start = ((), (), s32[]{:S(2)}) async-start(), calls=%async_computation.8 | async-start | bytes 1769472 | tf_op jit(solution)/shard_map/reduce_scatter | solution.py:315
  31.4 22.8 %copy-start.9 = (f32[896]{0:T(1024)S(1)}, f32[896]{0:T(1024)}, u32[]{:S(2)}) copy-start(f32[896]{0:T(1024)} %param.14) | copy-start | bytes 10756
  50.8 8.4 %all-to-all-start.2 = ((bf16[4,24,896]{2,1,0:T(8,128)(2,1)}), bf16[4,24,896]{2,1,0:T(8,128)(2,1)S(1)}, u32[]{:S(2)}, u32[]{:S(2)}) async-start(bf16[4,24,896]{2,1,0:T(8,128)(2,1)} %shard_map.116), calls=%async_computation.2 | async-start | bytes 344064 | tf_op jit(solution)/shard_map/all_to_all | solution.py:273
  63.0 1.4 copy-start.4
  83.7 16.7 %all-to-all-start.4 = ((bf16[32,48,128]{2,1,0:T(8,128)(2,1)}), bf16[32,48,128]{2,1,0:T(8,128)(2,1)S(1)}, u32[]{:S(2)}, u32[]{:S(2)}) async-start(bf16[32,48,128]{2,1,0:T(8,128)(2,1)} %shard_map.118), calls=%async_computation.4 | async-start | bytes 786432 | tf_op jit(solution)/shard_map/all_to_all | solution.py:273
  89.0 1.5 copy-start.3
  110.7 27.8 %all-to-all-start.5 = ((bf16[8,400,128]{2,1,0:T(8,128)(2,1)}), bf16[8,400,128]{2,1,0:T(8,128)(2,1)S(1)}, u32[]{:S(2)}, u32[]{:S(2)}) async-start(bf16[8,400,128]{2,1,0:T(8,128)(2,1)} %shard_map.120), calls=%async_computation.5 | async-start | bytes 1638400 | tf_op jit(solution)/shard_map/all_to_all | solution.py:341
  114.3 0.9 copy-start.6
Sparse Core Ops, SparseCore 0:
  10.9 51.5 all-gather.4
Sparse Core Ops, SparseCore 1:
  32.5 42.2 reduce-scatter.1

commit v9 on v7

--- a/solution.py
+++ b/solution.py
@@ -60,14 +60,17 @@
     return out
 
 
-def call(kernel, outs, *args, scratch=(), space=pltpu.VMEM):
+def call(kernel, outs, *args, scratch=(), space=pltpu.VMEM, far=()):
+    args = [pltpu.with_memory_space_constraint(a, pltpu.HBM) if k in far else a for k, a in enumerate(args)]
     single = not isinstance(outs, (list, tuple))
     shapes = [outs] if single else list(outs)
+    if space is pltpu.HBM:
+        shapes = [pltpu.HBM(s.shape, s.dtype) for s in shapes]
     specs = [pl.BlockSpec(memory_space=space) for _ in shapes]
     return pl.pallas_call(
         kernel,
         out_shape=shapes[0] if single else shapes,
-        in_specs=[pl.BlockSpec(memory_space=pltpu.VMEM)] * len(args),
+        in_specs=[pl.BlockSpec(memory_space=pltpu.HBM if k in far else pltpu.VMEM) for k in range(len(args))],
         out_specs=specs[0] if single else specs,
         scratch_shapes=list(scratch),
         compiler_params=PARAMS,
@@ -131,7 +134,10 @@
     out[...] = jnp.broadcast_to(total.astype(BF)[None], out.shape)
 
 
-def proj_kernel(picked, lines, hidden, embed_gain, weights, out):
+def proj_kernel(picked, lines, hidden, embed_gain, weights, out, weights_v, sems):
+    copies = [pltpu.make_async_copy(weights.at[t], weights_v.at[t], sems.at[t]) for t in range(NY)]
+    for copy in copies:
+        copy.start()
     y = lax.axis_index("vocab") // (NX * NC)
     h = hidden[pl.ds(pl.multiple_of(y * RB, 16), RB), :].astype(F32)
     halves = []
@@ -148,10 +154,11 @@
         return jnp.where(lane == CW, hi, jnp.where(lane == CW + 1, low, 0.0))
 
     extra_h, extra_e = extra(h), extra(e)
-    eg = (e * embed_gain[...]).astype(BF)
+    eg = (e * embed_gain[...].reshape(1, FD)).astype(BF)
     pad = jnp.zeros((L - CW, FD), BF)
     for t in range(NY):
-        w = jnp.concatenate([weights[t], pad], axis=0)
+        copies[t].wait()
+        w = jnp.concatenate([weights_v[t], pad], axis=0)
         block = lines[t].astype(F32)[HB : HB + 8]
         side = jnp.concatenate([block[:, i * L : (i + 1) * L] for i in range(RB // 8)], axis=0)
         out[t, 0:RB, :] = (side + extra_h).astype(BF)
@@ -312,8 +319,10 @@
         got,
         lines,
         hidden,
-        embed_gain[None],
+        embed_gain,
         weights,
+        far=(4,),
+        scratch=[pltpu.VMEM((NY, CW, FD), BF), pltpu.SemaphoreType.DMA((NY,))],
     )
     joined = call(join_kernel, struct((NQ, RB, L), BF), lax.all_to_all(partial, "dp", 0, 0), lines)
     rows = lax.all_gather(exchange(joined, XY), "vocab", axis_index_groups=CORE)

time: 165 us -> 165 us (level)
  blocking collectives: 62.6 us -> 71.3 us
  waiting for transfers between devices: 48.1 us -> 43.8 us
  starting transfers between devices: 20.8 us -> 17.5 us
  local copies, waits for them, and re-layouts: 6.23 us -> 4.05 us
  Pallas kernels: 8.34 us -> 10.1 us
    all_to_all x1 -> x2, blocking collectives: 14.8 us -> 24.9 us  [exchange(): return lax.all_to_all(x, 'vocab', 0, 0, axis_index_groups=groups)]
    all_to_all x3 -> x2, waiting for transfers between devices: 24.3 us -> 18.9 us  [exchange(): return lax.all_to_all(x, 'vocab', 0, 0, axis_index_groups=groups)]
    all_to_all x3 -> x2, starting transfers between devices: 17.2 us -> 13.9 us  [exchange(): return lax.all_to_all(x, 'vocab', 0, 0, axis_index_groups=groups)]
    unnamed x24 -> x20, local copies, waits for them, and re-layouts: 6.22 us -> 4.04 us
    pallas_call x10, Pallas kernels: 8.34 us -> 10.1 us  [call(): pl.pallas_call(kernel, out_shape=shapes[0] if single else shapes, in_spec...]
  transfers between devices with their start and end apart: 6 -> 5, of which waited for: 4 -> 4; matrix products, arithmetic and copies ran while one was open for 1% -> 1% of each run, Pallas kernels for 4% -> 5%
where the time goes in v9:
time: 165 us; the launch traced here: 164 us
  blocking collectives  71.3 us (43%)
  waiting for transfers between devices  43.8 us (27%)
  starting transfers between devices  17.5 us (11%)
  between operations  15.6 us (9%)
  Pallas kernels  10.1 us (6%)
  local copies, waits for them, and re-layouts  4.05 us (2%)
  matrix products  2.12 us (1%)
    all_to_all x2, blocking collectives, exchange(): return lax.all_to_all(x, 'vocab', 0, 0, axis_index_groups=groups)  24.9 us
    all_to_all x1, waiting for transfers between devices, per_device(): parts = lax.all_to_all(blocks, 'dp', 0, 0)  23 us
    all_to_all x2, waiting for transfers between devices, exchange(): return lax.all_to_all(x, 'vocab', 0, 0, axis_index_groups=groups)  18.9 us
    all_to_all x1, blocking collectives, per_device(): stats = lax.all_to_all(stats, 'vocab', 0, 0)  17.7 us
    all_to_all x1, blocking collectives, per_device(): lax.all_to_all(partial, 'dp', 0, 0)  17.4 us
    all_to_all x2, starting transfers between devices, exchange(): return lax.all_to_all(x, 'vocab', 0, 0, axis_index_groups=groups)  13.9 us
    pallas_call x10, Pallas kernels, call(): pl.pallas_call(kernel, out_shape=shapes[0] if single else shapes, in_spec...  10.1 us
    all_gather x1, blocking collectives, per_device(): rows = lax.all_gather(exchange(joined, XY), 'vocab', axis_index_groups=CORE)  7.64 us
  transfers between devices with their start and end apart: 5, of which 4 were waited for; matrix products, arithmetic and copies ran while one was open for 1% of the time, Pallas kernels for 5%

profile of v9, /device:TPU:1, one launch (start us, length us, event | category | flops | bytes accessed | tf_op | source)
XLA Modules:
  0.0 164.4 jit_solution(13152067603547755445)
XLA Ops:
  8.0 0.0 all-gather.5.cloned.1.call-start
  8.0 0.7 all-gather.5.cloned.1.call-update
  8.7 0.0 copy-start.1
  8.7 1.5 copy-done.1
  10.2 0.0 copy-start.6
  10.2 0.7 copy-done.6
  10.9 0.0 copy-start.7
  10.9 0.0 copy-start.9
  10.9 2.1 %shard_map.113 = bf16[384,896]{1,0:T(8,128)(2,1)} custom-call(s32[384]{0:T(512)S(1)} %copy-done.6, bf16[1024,896]{1,0:T(8,128)(2,1)S(1)} %copy-done.1), custom_call_target="tpu_custom_call" | custom-call | tf_op jit(solution)/shard_map/pallas_call | solution.py:70
  13.0 10.4 %all-to-all-start = ((bf16[2,8,24,896]{3,2,1,0:T(8,128)(2,1)}), bf16[2,8,24,896]{3,2,1,0:T(8,128)(2,1)S(1)}, u32[]{:S(2)}, u32[]{:S(2)}) async-start(bf16[2,8,24,896]{3,2,1,0:T(8,128)(2,1)} %bitcast.13), calls=%async_computation | async-start | bytes 1376256 | tf_op jit(solution)/shard_map/all_to_all | solution.py:272
  23.4 0.0 copy-done.7
  23.4 0.0 copy-done.9
  23.4 0.0 copy-done
  23.4 0.0 copy-start.3
  23.4 0.9 copy-done.3
  24.4 0.0 copy-start.2
  24.4 0.0 copy-start.8
  24.4 0.4 shard_map.114.side
  24.7 0.1 all-to-all-done.half
  24.9 0.8 shard_map.115
  25.7 3.5 %all-to-all-start.1 = ((bf16[8,32,896]{2,1,0:T(8,128)(2,1)}), bf16[8,32,896]{2,1,0:T(8,128)(2,1)S(1)}, u32[]{:S(2)}, u32[]{:S(2)}) async-start(bf16[8,32,896]{2,1,0:T(8,128)(2,1)} %shard_map.115), calls=%async_computation.1 | async-start | bytes 917504 | tf_op jit(solution)/shard_map/all_to_all | solution.py:272
  29.2 0.0 reduce-scatter.2.cloned.1.call-start
  29.3 0.0 copy-done.2
  29.3 0.0 copy-done.8
  29.3 2.1 %fusion = f32[384,1024]{1,0:T(8,128)} fusion(bf16[896,1024]{1,0:T(8,128)(2,1)S(1)} %copy-done.2, bf16[384,896]{1,0:T(8,128)(2,1)S(1)} %copy-done, f32[896]{0:T(1024)S(1)} %copy-done.8), kind=kOutput, calls=%fused_computation.1 | convolution fusion | flops 705675264 | bytes 4099584 | tf_op jit(solution)/shard_map/dot_general | solution.py:313
  31.4 0.0 copy-start.5
  31.4 0.0 reduce-scatter.2.cloned.1.call-update
  31.4 18.8 %all-to-all-done.1.got.lines = bf16[8,32,896]{2,1,0:T(8,128)(2,1)S(1)} async-done(((bf16[8,32,896]{2,1,0:T(8,128)(2,1)}), bf16[8,32,896]{2,1,0:T(8,128)(2,1)S(1)}, u32[]{:S(2)}, u32[]{:S(2)}) %all-to-all-start.1) | async-done | bytes 458784 | tf_op jit(solution)/shard_map/all_to_all | solution.py:272
  50.2 0.1 shard_map.116
  50.2 7.4 %all_to_all.35 = bf16[4,24,896]{2,1,0:T(8,128)(2,1)S(1)} all-to-all(bf16[4,24,896]{2,1,0:T(8,128)(2,1)S(1)} %shard_map.116), channel_id=1, replica_groups={{0,2,4,6},{1,3,5,7},{8,10,12,14},{9,11,13,15},{16,18,20,22},{17,19,21,2..., dimensions={0} | all-to-all | bytes 344064 | tf_op jit(solution)/shard_map/all_to_all | solution.py:272
  57.6 3.7 %all-gather = bf16[8,24,896]{2,1,0:T(8,128)(2,1)S(1)} all-gather(bf16[4,24,896]{2,1,0:T(8,128)(2,1)S(1)} %all_to_all.35), channel_id=2, replica_groups={{0,1},{2,3},{4,5},{6,7},{8,9},{10,11},{12,13},{14,15},{16,17},{18,19},{..., dimensions={0}, use_global_device_ids=true | all-gather | bytes 516096 | tf_op jit(solution)/shard_map/all_gather | solution.py:310
  61.3 1.1 all-gather.5.cloned.1.call-done
  62.5 0.0 copy-done.5
  62.5 3.0 %shard_map.117 = bf16[8,96,128]{2,1,0:T(8,128)(2,1)S(1)} custom-call(bf16[2,4,24,896]{3,2,1,0:T(8,128)(2,1)S(1)} %bitcast.11, bf16[8,32,896]{2,1,0:T(8,128)(2,1)S(1)} %all-to-all-done.1.got.lines, bf16[384,896]{1,0:T(8,128)(2,1)S(1)} %copy-done, f32[896]{0:T(1024)S(1)} %copy-done.5, bf16[8,112,896]{2,1,0:T(8,128)(2,1)} %bitcast.14), custom_call_target="tpu_custom_call" | custom-call | tf_op jit(solution)/shard_map/pallas_call | solution.py:70
  65.5 17.4 %all_to_all.36.parts = bf16[8,96,128]{2,1,0:T(8,128)(2,1)S(1)} all-to-all(bf16[8,96,128]{2,1,0:T(8,128)(2,1)S(1)} %shard_map.117), channel_id=1, replica_groups=mesh['dp'=8,'vocab'=64] {'dp'}, dimensions={0} | all-to-all | bytes 393216 | tf_op jit(solution)/shard_map/all_to_all | solution.py:327
  82.9 0.2 shard_map.118
  83.1 17.5 %all_to_all.37 = bf16[32,48,128]{2,1,0:T(8,128)(2,1)S(1)} all-to-all(bf16[32,48,128]{2,1,0:T(8,128)(2,1)S(1)} %shard_map.118), channel_id=1, replica_groups={{0,2,4,6,8,10,12,14,16,18,20,22,24,26,28,30,32,34,36,38,40,42,44,46,48,..., dimensions={0} | all-to-all | bytes 786432 | tf_op jit(solution)/shard_map/all_to_all | solution.py:272
  100.6 7.6 %all-gather.2 = bf16[64,48,128]{2,1,0:T(8,128)(2,1)S(1)} all-gather(bf16[32,48,128]{2,1,0:T(8,128)(2,1)S(1)} %all_to_all.37), channel_id=4, replica_groups={{0,1},{2,3},{4,5},{6,7},{8,9},{10,11},{12,13},{14,15},{16,17},{18,19},{..., dimensions={0}, use_global_device_ids=true | all-gather | bytes 1179648 | tf_op jit(solution)/shard_map/all_gather | solution.py:328
  108.2 2.0 %shard_map.119 = bf16[8,400,128]{2,1,0:T(8,128)(2,1)} custom-call(bf16[2,32,48,128]{3,2,1,0:T(8,128)(2,1)S(1)} %bitcast.9, bf16[896,1024]{1,0:T(8,128)(2,1)S(1)} %copy-done.2), custom_call_target="tpu_custom_call" | custom-call | tf_op jit(solution)/shard_map/pallas_call | solution.py:70
  110.2 3.6 %all-to-all-start.5 = ((bf16[8,400,128]{2,1,0:T(8,128)(2,1)}), bf16[8,400,128]{2,1,0:T(8,128)(2,1)S(1)}, u32[]{:S(2)}, u32[]{:S(2)}) async-start(bf16[8,400,128]{2,1,0:T(8,128)(2,1)} %shard_map.119), calls=%async_computation.5 | async-start | bytes 1638400 | tf_op jit(solution)/shard_map/all_to_all | solution.py:341
  113.8 0.0 reduce-scatter.2.cloned.1.call-done.sums
  113.8 0.0 copy-start.4
  113.8 0.9 copy-done.4
  114.8 0.3 shard_map.120
  115.0 23.0 %all-to-all-done.5.parts = bf16[8,400,128]{2,1,0:T(8,128)(2,1)S(1)} async-done(((bf16[8,400,128]{2,1,0:T(8,128)(2,1)}), bf16[8,400,128]{2,1,0:T(8,128)(2,1)S(1)}, u32[]{:S(2)}, u32[]{:S(2)}) %all-to-all-start.5) | async-done | bytes 819232 | tf_op jit(solution)/shard_map/all_to_all | solution.py:341
  138.1 0.3 shard_map.121
  138.4 17.7 %all_to_all.38.stats = f32[64,8,128]{2,1,0:T(8,128)S(1)} all-to-all(f32[64,8,128]{2,1,0:T(8,128)S(1)} %get-tuple-element.7), channel_id=1, replica_groups=mesh['dp'=8,'vocab'=64] {'vocab'}, dimensions={0} | all-to-all | bytes 524288 | tf_op jit(solution)/shard_map/all_to_all | solution.py:346
  156.1 0.9 shard_map.122
  (3 shorter events, 0.0 us)
Async XLA Ops:
  8.0 54.5 %all-gather.5.cloned.1.call-start = ((), (), s32[]{:S(2)}) async-start(), calls=%async_computation.9 | async-start | bytes 1806336 | tf_op jit(solution)/shard_map/all_gather | solution.py:287
  8.7 1.5 copy-start.1
  10.2 0.7 copy-start.6
  10.9 12.5 %copy-start.7 = (f32[896]{0:T(1024)S(1)}, f32[896]{0:T(1024)}, u32[]{:S(2)}) copy-start(f32[896]{0:T(1024)} %param.13) | copy-start | bytes 10756
  10.9 12.5 %copy-start.9 = (f32[112]{0:T(128)S(1)}, f32[112]{0:T(128)}, u32[]{:S(2)}) copy-start(f32[112]{0:T(128)} %param.18) | copy-start | bytes 1348
  10.9 12.5 %copy-start = (bf16[384,896]{1,0:T(8,128)(2,1)S(1)}, bf16[384,896]{1,0:T(8,128)(2,1)}, u32[]{:S(2)}) copy-start(bf16[384,896]{1,0:T(8,128)(2,1)} %hidden.3) | copy-start | bytes 2064388
  13.0 11.9 %all-to-all-start = ((bf16[2,8,24,896]{3,2,1,0:T(8,128)(2,1)}), bf16[2,8,24,896]{3,2,1,0:T(8,128)(2,1)S(1)}, u32[]{:S(2)}, u32[]{:S(2)}) async-start(bf16[2,8,24,896]{3,2,1,0:T(8,128)(2,1)} %bitcast.13), calls=%async_computation | async-start | bytes 1376256 | tf_op jit(solution)/shard_map/all_to_all | solution.py:272
  23.4 0.9 copy-start.3
  24.4 4.9 %copy-start.2 = (bf16[896,1024]{1,0:T(8,128)(2,1)S(1)}, bf16[896,1024]{1,0:T(8,128)(2,1)}, u32[]{:S(2)}) copy-start(bf16[896,1024]{1,0:T(8,128)(2,1)} %head.1) | copy-start | bytes 5505028
  24.4 4.9 %copy-start.8 = (f32[896]{0:T(1024)S(1)}, f32[896]{0:T(1024)}, u32[]{:S(2)}) copy-start(f32[896]{0:T(1024)} %param.12) | copy-start | bytes 10756
  25.7 24.5 %all-to-all-start.1 = ((bf16[8,32,896]{2,1,0:T(8,128)(2,1)}), bf16[8,32,896]{2,1,0:T(8,128)(2,1)S(1)}, u32[]{:S(2)}, u32[]{:S(2)}) async-start(bf16[8,32,896]{2,1,0:T(8,128)(2,1)} %shard_map.115), calls=%async_computation.1 | async-start | bytes 917504 | tf_op jit(solution)/shard_map/all_to_all | solution.py:272
  29.2 84.6 %reduce-scatter.2.cloned.1.call-start = ((), (), s32[]{:S(2)}) async-start(), calls=%async_computation.8 | async-start | bytes 1769472 | tf_op jit(solution)/shard_map/reduce_scatter | solution.py:314
  31.4 31.1 %copy-start.5 = (f32[896]{0:T(1024)S(1)}, f32[896]{0:T(1024)}, u32[]{:S(2)}) copy-start(f32[896]{0:T(1024)} %embed_gain.1) | copy-start | bytes 10756
  110.2 27.8 %all-to-all-start.5 = ((bf16[8,400,128]{2,1,0:T(8,128)(2,1)}), bf16[8,400,128]{2,1,0:T(8,128)(2,1)S(1)}, u32[]{:S(2)}, u32[]{:S(2)}) async-start(bf16[8,400,128]{2,1,0:T(8,128)(2,1)} %shard_map.119), calls=%async_computation.5 | async-start | bytes 1638400 | tf_op jit(solution)/shard_map/all_to_all | solution.py:341
  113.8 0.9 copy-start.4
Sparse Core Ops, SparseCore 0:
  10.9 51.5 all-gather.4
Sparse Core Ops, SparseCore 1:
  32.5 42.3 reduce-scatter.1

commit v10 on v7

--- a/solution.py
+++ b/solution.py
@@ -63,6 +63,8 @@
 def call(kernel, outs, *args, scratch=(), space=pltpu.VMEM):
     single = not isinstance(outs, (list, tuple))
     shapes = [outs] if single else list(outs)
+    if space is pltpu.HBM:
+        shapes = [pltpu.HBM(s.shape, s.dtype) for s in shapes]
     specs = [pl.BlockSpec(memory_space=space) for _ in shapes]
     return pl.pallas_call(
         kernel,
@@ -148,7 +150,7 @@
         return jnp.where(lane == CW, hi, jnp.where(lane == CW + 1, low, 0.0))
 
     extra_h, extra_e = extra(h), extra(e)
-    eg = (e * embed_gain[...]).astype(BF)
+    eg = (e * embed_gain[...].reshape(1, FD)).astype(BF)
     pad = jnp.zeros((L - CW, FD), BF)
     for t in range(NY):
         w = jnp.concatenate([weights[t], pad], axis=0)
@@ -312,7 +314,7 @@
         got,
         lines,
         hidden,
-        embed_gain[None],
+        embed_gain,
         weights,
     )
     joined = call(join_kernel, struct((NQ, RB, L), BF), lax.all_to_all(partial, "dp", 0, 0), lines)

time: 165 us -> 164 us (level)
  blocking collectives: 62.6 us -> 71.6 us
  waiting for transfers between devices: 48.1 us -> 43.7 us
  starting transfers between devices: 20.8 us -> 17.5 us
    all_to_all x1 -> x2, blocking collectives: 14.8 us -> 24.7 us  [exchange(): return lax.all_to_all(x, 'vocab', 0, 0, axis_index_groups=groups)]
    all_to_all x3 -> x2, waiting for transfers between devices: 24.3 us -> 18.9 us  [exchange(): return lax.all_to_all(x, 'vocab', 0, 0, axis_index_groups=groups)]
    all_to_all x3 -> x2, starting transfers between devices: 17.2 us -> 13.9 us  [exchange(): return lax.all_to_all(x, 'vocab', 0, 0, axis_index_groups=groups)]
    unnamed x24 -> x22, local copies, waits for them, and re-layouts: 6.22 us -> 5.46 us
  transfers between devices with their start and end apart: 6 -> 5, of which waited for: 4 -> 4; matrix products, arithmetic and copies ran while one was open for 1% -> 1% of each run, Pallas kernels for 4% -> 4%
where the time goes in v10:
time: 164 us
  blocking collectives  71.6 us (44%)
  waiting for transfers between devices  43.7 us (27%)
  starting transfers between devices  17.5 us (11%)
  between operations  15.6 us (10%)
  Pallas kernels  7.8 us (5%)
  local copies, waits for them, and re-layouts  5.47 us (3%)
  matrix products  2.13 us (1%)
    all_to_all x2, blocking collectives, exchange(): return lax.all_to_all(x, 'vocab', 0, 0, axis_index_groups=groups)  24.7 us
    all_to_all x1, waiting for transfers between devices, per_device(): parts = lax.all_to_all(blocks, 'dp', 0, 0)  23 us
    all_to_all x2, waiting for transfers between devices, exchange(): return lax.all_to_all(x, 'vocab', 0, 0, axis_index_groups=groups)  18.9 us
    all_to_all x1, blocking collectives, per_device(): stats = lax.all_to_all(stats, 'vocab', 0, 0)  17.7 us
    all_to_all x1, blocking collectives, per_device(): lax.all_to_all(partial, 'dp', 0, 0)  17.3 us
    all_to_all x2, starting transfers between devices, exchange(): return lax.all_to_all(x, 'vocab', 0, 0, axis_index_groups=groups)  13.9 us
    all_gather x1, blocking collectives, per_device(): rows = lax.all_gather(exchange(joined, XY), 'vocab', axis_index_groups=CORE)  8.18 us
    pallas_call x10, Pallas kernels, call(): pl.pallas_call(kernel, out_shape=shapes[0] if single else shapes, in_spec...  7.8 us
  transfers between devices with their start and end apart: 5, of which 4 were waited for; matrix products, arithmetic and copies ran while one was open for 1% of the time, Pallas kernels for 4%

profile of v10, /device:TPU:1, one launch (start us, length us, event | category | flops | bytes accessed | tf_op | source)
XLA Modules:
  0.0 163.8 jit_solution(3885627547242447712)
XLA Ops:
  8.0 0.0 all-gather.5.cloned.1.call-start
  8.0 0.7 all-gather.5.cloned.1.call-update
  8.7 0.0 copy-start.1
  8.7 1.5 copy-done.1
  10.2 0.0 copy-start.7
  10.2 0.7 copy-done.7
  10.9 0.0 copy-start.8
  10.9 0.0 copy-start.10
  10.9 0.0 copy-start
  10.9 2.1 %shard_map.113 = bf16[384,896]{1,0:T(8,128)(2,1)} custom-call(s32[384]{0:T(512)S(1)} %copy-done.7, bf16[1024,896]{1,0:T(8,128)(2,1)S(1)} %copy-done.1), custom_call_target="tpu_custom_call" | custom-call | tf_op jit(solution)/shard_map/pallas_call | solution.py:69
  13.0 10.4 %all-to-all-start = ((bf16[2,8,24,896]{3,2,1,0:T(8,128)(2,1)}), bf16[2,8,24,896]{3,2,1,0:T(8,128)(2,1)S(1)}, u32[]{:S(2)}, u32[]{:S(2)}) async-start(bf16[2,8,24,896]{3,2,1,0:T(8,128)(2,1)} %bitcast.14), calls=%async_computation | async-start | bytes 1376256 | tf_op jit(solution)/shard_map/all_to_all | solution.py:267
  23.4 0.0 copy-done.8
  23.4 0.0 copy-done.10
  23.4 0.0 copy-done
  23.4 0.0 copy-start.4
  23.4 0.9 copy-done.4
  24.3 0.0 copy-start.2
  24.3 0.4 shard_map.114.side
  24.7 0.1 all-to-all-done.half
  24.9 0.8 shard_map.115
  25.7 3.5 %all-to-all-start.1 = ((bf16[8,32,896]{2,1,0:T(8,128)(2,1)}), bf16[8,32,896]{2,1,0:T(8,128)(2,1)S(1)}, u32[]{:S(2)}, u32[]{:S(2)}) async-start(bf16[8,32,896]{2,1,0:T(8,128)(2,1)} %shard_map.115), calls=%async_computation.1 | async-start | bytes 917504 | tf_op jit(solution)/shard_map/all_to_all | solution.py:267
  29.2 0.0 reduce-scatter.2.cloned.1.call-start
  29.2 0.0 copy-done.2
  29.2 0.0 copy-done.9
  29.3 2.1 %fusion = f32[384,1024]{1,0:T(8,128)} fusion(bf16[896,1024]{1,0:T(8,128)(2,1)S(1)} %copy-done.2, bf16[384,896]{1,0:T(8,128)(2,1)S(1)} %copy-done, f32[896]{0:T(1024)S(1)} %copy-done.9), kind=kOutput, calls=%fused_computation.1 | convolution fusion | flops 705675264 | bytes 4099584 | tf_op jit(solution)/shard_map/dot_general | solution.py:308
  31.4 0.0 reduce-scatter.2.cloned.1.call-update
  31.4 18.7 %all-to-all-done.1.got.lines = bf16[8,32,896]{2,1,0:T(8,128)(2,1)S(1)} async-done(((bf16[8,32,896]{2,1,0:T(8,128)(2,1)}), bf16[8,32,896]{2,1,0:T(8,128)(2,1)S(1)}, u32[]{:S(2)}, u32[]{:S(2)}) %all-to-all-start.1) | async-done | bytes 458784 | tf_op jit(solution)/shard_map/all_to_all | solution.py:267
  50.1 0.1 shard_map.116
  50.2 7.4 %all_to_all.35 = bf16[4,24,896]{2,1,0:T(8,128)(2,1)S(1)} all-to-all(bf16[4,24,896]{2,1,0:T(8,128)(2,1)S(1)} %shard_map.116), channel_id=1, replica_groups={{0,2,4,6},{1,3,5,7},{8,10,12,14},{9,11,13,15},{16,18,20,22},{17,19,21,2..., dimensions={0} | all-to-all | bytes 344064 | tf_op jit(solution)/shard_map/all_to_all | solution.py:267
  57.6 3.7 %all-gather = bf16[8,24,896]{2,1,0:T(8,128)(2,1)S(1)} all-gather(bf16[4,24,896]{2,1,0:T(8,128)(2,1)S(1)} %all_to_all.35), channel_id=2, replica_groups={{0,1},{2,3},{4,5},{6,7},{8,9},{10,11},{12,13},{14,15},{16,17},{18,19},{..., dimensions={0}, use_global_device_ids=true | all-gather | bytes 516096 | tf_op jit(solution)/shard_map/all_gather | solution.py:305
  61.3 1.1 all-gather.5.cloned.1.call-done
  62.5 0.0 copy-done.6
  62.5 1.4 copy-done.3
  63.9 0.7 shard_map.117
  64.7 17.3 %all_to_all.36.parts = bf16[8,96,128]{2,1,0:T(8,128)(2,1)S(1)} all-to-all(bf16[8,96,128]{2,1,0:T(8,128)(2,1)S(1)} %shard_map.117), channel_id=1, replica_groups=mesh['dp'=8,'vocab'=64] {'dp'}, dimensions={0} | all-to-all | bytes 393216 | tf_op jit(solution)/shard_map/all_to_all | solution.py:320
  82.0 0.2 shard_map.118
  82.2 17.3 %all_to_all.37 = bf16[32,48,128]{2,1,0:T(8,128)(2,1)S(1)} all-to-all(bf16[32,48,128]{2,1,0:T(8,128)(2,1)S(1)} %shard_map.118), channel_id=1, replica_groups={{0,2,4,6,8,10,12,14,16,18,20,22,24,26,28,30,32,34,36,38,40,42,44,46,48,..., dimensions={0} | all-to-all | bytes 786432 | tf_op jit(solution)/shard_map/all_to_all | solution.py:267
  99.5 8.2 %all-gather.2 = bf16[64,48,128]{2,1,0:T(8,128)(2,1)S(1)} all-gather(bf16[32,48,128]{2,1,0:T(8,128)(2,1)S(1)} %all_to_all.37), channel_id=4, replica_groups={{0,1},{2,3},{4,5},{6,7},{8,9},{10,11},{12,13},{14,15},{16,17},{18,19},{..., dimensions={0}, use_global_device_ids=true | all-gather | bytes 1179648 | tf_op jit(solution)/shard_map/all_gather | solution.py:321
  107.7 2.0 %shard_map.119 = bf16[8,400,128]{2,1,0:T(8,128)(2,1)} custom-call(bf16[2,32,48,128]{3,2,1,0:T(8,128)(2,1)S(1)} %bitcast.9, bf16[896,1024]{1,0:T(8,128)(2,1)S(1)} %copy-done.2), custom_call_target="tpu_custom_call" | custom-call | tf_op jit(solution)/shard_map/pallas_call | solution.py:69
  109.7 3.6 %all-to-all-start.5 = ((bf16[8,400,128]{2,1,0:T(8,128)(2,1)}), bf16[8,400,128]{2,1,0:T(8,128)(2,1)S(1)}, u32[]{:S(2)}, u32[]{:S(2)}) async-start(bf16[8,400,128]{2,1,0:T(8,128)(2,1)} %shard_map.119), calls=%async_computation.5 | async-start | bytes 1638400 | tf_op jit(solution)/shard_map/all_to_all | solution.py:334
  113.2 0.0 reduce-scatter.2.cloned.1.call-done.sums
  113.3 0.0 copy-start.5
  113.3 0.9 copy-done.5
  114.2 0.3 shard_map.120
  114.5 23.0 %all-to-all-done.5.parts = bf16[8,400,128]{2,1,0:T(8,128)(2,1)S(1)} async-done(((bf16[8,400,128]{2,1,0:T(8,128)(2,1)}), bf16[8,400,128]{2,1,0:T(8,128)(2,1)S(1)}, u32[]{:S(2)}, u32[]{:S(2)}) %all-to-all-start.5) | async-done | bytes 819232 | tf_op jit(solution)/shard_map/all_to_all | solution.py:334
  137.5 0.3 shard_map.121
  137.8 17.7 %all_to_all.38.stats = f32[64,8,128]{2,1,0:T(8,128)S(1)} all-to-all(f32[64,8,128]{2,1,0:T(8,128)S(1)} %get-tuple-element.7), channel_id=1, replica_groups=mesh['dp'=8,'vocab'=64] {'vocab'}, dimensions={0} | all-to-all | bytes 524288 | tf_op jit(solution)/shard_map/all_to_all | solution.py:339
  155.5 0.9 shard_map.122
  (5 shorter events, 0.0 us)
Async XLA Ops:
  8.0 54.5 %all-gather.5.cloned.1.call-start = ((), (), s32[]{:S(2)}) async-start(), calls=%async_computation.9 | async-start | bytes 1806336 | tf_op jit(solution)/shard_map/all_gather | solution.py:282
  8.7 1.5 copy-start.1
  10.2 0.7 copy-start.7
  10.9 12.5 %copy-start.8 = (f32[896]{0:T(1024)S(1)}, f32[896]{0:T(1024)}, u32[]{:S(2)}) copy-start(f32[896]{0:T(1024)} %param.13) | copy-start | bytes 10756
  10.9 12.5 %copy-start.10 = (f32[112]{0:T(128)S(1)}, f32[112]{0:T(128)}, u32[]{:S(2)}) copy-start(f32[112]{0:T(128)} %param.18) | copy-start | bytes 1348
  10.9 12.5 %copy-start = (bf16[384,896]{1,0:T(8,128)(2,1)S(1)}, bf16[384,896]{1,0:T(8,128)(2,1)}, u32[]{:S(2)}) copy-start(bf16[384,896]{1,0:T(8,128)(2,1)} %hidden.3) | copy-start | bytes 2064388
  13.0 11.9 %all-to-all-start = ((bf16[2,8,24,896]{3,2,1,0:T(8,128)(2,1)}), bf16[2,8,24,896]{3,2,1,0:T(8,128)(2,1)S(1)}, u32[]{:S(2)}, u32[]{:S(2)}) async-start(bf16[2,8,24,896]{3,2,1,0:T(8,128)(2,1)} %bitcast.14), calls=%async_computation | async-start | bytes 1376256 | tf_op jit(solution)/shard_map/all_to_all | solution.py:267
  23.4 0.9 copy-start.4
  24.3 4.9 %copy-start.2 = (bf16[896,1024]{1,0:T(8,128)(2,1)S(1)}, bf16[896,1024]{1,0:T(8,128)(2,1)}, u32[]{:S(2)}) copy-start(bf16[896,1024]{1,0:T(8,128)(2,1)} %head.1) | copy-start | bytes 5505028
  24.3 4.9 %copy-start.9 = (f32[896]{0:T(1024)S(1)}, f32[896]{0:T(1024)}, u32[]{:S(2)}) copy-start(f32[896]{0:T(1024)} %param.12) | copy-start | bytes 10756
  25.7 24.4 %all-to-all-start.1 = ((bf16[8,32,896]{2,1,0:T(8,128)(2,1)}), bf16[8,32,896]{2,1,0:T(8,128)(2,1)S(1)}, u32[]{:S(2)}, u32[]{:S(2)}) async-start(bf16[8,32,896]{2,1,0:T(8,128)(2,1)} %shard_map.115), calls=%async_computation.1 | async-start | bytes 917504 | tf_op jit(solution)/shard_map/all_to_all | solution.py:267
  29.2 84.1 %reduce-scatter.2.cloned.1.call-start = ((), (), s32[]{:S(2)}) async-start(), calls=%async_computation.8 | async-start | bytes 1769472 | tf_op jit(solution)/shard_map/reduce_scatter | solution.py:309
  31.4 31.1 %copy-start.6 = (f32[896]{0:T(1024)S(1)}, f32[896]{0:T(1024)}, u32[]{:S(2)}) copy-start(f32[896]{0:T(1024)} %embed_gain.1) | copy-start | bytes 10756
  62.5 1.4 copy-start.3
  109.7 27.8 %all-to-all-start.5 = ((bf16[8,400,128]{2,1,0:T(8,128)(2,1)}), bf16[8,400,128]{2,1,0:T(8,128)(2,1)S(1)}, u32[]{:S(2)}, u32[]{:S(2)}) async-start(bf16[8,400,128]{2,1,0:T(8,128)(2,1)} %shard_map.119), calls=%async_computation.5 | async-start | bytes 1638400 | tf_op jit(solution)/shard_map/all_to_all | solution.py:334
  113.3 0.9 copy-start.5
Sparse Core Ops, SparseCore 0:
  10.9 51.5 all-gather.4
Sparse Core Ops, SparseCore 1:
  32.5 42.2 reduce-scatter.1
